TPU v7x, 32 devices: a whole 2x2x4 slice. The times are simulated.
32 devices in a mesh: rows: 16 (over z, y, x), heads: 2 (over core).
Axes of the slice: x: 2, y: 2, z: 4, core: 2. Of those that a mesh axis runs over, the one named last changes fastest.
Arguments:
- feats: float32 [16384, 100], P(('rows', 'heads')), as said below
- feature_mask: int32 [16, 100], P('rows'), may hold values from 0 to 1, as said below
- splits: int32 [16], P('rows'), may hold values from 640 to 896
- prompt_index: int32 [16, 128], P('rows'), may hold values from 0 to 511
- prompt_bank: bfloat16 [512, 512], replicated, may hold values from -6 to 6
- enc_weight: bfloat16 [100, 512], replicated, may hold values from -0.625 to 0.625
- enc_bias: float32 [512], replicated, may hold values from -4 to 4
- qkv_weight: bfloat16 [3, 512, 512], P(None, None, 'heads'), may hold values from -0.25 to 0.25
- out_weight: bfloat16 [512, 512], P('heads'), may hold values from -2 to 2
- out_bias: float32 [512], replicated, may hold values from -4 to 4
- attn_gain: float32 [512], replicated, may hold values from 0.25 to 1.75
- attn_shift: float32 [512], replicated, may hold values from -4 to 4
- up_weight: bfloat16 [512, 1024], P(None, 'heads'), may hold values from -0.25 to 0.25
- up_bias: float32 [1024], P('heads'), may hold values from -6 to 6
- down_weight: bfloat16 [1024, 512], P('heads'), may hold values from -0.1875 to 0.1875
- down_bias: float32 [512], replicated, may hold values from -4 to 4
- ffn_gain: float32 [512], replicated, may hold values from 0.25 to 1.75
- ffn_shift: float32 [512], replicated, may hold values from -4 to 4
- cotangent: float32 [16384, 512], P(('rows', 'heads'))
Outputs:
- output: float32 [16384, 512], P(('rows', 'heads'))
- grad_feats: float32 [16384, 100], P(('rows', 'heads'))
- grad_prompt_bank: float32 [512, 512], replicated
- grad_enc_weight: float32 [100, 512], replicated
- grad_enc_bias: float32 [512], replicated
- grad_qkv_weight: float32 [3, 512, 512], P(None, None, 'heads')
- grad_out_weight: float32 [512, 512], P('heads')
- grad_out_bias: float32 [512], replicated
- grad_attn_gain: float32 [512], replicated
- grad_attn_shift: float32 [512], replicated
- grad_up_weight: float32 [512, 1024], P(None, 'heads')
- grad_up_bias: float32 [1024], P('heads')
- grad_down_weight: float32 [1024, 512], P('heads')
- grad_down_bias: float32 [512], replicated
- grad_ffn_gain: float32 [512], replicated
- grad_ffn_shift: float32 [512], replicated
Inputs may be any that keep to these rules, and one draw needn't show every extreme that they name: `feature_mask`: each row holds ones first and zeros after them, between 25 and 100 ones. `feats`: zero wherever the episode's feature_mask is zero.
All inputs are finite; a program needn't handle non-finite values.
Results may differ from a plain program's by a relative error of at most 0.015.
Values may be sent and summed in bfloat16 or wider, within the bound.
A program may use at most 64 MiB of HBM per device.

v0:
```python
import jax
import jax.numpy as jnp
from jax import lax
from jax.sharding import PartitionSpec as P

DH = 128
P_SIZE = 128


epsilon = 1e-05
highest = lax.Precision.HIGHEST


def normalize(values, gain, shift):
    center = values - jnp.mean(values, axis=-1, keepdims=True)
    spread = jnp.mean(center * center, axis=-1, keepdims=True)
    return center * lax.rsqrt(spread + epsilon) * gain + shift


def product(left, right):
    return jnp.dot(left, right, preferred_element_type=jnp.float32)


def product_tn(left, right):
    return lax.dot_general(
        left, right, (((0,), (0,)), ((), ())), preferred_element_type=jnp.float32
    )


def product_nt(left, right):
    return lax.dot_general(
        left, right, (((1,), (1,)), ((), ())), preferred_element_type=jnp.float32
    )


def exact_gelu(values):
    return jax.nn.gelu(values, approximate=False)


def per_device(
    feats,
    feature_mask,
    splits,
    prompt_index,
    prompt_bank,
    enc_weight,
    enc_bias,
    qkv_weight,
    out_weight,
    out_bias,
    attn_gain,
    attn_shift,
    up_weight,
    up_bias,
    down_weight,
    down_bias,
    ffn_gain,
    ffn_shift,
    cotangent,
):
    local_rows = feats.shape[0]
    features = feats.shape[1]
    all_rows = local_rows * lax.axis_size("rows") * lax.axis_size("heads")
    episode_rows = local_rows * lax.axis_size("heads")
    head_count = qkv_weight.shape[2] // DH
    key_count = P_SIZE + episode_rows
    score_scale = DH ** (-0.5)
    moments = lax.psum((jnp.sum(feats, axis=0), jnp.sum(feats * feats, axis=0)), ("rows", "heads"))
    feat_mean = moments[0] / all_rows
    feat_var = moments[1] / all_rows - feat_mean * feat_mean
    inverse = lax.rsqrt(feat_var + epsilon)
    live = feature_mask[0].astype(jnp.float32)
    boost = jnp.sqrt(features / jnp.sum(live))
    centered = feats - feat_mean
    normed = centered * inverse * (live * boost)
    normed_low = normed.astype(jnp.bfloat16)
    hidden_in = product(normed_low, enc_weight) + enc_bias
    hidden_low = hidden_in.astype(jnp.bfloat16)
    episode_hidden = lax.all_gather(hidden_low, "heads", axis=0, tiled=True)
    selector = prompt_index[0][:, None] == jnp.arange(prompt_bank.shape[0])[None, :]
    prompt_low = product(selector.astype(jnp.bfloat16), prompt_bank).astype(jnp.bfloat16)
    source_rows = jnp.concatenate([prompt_low, episode_hidden], axis=0)
    queries = product(episode_hidden, qkv_weight[0]).astype(jnp.bfloat16)
    key_rows = product(source_rows, qkv_weight[1]).astype(jnp.bfloat16)
    value_rows = product(source_rows, qkv_weight[2]).astype(jnp.bfloat16)
    block = min(512, episode_rows)
    blocks = episode_rows // block
    visible = jnp.arange(key_count) < P_SIZE + splits[0]
    heads_k = key_rows.reshape(key_count, head_count, DH)
    heads_v = value_rows.reshape(key_count, head_count, DH)
    query_blocks = queries.reshape(blocks, block, head_count, DH)

    def scores_of(query_block):
        products = jnp.einsum(
            "qhd,khd->hqk", query_block, heads_k, preferred_element_type=jnp.float32
        )
        return jnp.where(visible[None, None, :], products * score_scale, -1e30)

    def attend(query_block):
        scaled = scores_of(query_block)
        largest = jnp.max(scaled, axis=-1, keepdims=True)
        exponent = jnp.exp(scaled - largest)
        totals = jnp.sum(exponent, axis=-1, keepdims=True)
        shares = exponent / totals
        result = jnp.einsum(
            "hqk,khd->qhd", shares.astype(jnp.bfloat16), heads_v, preferred_element_type=jnp.float32
        )
        return (result.astype(jnp.bfloat16), (largest + jnp.log(totals))[..., 0])

    attended, log_totals = lax.map(attend, query_blocks)
    attended = attended.reshape(episode_rows, head_count * DH)
    branch = (
        lax.psum_scatter(
            product(attended, out_weight).astype(jnp.bfloat16),
            "heads",
            scatter_dimension=0,
            tiled=True,
        ).astype(jnp.float32)
        + out_bias
    )
    joined = hidden_in + branch
    after_attn = normalize(joined, attn_gain, attn_shift)
    episode_after = lax.all_gather(after_attn.astype(jnp.bfloat16), "heads", axis=0, tiled=True)
    upper = product(episode_after, up_weight) + up_bias
    activated = exact_gelu(upper).astype(jnp.bfloat16)
    mixed = (
        lax.psum_scatter(
            product(activated, down_weight).astype(jnp.bfloat16),
            "heads",
            scatter_dimension=0,
            tiled=True,
        ).astype(jnp.float32)
        + down_bias
    )
    joined_ffn = after_attn + mixed
    output, ffn_back = jax.vjp(normalize, joined_ffn, ffn_gain, ffn_shift)
    d_joined_ffn, d_ffn_gain, d_ffn_shift = ffn_back(cotangent)
    grad_mixed = d_joined_ffn.astype(jnp.bfloat16)
    d_down_bias = jnp.sum(grad_mixed.astype(jnp.float32), axis=0)
    episode_grad_mixed = lax.all_gather(grad_mixed, "heads", axis=0, tiled=True)
    d_down_weight = product_tn(activated, episode_grad_mixed)
    d_activated = product_nt(episode_grad_mixed, down_weight)
    _, gelu_back = jax.vjp(exact_gelu, upper)
    d_upper = gelu_back(d_activated)[0].astype(jnp.bfloat16)
    d_up_bias = jnp.sum(d_upper.astype(jnp.float32), axis=0)
    d_up_weight = product_tn(episode_after, d_upper)
    d_after = d_joined_ffn + lax.psum_scatter(
        product_nt(d_upper, up_weight).astype(jnp.bfloat16),
        "heads",
        scatter_dimension=0,
        tiled=True,
    ).astype(jnp.float32)
    _, attn_back = jax.vjp(normalize, joined, attn_gain, attn_shift)
    d_joined, d_attn_gain, d_attn_shift = attn_back(d_after)
    grad_branch = d_joined.astype(jnp.bfloat16)
    d_out_bias = jnp.sum(grad_branch.astype(jnp.float32), axis=0)
    episode_grad_branch = lax.all_gather(grad_branch, "heads", axis=0, tiled=True)
    d_out_weight = product_tn(attended, episode_grad_branch)
    d_attended = product_nt(episode_grad_branch, out_weight).astype(jnp.bfloat16)
    grad_blocks = d_attended.reshape(blocks, block, head_count, DH)

    def attend_back(carry, inputs):
        query_block, grad_block, log_block = inputs
        key_grad, value_grad = carry
        shares = jnp.exp(scores_of(query_block) - log_block[..., None])
        upstream = jnp.einsum(
            "qhd,khd->hqk", grad_block, heads_v, preferred_element_type=jnp.float32
        )
        inner = jnp.sum(upstream * shares, axis=-1, keepdims=True)
        d_scores = (shares * (upstream - inner) * score_scale).astype(jnp.bfloat16)
        d_query = jnp.einsum(
            "hqk,khd->qhd", d_scores, heads_k, preferred_element_type=jnp.float32
        ).astype(jnp.bfloat16)
        key_grad = key_grad + jnp.einsum(
            "hqk,qhd->khd", d_scores, query_block, preferred_element_type=jnp.float32
        )
        value_grad = value_grad + jnp.einsum(
            "hqk,qhd->khd",
            shares.astype(jnp.bfloat16),
            grad_block,
            preferred_element_type=jnp.float32,
        )
        return ((key_grad, value_grad), d_query)

    empty = jnp.zeros((key_count, head_count, DH), jnp.float32)
    (key_grad, value_grad), d_queries = lax.scan(
        attend_back, (empty, empty), (query_blocks, grad_blocks, log_totals)
    )
    d_queries = d_queries.reshape(episode_rows, head_count * DH)
    d_keys = key_grad.reshape(key_count, head_count * DH).astype(jnp.bfloat16)
    d_values = value_grad.reshape(key_count, head_count * DH).astype(jnp.bfloat16)
    d_qkv_weight = jnp.stack(
        [
            product_tn(episode_hidden, d_queries),
            product_tn(source_rows, d_keys),
            product_tn(source_rows, d_values),
        ]
    )
    d_prompt = product_nt(d_keys[:P_SIZE], qkv_weight[1]) + product_nt(
        d_values[:P_SIZE], qkv_weight[2]
    )
    d_bank = lax.dot_general(
        selector.astype(jnp.float32),
        d_prompt,
        (((0,), (0,)), ((), ())),
        precision=highest,
        preferred_element_type=jnp.float32,
    )
    data_grads = jnp.stack([d_queries, d_keys[P_SIZE:], d_values[P_SIZE:]])
    d_hidden = d_joined + lax.psum_scatter(
        jnp.einsum(
            "crh,cdh->rd", data_grads, qkv_weight, preferred_element_type=jnp.float32
        ).astype(jnp.bfloat16),
        "heads",
        scatter_dimension=0,
        tiled=True,
    ).astype(jnp.float32)
    grad_hidden = d_hidden.astype(jnp.bfloat16)
    d_enc_bias = jnp.sum(grad_hidden.astype(jnp.float32), axis=0)
    d_enc_weight = product_tn(normed_low, grad_hidden)
    upstream_feat = product_nt(grad_hidden, enc_weight) * (live * boost)
    feat_terms = (jnp.sum(upstream_feat, axis=0), jnp.sum(upstream_feat * centered, axis=0))
    shared = (
        d_enc_weight,
        d_enc_bias,
        d_out_bias,
        d_attn_gain,
        d_attn_shift,
        d_down_bias,
        d_ffn_gain,
        d_ffn_shift,
        d_bank,
    )
    feat_sums = lax.psum((feat_terms[0], feat_terms[1]), ("rows", "heads"))
    shared_sums = lax.psum(
        (
            shared[0],
            shared[1],
            shared[2],
            shared[3],
            shared[4],
            shared[5],
            shared[6],
            shared[7],
            shared[8],
        ),
        ("rows", "heads"),
    )
    var_grad = -0.5 * inverse * inverse * inverse * feat_sums[1]
    first_grad = (-inverse * feat_sums[0] - 2.0 * feat_mean * var_grad) / all_rows
    grad_feats = upstream_feat * inverse + first_grad + 2.0 * feats * var_grad / all_rows
    local_sharded = (d_qkv_weight, d_out_weight, d_up_weight, d_up_bias, d_down_weight)
    sharded_sums = lax.psum(
        (local_sharded[0], local_sharded[1], local_sharded[2], local_sharded[3], local_sharded[4]),
        "rows",
    )
    ffn_grads = sharded_sums[2:]
    return (
        output,
        grad_feats,
        shared_sums[8],
        shared_sums[0],
        shared_sums[1],
        sharded_sums[0],
        sharded_sums[1],
        shared_sums[2],
        shared_sums[3],
        shared_sums[4],
        ffn_grads[0],
        ffn_grads[1],
        ffn_grads[2],
        shared_sums[5],
        shared_sums[6],
        shared_sums[7],
    )


def solution(mesh):
    placed = (
        P(("rows", "heads"), None),
        P("rows", None),
        P("rows"),
        P("rows", None),
        P(),
        P(),
        P(),
        P(None, None, "heads"),
        P("heads", None),
        P(),
        P(),
        P(),
        P(None, "heads"),
        P("heads"),
        P("heads", None),
        P(),
        P(),
        P(),
        P(("rows", "heads"), None),
    )
    return jax.shard_map(
        per_device,
        mesh=mesh,
        in_specs=placed,
        out_specs=(
            P(("rows", "heads"), None),
            P(("rows", "heads"), None),
            P(),
            P(),
            P(),
            P(None, None, "heads"),
            P("heads", None),
            P(),
            P(),
            P(),
            P(None, "heads"),
            P("heads"),
            P("heads", None),
            P(),
            P(),
            P(),
        ),
        check_vma=False,
    )
```

profile of v0, /device:TPU:0, one launch (start us, length us, event | category | flops | bytes accessed | tf_op | source)
XLA Modules:
  0.0 573.5 jit_solution(9657164222317039882)
XLA Ops:
  7.3 1.4 convert_reduce_fusion.4
  11.1 42.0 %all-reduce.1 = (f32[100]{0:T(128)S(1)}, f32[100]{0:T(128)S(1)}) all-reduce(f32[100]{0:T(128)S(1)} %get-tuple-element.240, f32[100]{0:T(128)S(1)} %get-tuple-element.239), channel_id=1, replica_groups=mesh['rows'=16,'heads'=2] {'rows','heads'}, use_global_device_ids=true, to_apply=%region_3.0 | all-reduce | flops 200 | bytes 1600 | tf_op jit(solution)/shard_map/psum | solution.py:68
  53.2 2.5 fusion.97
  56.9 7.9 %all-gather.5.cloned.1.call-done = bf16[1024,512]{0,1:T(8,128)(2,1)} async-done(((bf16[512,512]{0,1:T(8,128)(2,1)}), bf16[1024,512]{0,1:T(8,128)(2,1)}) %all-gather.5.cloned.1.call-update) | async-done | bytes 1048592 | tf_op jit(solution)/shard_map/all_gather | solution.py:79
  64.7 1.7 convolution_convert_fusion.6
  66.7 1.8 convolution_convert_fusion
  68.8 1.8 convolution_convert_fusion.1
  71.2 6.9 %while.28 = (s32[]{:T(128)}, bf16[2,512,2,128]{3,2,1,0:T(2,128)(2,1)S(1)}, f32[2,2,512]{2,1,0:T(2,128)S(1)}, bf16[2,512,2,128]{3,1,2,0:T(8,128)(2,1)S(1)}, bf16[...) while((s32[]{:T(128)}, ...), condition=%wide.region_8.9_spmd.clone, body=%wide.region_5.8_spmd.clone.sunk | while | flops 613548160 | bytes 16420077 | solution.py:110
  78.2 1.5 convolution_convert_fusion.2
  79.7 9.8 %reduce-scatter.5.cloned.1.call-done = bf16[512,512]{0,1:T(8,128)(2,1)} async-done(((bf16[1024,512]{0,1:T(8,128)(2,1)}), bf16[512,512]{0,1:T(8,128)(2,1)}) %reduce-scatter.5.cloned.1.call-update) | async-done | bytes 524304 | tf_op jit(solution)/shard_map/reduce_scatter | solution.py:113
  89.5 1.6 fusion.95
  92.4 10.3 %all-gather.7.cloned.1.call-done = bf16[1024,512]{0,1:T(8,128)(2,1)} async-done(((bf16[512,512]{0,1:T(8,128)(2,1)}), bf16[1024,512]{0,1:T(8,128)(2,1)}) %all-gather.7.cloned.1.call-update) | async-done | bytes 1048592 | tf_op jit(solution)/shard_map/all_gather | solution.py:123
  102.7 7.7 %multiply_convert_fusion = (bf16[1024,512]{1,0:T(8,128)(2,1)S(1)}, f32[1024,512]{1,0:T(8,128)}, f32[1024,512]{1,0:T(8,128)}) fusion(f32[512]{0:T(512)S(1)} %copy-done.50, bf16[1024,512]{0,1:T(8,128)(2,1)} %all-gather.7.cloned.1.call-done, bf16[512,512]{1,0:T(8,128)(2,1)S(1)} %copy-done), kind=kOutput, calls=%fused_computation.60 | convolution fusion | flops 571473920 | bytes 6817792 | tf_op jit(solution)/shard_map/dot_general | solution.py:21
  111.4 1.7 convolution_convert_fusion.4
  113.4 2.5 copy.64
  116.0 7.1 %reduce-scatter.7.cloned.1.call-done = bf16[512,512]{0,1:T(8,128)(2,1)} async-done(((bf16[1024,512]{0,1:T(8,128)(2,1)}), bf16[512,512]{0,1:T(8,128)(2,1)}) %reduce-scatter.7.cloned.1.call-update) | async-done | bytes 524304 | tf_op jit(solution)/shard_map/reduce_scatter | solution.py:127
  123.1 1.5 fusion.93
  125.8 1.4 fusion.92
  128.2 1.5 convert_reduce_fusion.1
  129.7 10.3 %all-gather.9.cloned.1.call-done = bf16[1024,512]{0,1:T(8,128)(2,1)} async-done(((bf16[512,512]{0,1:T(8,128)(2,1)}), bf16[1024,512]{0,1:T(8,128)(2,1)}) %all-gather.9.cloned.1.call-update) | async-done | bytes 1048592 | tf_op jit(solution)/shard_map/all_gather | solution.py:140
  140.0 4.8 convert_reduce_fusion
  145.7 1.7 convolution_convert_fusion.3
  147.5 9.8 %reduce-scatter.9.cloned.1.call-done = bf16[512,512]{0,1:T(8,128)(2,1)} async-done(((bf16[1024,512]{0,1:T(8,128)(2,1)}), bf16[512,512]{0,1:T(8,128)(2,1)}) %reduce-scatter.9.cloned.1.call-update) | async-done | bytes 524304 | tf_op jit(solution)/shard_map/reduce_scatter | solution.py:147
  157.3 2.6 multiply_reduce_fusion.2
  159.9 1.6 fusion.91
  162.5 1.5 convert_reduce_fusion.2
  164.0 10.3 %all-gather.11.cloned.1.call-done = bf16[1024,512]{0,1:T(8,128)(2,1)} async-done(((bf16[512,512]{0,1:T(8,128)(2,1)}), bf16[1024,512]{0,1:T(8,128)(2,1)}) %all-gather.11.cloned.1.call-update) | async-done | bytes 1048592 | tf_op jit(solution)/shard_map/all_gather | solution.py:157
  174.3 1.8 convolution_convert_fusion.5
  178.1 49.6 %while.29 = (s32[]{:T(128)}, f32[1152,2,128]{0,2,1:T(8,128)}, f32[1152,2,128]{0,2,1:T(8,128)S(1)}, bf16[2,512,2,128]{3,2,1,0:T(2,128)(2,1)}, bf16[2,512,2,128]{3...) while((s32[]{:T(128)}, f32[1152,2,128]{0,2,1:T(8,128)}, ...), condition=%wide.region_22.23_spmd.clone, body=%wide.region_20.22_spmd.clone.sunk | while | flops 1527780736 | bytes 70204728 | solution.py:186
  182.5 2.9 fusion.166
  185.4 7.6 %fusion.169 = bf16[1,512,2,128]{3,1,2,0:T(8,128)(2,1)S(1)} fusion(bf16[1152,2,128]{2,0,1:T(8,128)(2,1)S(1)} %get-tuple-element.482, f32[2,512,1152]{2,1,0:T(8,128)} %copy-done.2, f32[2,512,1152]{2,1,0:T(8,128)} %fusion.166), kind=kOutput, calls=%fused_computation.36.clone.1 | convolution fusion | flops 308021376 | bytes 10289152 | tf_op jit(solution)/shard_map/while/body/eval_jaxpr/hqk,khd->qhd/dot_general | solution.py:171
  193.0 8.7 %fusion.167 = f32[1152,2,128]{0,2,1:T(8,128)} fusion(f32[2,512,1152]{2,1,0:T(8,128)} %copy-done.2, f32[2,512,1152]{2,1,0:T(8,128)} %fusion.166, f32[1152,2,128]{0,2,1:T(8,128)} %get-tuple-element.466, pred[]{:T(512)S(6)} %compare.3, bf16[2,512,2,128]{3,1,2,0:T(8,128)(2,1)S(1)} %get-tuple-element.481, s32[]{:T(128)S(6)} %copy.135), kind=kOutput, calls=%fused_computation.30.clone.1 | convolution fusion | flops 308480128 | bytes 21495812 | tf_op jit(solution)/shard_map/while/body/eval_jaxpr/hqk,qhd->khd/dot_general | solution.py:174
  207.1 2.9 fusion.166
  210.1 7.6 %fusion.169 = bf16[1,512,2,128]{3,1,2,0:T(8,128)(2,1)S(1)} fusion(bf16[1152,2,128]{2,0,1:T(8,128)(2,1)S(1)} %get-tuple-element.482, f32[2,512,1152]{2,1,0:T(8,128)} %copy-done.2, f32[2,512,1152]{2,1,0:T(8,128)} %fusion.166), kind=kOutput, calls=%fused_computation.36.clone.1 | convolution fusion | flops 308021376 | bytes 10289152 | tf_op jit(solution)/shard_map/while/body/eval_jaxpr/hqk,khd->qhd/dot_general | solution.py:171
  217.7 9.0 %fusion.167 = f32[1152,2,128]{0,2,1:T(8,128)} fusion(f32[2,512,1152]{2,1,0:T(8,128)} %copy-done.2, f32[2,512,1152]{2,1,0:T(8,128)} %fusion.166, f32[1152,2,128]{0,2,1:T(8,128)} %get-tuple-element.466, pred[]{:T(512)S(6)} %compare.3, bf16[2,512,2,128]{3,1,2,0:T(8,128)(2,1)S(1)} %get-tuple-element.481, s32[]{:T(128)S(6)} %copy.135), kind=kOutput, calls=%fused_computation.30.clone.1 | convolution fusion | flops 308480128 | bytes 21495812 | tf_op jit(solution)/shard_map/while/body/eval_jaxpr/hqk,qhd->khd/dot_general | solution.py:174
  227.7 1.4 convert_element_type.134
  232.4 3.3 bitcast_convert_fusion
  235.7 3.4 fusion.99
  239.1 3.0 fusion.98
  244.3 1.7 fusion.75
  246.0 1.3 convert_reduce_fusion.3
  248.7 1.7 convolution_bitcast_fusion.4
  255.1 1.3 copy.76
  256.4 42.7 %psum.139 = f32[512]{0:T(512)} all-reduce(f32[512]{0:T(512)S(1)} %copy-done.42), channel_id=1, replica_groups=mesh['rows'=16,'heads'=2] {'rows'}, use_global_device_ids=true, to_apply=%region_42.43 | all-reduce | flops 512 | bytes 4096 | tf_op jit(solution)/shard_map/psum | solution.py:253
  299.5 37.2 %all-reduce = (f32[100]{0:T(128)S(1)}, f32[100]{0:T(128)S(1)}, f32[512]{0:T(512)}, f32[512]{0:T(512)}, f32[512]{0:T(512)}, /*index=5*/f32[512]{0:T(512)}, f32[512]{0:T(512)}, f32[512]{0:T(512)}, f32[512]{0:T(512)}) all-reduce(f32[100]{0:T(128)S(1)} %get-tuple-element.238, ...), channel_id=1, replica_groups=mesh['rows'=16,'heads'=2] {'rows','heads'}, use_global_device_ids=true, to_apply=%region_27.28 | all-reduce | flops 3784 | bytes 30272 | tf_op jit(solution)/shard_map/psum | solution.py:234
  337.5 46.1 %all-reduce.7.cloned.1.call-done = (f32[512,512]{1,0:T(8,128)}, f32[100,512]{1,0:T(8,128)}) async-done(((f32[512,512]{1,0:T(8,128)}, f32[100,512]{1,0:T(8,128)}), (f32[512,512]{1,0:T(8,128)}, f32[100,512]{1,0:T(8,128)})) %all-reduce.7.cloned.1.call-update) | async-done | bytes 1253392 | tf_op jit(solution)/shard_map/psum | solution.py:235
  383.7 176.0 %all-reduce.9.cloned.1.call-done = (f32[3,512,256]{2,1,0:T(8,128)}, f32[256,512]{1,0:T(8,128)}, f32[512,512]{1,0:T(8,128)}, f32[512,512]{1,0:T(8,128)}) async-done(((f32[3,512,256]{2,1,0:T(8,128)}, f32[256,512]{1,0:T(8,128)}, f32[512,512]{1,0:T(8,128)}, f32[512,512]{1,0:T(8,128)}), (f32[3,512,256]{2,1,0:T(8,128)}, f32[256,512]{1,0:T(8,128)}, f32[512,512]{1,0:T(8,128)}, ...) | async-done | bytes 4194320 | tf_op jit(solution)/shard_map/psum | solution.py:253
  559.7 2.4 copy.150
  (203 shorter events, 47.0 us)
Async XLA Ops:
  7.2 95.5 %copy-start = (bf16[512,512]{1,0:T(8,128)(2,1)S(1)}, bf16[512,512]{1,0:T(8,128)(2,1)}, u32[]{:S(2)}) copy-start(bf16[512,512]{1,0:T(8,128)(2,1)} %param.35) | copy-start | bytes 1572868
  7.2 49.2 %copy-start.20 = (bf16[512,512]{1,0:T(8,128)(2,1)S(1)}, bf16[512,512]{1,0:T(8,128)(2,1)}, u32[]{:S(2)}) copy-start(bf16[512,512]{1,0:T(8,128)(2,1)} %param.27) | copy-start | bytes 1572868
  7.2 49.2 %copy-start.45 = (s32[1,128]{1,0:T(1,128)S(1)}, s32[1,128]{1,0:T(1,128)}, u32[]{:S(2)}) copy-start(s32[1,128]{1,0:T(1,128)} %param.26) | copy-start | bytes 1540
  7.2 57.5 %copy-start.24 = (bf16[3,512,256]{2,1,0:T(8,128)(2,1)S(1)}, bf16[3,512,256]{2,1,0:T(8,128)(2,1)}, u32[]{:S(2)}) copy-start(bf16[3,512,256]{2,1,0:T(8,128)(2,1)} %param.30) | copy-start | bytes 2359300
  7.2 57.5 %all-gather.5.cloned.1.call-start = ((), (), s32[]{:S(2)}) async-start(), calls=%async_computation.4 | async-start | bytes 1572864 | tf_op jit(solution)/shard_map/all_gather | solution.py:79
  10.1 56.4 %copy-start.37 = (f32[100]{0:T(128)}, f32[100]{0:T(128)S(1)}, u32[]{:S(2)}) copy-start(f32[100]{0:T(128)S(1)} %multiply_bitcast_fusion) | copy-start | bytes 1204
  53.1 13.3 %copy-start.43 = (f32[100]{0:T(128)}, f32[100]{0:T(128)S(1)}, u32[]{:S(2)}) copy-start(f32[100]{0:T(128)S(1)} %get-tuple-element.285) | copy-start | bytes 1204
  53.2 13.3 %copy-start.30 = (f32[100]{0:T(128)}, f32[100]{0:T(128)S(1)}, u32[]{:S(2)}) copy-start(f32[100]{0:T(128)S(1)} %get-tuple-element.315) | copy-start | bytes 1204
  55.7 33.8 %reduce-scatter.5.cloned.1.call-start = ((), (), s32[]{:S(2)}) async-start(), calls=%async_computation.5 | async-start | bytes 1572864 | tf_op jit(solution)/shard_map/reduce_scatter | solution.py:113
  71.2 7.0 %copy-start.17 = (bf16[256,512]{1,0:T(8,128)(2,1)S(1)}, bf16[256,512]{1,0:T(8,128)(2,1)}, u32[]{:S(2)}) copy-start(bf16[256,512]{1,0:T(8,128)(2,1)} %param.31) | copy-start | bytes 786436
  78.1 11.4 %copy-start.8 = (bf16[2,512,2,128]{3,2,1,0:T(2,128)(2,1)}, bf16[2,512,2,128]{3,2,1,0:T(2,128)(2,1)S(1)}, u32[]{:S(2)}) copy-start(bf16[2,512,2,128]{3,2,1,0:T(2,128)(2,1)S(1)} %get-tuple-element.108) | copy-start | bytes 1572868
  78.2 11.3 %copy-start.40 = (f32[512]{0:T(512)S(1)}, f32[512]{0:T(512)}, u32[]{:S(2)}) copy-start(f32[512]{0:T(512)} %param.32) | copy-start | bytes 6148
  79.7 11.6 %copy-start.27 = (f32[512]{0:T(512)S(1)}, f32[512]{0:T(512)}, u32[]{:S(2)}) copy-start(f32[512]{0:T(512)} %param.33) | copy-start | bytes 6148
  79.7 11.6 %copy-start.29 = (f32[512]{0:T(512)S(1)}, f32[512]{0:T(512)}, u32[]{:S(2)}) copy-start(f32[512]{0:T(512)} %param.34) | copy-start | bytes 6148
  79.7 23.0 %all-gather.7.cloned.1.call-start = ((), (), s32[]{:S(2)}) async-start(), calls=%async_computation.6 | async-start | bytes 1572864 | tf_op jit(solution)/shard_map/all_gather | solution.py:123
  91.1 11.6 %copy-start.50 = (f32[512]{0:T(512)S(1)}, f32[512]{0:T(512)}, u32[]{:S(2)}) copy-start(f32[512]{0:T(512)} %param.36) | copy-start | bytes 6148
  92.3 30.7 %reduce-scatter.7.cloned.1.call-start = ((), (), s32[]{:S(2)}) async-start(), calls=%async_computation.7 | async-start | bytes 1572864 | tf_op jit(solution)/shard_map/reduce_scatter | solution.py:127
  102.7 8.7 %copy-start.49 = (bf16[512,512]{1,0:T(8,128)(2,1)S(1)}, bf16[512,512]{1,0:T(8,128)(2,1)}, u32[]{:S(2)}) copy-start(bf16[512,512]{1,0:T(8,128)(2,1)} %param.37) | copy-start | bytes 1572868
  113.2 9.9 %copy-start.41 = (f32[512]{0:T(512)S(1)}, f32[512]{0:T(512)}, u32[]{:S(2)}) copy-start(f32[512]{0:T(512)} %param.38) | copy-start | bytes 6148
  113.2 26.8 %all-gather.9.cloned.1.call-start = ((), (), s32[]{:S(2)}) async-start(), calls=%async_computation.8 | async-start | bytes 1572864 | tf_op jit(solution)/shard_map/all_gather | solution.py:140
  116.0 8.8 %copy-start.28 = (f32[512]{0:T(512)S(1)}, f32[512]{0:T(512)}, u32[]{:S(2)}) copy-start(f32[512]{0:T(512)} %param.39) | copy-start | bytes 6148
  129.6 27.7 %reduce-scatter.9.cloned.1.call-start = ((), (), s32[]{:S(2)}) async-start(), calls=%async_computation.9 | async-start | bytes 1572864 | tf_op jit(solution)/shard_map/reduce_scatter | solution.py:147
  147.5 26.8 %all-gather.11.cloned.1.call-start = ((), (), s32[]{:S(2)}) async-start(), calls=%async_computation.10 | async-start | bytes 1572864 | tf_op jit(solution)/shard_map/all_gather | solution.py:157
  157.3 2.6 copy-start.15
  164.0 82.0 %reduce-scatter.11.cloned.1.call-start = ((), (), s32[]{:S(2)}) async-start(), calls=%async_computation.11 | async-start | bytes 1572864 | tf_op jit(solution)/shard_map/reduce_scatter | solution.py:210
  180.3 2.1 copy-start.2
  205.0 2.1 copy-start.2
  227.7 2.5 copy-start.13
  235.7 3.4 copy-start.48
  235.7 148.0 %all-reduce.7.cloned.1.call-start = ((), (), s32[]{:S(2)}) async-start(), calls=%async_computation.12 | async-start | bytes 2523136 | tf_op jit(solution)/shard_map/psum | solution.py:235
  239.1 3.0 copy-start.47
  243.2 2.8 copy-start.6
  244.1 3.3 copy-start.7
  244.1 3.3 copy-start.31
  244.1 3.3 copy-start.38
  246.0 2.7 copy-start.14
  248.4 311.3 %all-reduce.9.cloned.1.call-start = ((), (), s32[]{:S(2)}) async-start(), calls=%async_computation.13 | async-start | bytes 8388608 | tf_op jit(solution)/shard_map/psum | solution.py:253
  250.3 1.9 copy-start.11
  254.8 44.3 %copy-start.23 = (bf16[100,512]{1,0:T(8,128)(2,1)S(1)}, bf16[100,512]{1,0:T(8,128)(2,1)}, u32[]{:S(2)}) copy-start(bf16[100,512]{1,0:T(8,128)(2,1)} %param.28) | copy-start | bytes 307204
  254.8 44.6 %copy-start.32 = (f32[512]{0:T(512)S(1)}, f32[512]{0:T(512)}, u32[]{:S(2)}) copy-start(f32[512]{0:T(512)} %get-tuple-element.234) | copy-start | bytes 6148
  254.8 44.7 %copy-start.33 = (f32[512]{0:T(512)S(1)}, f32[512]{0:T(512)}, u32[]{:S(2)}) copy-start(f32[512]{0:T(512)} %get-tuple-element.294) | copy-start | bytes 6148
  254.8 44.7 %copy-start.34 = (f32[512]{0:T(512)S(1)}, f32[512]{0:T(512)}, u32[]{:S(2)}) copy-start(f32[512]{0:T(512)} %get-tuple-element.296) | copy-start | bytes 6148
  254.8 44.7 %copy-start.35 = (f32[512]{0:T(512)S(1)}, f32[512]{0:T(512)}, u32[]{:S(2)}) copy-start(f32[512]{0:T(512)} %get-tuple-element.232) | copy-start | bytes 6148
  254.8 44.7 %copy-start.36 = (f32[512]{0:T(512)S(1)}, f32[512]{0:T(512)}, u32[]{:S(2)}) copy-start(f32[512]{0:T(512)} %get-tuple-element.236) | copy-start | bytes 6148
  254.8 81.9 %copy-start.44 = (f32[100]{0:T(128)S(1)}, f32[100]{0:T(128)}, u32[]{:S(2)}) copy-start(f32[100]{0:T(128)} %copy-done.43) | copy-start | bytes 1204
  383.7 178.4 %copy-start.26 = (f32[100,512]{1,0:T(8,128)S(1)}, f32[100,512]{1,0:T(8,128)}, u32[]{:S(2)}) copy-start(f32[100,512]{1,0:T(8,128)} %get-tuple-element.492) | copy-start | bytes 614404
  559.7 3.1 copy-start.16
  563.9 2.7 copy-start.1
  (16 other events, 21.9 us)
Sparse Core Ops, SparseCore 0:
  55.9 8.8 all-gather.4
  79.8 9.6 reduce-scatter.4
  92.5 10.1 all-gather.6
  113.3 9.6 reduce-scatter.6
  129.8 10.1 all-gather.8
  147.6 9.6 reduce-scatter.8
  164.1 10.1 all-gather.10
  235.8 9.6 reduce-scatter.10
  251.6 132.0 all-reduce.6
  390.0 169.6 all-reduce.8
where the time goes:
time: 575 us; the launch traced here: 574 us
  waiting for transfers between devices  288 us (50%)
  blocking collectives  122 us (21%)
  matrix products  91.4 us (16%)
  local copies, waits for them, and re-layouts  31.1 us (5%)
  other arithmetic  24.1 us (4%)
  between operations  16.2 us (3%)
    psum x1, waiting for transfers between devices, per_device(): lax.psum((local_sharded[0], local_sharded[1], local_sharded[2], local_sha...  176 us
    psum x1, waiting for transfers between devices, per_device(): lax.psum((shared[0], shared[1], shared[2], shared[3], shared[4], shared[5...  46.1 us
    psum x1, blocking collectives, per_device(): lax.psum((local_sharded[0], local_sharded[1], local_sharded[2], local_sha...  42.7 us
    psum x1, blocking collectives, per_device(): lax.psum((jnp.sum(feats, axis=0), jnp.sum(feats * feats, axis=0)), ('rows...  42 us
    psum x1, blocking collectives, per_device(): feat_sums = lax.psum((feat_terms[0], feat_terms[1]), ('rows', 'heads'))  37.2 us
    dot_general x8, matrix products, product(): return jnp.dot(left, right, preferred_element_type=jnp.float32)  19.1 us
    unnamed x115, local copies, waits for them, and re-layouts  19 us
    dot_general x2, matrix products, attend_back(): jnp.einsum('hqk,qhd->khd', d_scores, query_block, preferred_element_type=...  17.7 us
  transfers between devices with their start and end apart: 10, of which 9 were waited for; matrix products, arithmetic and copies ran while one was open for 3% of the time, Pallas kernels for 0%

commit v1 on v0

v1 whole, which is shorter than its diff:
```python
import functools
import math

import jax
import jax.numpy as jnp
from jax import lax
from jax.experimental import pallas as pl
from jax.experimental.pallas import tpu as pltpu
from jax.sharding import PartitionSpec as P

BF = jnp.bfloat16
F32 = jnp.float32
MESH = pl.DeviceIdType.MESH
DH = 128
P_SIZE = 128
CONTEXT_MAX = 896
KEYS = CONTEXT_MAX + P_SIZE
EPS = 1e-05
HALF_ROOT = math.sqrt(0.5)
PDF_SCALE = 1.0 / math.sqrt(2.0 * math.pi)
LOG2E = math.log2(math.e)
SEMS = 400
VMEM_LIMIT = 60 * 2**20


def _dot(a, b, ca, cb):
    return lax.dot_general(a, b, (((ca,), (cb,)), ((), ())), preferred_element_type=F32)


def nn(a, b):
    return _dot(a, b, 1, 0)


def nt(a, b):
    return _dot(a, b, 1, 1)


def tn(a, b):
    return _dot(a, b, 0, 0)


def row_sum(v):
    return jnp.sum(v, axis=0, keepdims=True)


def lane_mean(v):
    return jnp.mean(v, axis=-1, keepdims=True)


class Links:
    def __init__(self, send, recv):
        self.send, self.recv, self.used, self.open = send, recv, 0, []

    def copy(self, src, dst, device):
        i = self.used
        self.used += 1
        assert i < SEMS
        c = pltpu.make_async_remote_copy(
            src_ref=src,
            dst_ref=dst,
            send_sem=self.send.at[i],
            recv_sem=self.recv.at[i],
            device_id=device,
            device_id_type=MESH,
        )
        c.start()
        self.open.append(c)
        return c

    def drain(self):
        for c in self.open:
            c.wait_send()
        self.open = []


class Loads:
    def __init__(self, sems):
        self.sems, self.used = sems, 0

    def copy(self, src, dst):
        c = pltpu.make_async_copy(src, dst, self.sems.at[self.used])
        self.used += 1
        c.start()
        return c


class Chunk:
    def __init__(self, ctx, refs, stages):
        self.ctx = ctx
        self.give, self.got, self.acc, self.recv, self.full = refs
        self.stages = stages
        self.n = self.acc.shape[0]
        self.at = 0
        self.core_copy = None

    def send_core(self):
        self.core_copy = self.ctx.links.copy(self.give, self.got, self.ctx.twin)

    def merge_core(self):
        self.core_copy.wait_recv()
        self.acc[...] = (self.acc[...].astype(F32) + self.got[...].astype(F32)).astype(BF)
        self.begin()

    def begin(self):
        self.base, self.len, self.off, self.k = 0, self.n, 0, 0
        self._start_scatter()

    def _digits(self, bits, mask):
        digit, row = 0, self.ctx.row
        for i, b in enumerate(bits):
            bit = (self.ctx.row // b) % 2
            if mask >> i & 1:
                row = row + b * (1 - 2 * bit)
                bit = 1 - bit
            digit = digit * 2 + bit
        return digit, row

    def _start_scatter(self):
        bits = self.stages[self.k]
        ways = 2 ** len(bits)
        q = self.len // ways
        self.copies = []
        for mask in range(1, ways):
            digit, row = self._digits(bits, mask)
            src = self.acc.at[pl.ds(pl.multiple_of(self.base + digit * q, 16), q)]
            dst = self.recv.at[pl.ds(self.off + (mask - 1) * q, q)]
            self.copies.append(self.ctx.links.copy(src, dst, (row, self.ctx.head)))

    def _end_scatter(self):
        bits = self.stages[self.k]
        ways = 2 ** len(bits)
        q = self.len // ways
        digit, _ = self._digits(bits, 0)
        self.base = self.base + digit * q
        mine = pl.ds(pl.multiple_of(self.base, 16), q)
        total = self.acc[mine, :].astype(F32)
        for i, c in enumerate(self.copies):
            c.wait_recv()
            total = total + self.recv[pl.ds(self.off + i * q, q), :].astype(F32)
        self.off += (ways - 1) * q
        self.len = q
        self.k += 1
        if self.k < len(self.stages):
            self.acc[mine, :] = total.astype(BF)
            self._start_scatter()
        else:
            self.full[mine, :] = total.astype(BF)
            self._start_gather()

    def _start_gather(self):
        bits = self.stages[self.k - 1]
        mine = pl.ds(pl.multiple_of(self.base, 16), self.len)
        self.copies = []
        for mask in range(1, 2 ** len(bits)):
            _, row = self._digits(bits, mask)
            self.copies.append(
                self.ctx.links.copy(self.full.at[mine], self.full.at[mine], (row, self.ctx.head))
            )

    def _end_gather(self):
        bits = self.stages[self.k - 1]
        for c in self.copies:
            c.wait_recv()
        digit, _ = self._digits(bits, 0)
        self.base = self.base - digit * self.len
        self.len = self.len * 2 ** len(bits)
        self.k -= 1
        if self.k > 0:
            self._start_gather()

    def steps(self):
        return 2 * len(self.stages)

    def advance(self):
        if self.at < len(self.stages):
            self._end_scatter()
        elif self.at < self.steps():
            self._end_gather()
        self.at += 1

    def finish(self):
        while self.at < self.steps():
            self.advance()


class Ctx:
    pass


def share_rows(ctx, slots, count):
    mine = slots.at[ctx.row]
    return [
        ctx.links.copy(mine, mine, (lax.rem(ctx.row + k, count), ctx.head)) for k in range(1, count)
    ]


IN_NAMES = [
    "feats", "mask", "splits", "pidx", "bank", "encw", "encb", "qkvw", "outw", "outb", "ag", "ash", "upw",
    "upb", "downw", "downb", "fg", "fsh", "cot",
]
OUT_NAMES = [
    "output", "uf", "rffn", "rqkv", "rbank", "vec", "late", "stat",
]


def layer_kernel(count, total_rows, stages, chunk_rows, names, *refs):
    g = Ctx()
    for name, ref in zip(names, refs, strict=True):
        setattr(g, name, ref)
    n, features = g.feats.shape
    ctx = Ctx()
    ctx.row, ctx.head = lax.axis_index("rows"), lax.axis_index("heads")
    h = ctx.head
    o = 1 - h
    ctx.twin = (ctx.row, o)
    ctx.links = links = Links(g.ssem, g.rsem)
    loads = Loads(g.lsem)

    l_feats = loads.copy(g.feats, g.F.at[h])
    own = {
        "qkv": (g.qkvw, g.WQKV.at[h]),
        "out": (g.outw, g.WO.at[h]),
        "upb": (g.upb, g.UB.at[h]),
        "up": (g.upw, g.WU.at[h]),
        "down": (g.downw, g.WD.at[h]),
    }
    barrier = pltpu.get_barrier_semaphore()
    pl.semaphore_signal(barrier, inc=1, device_id=ctx.twin, device_id_type=MESH)
    for k in range(1, count):
        pl.semaphore_signal(
            barrier, inc=1, device_id=(lax.rem(ctx.row + k, count), h), device_id_type=MESH
        )
    l_bank = loads.copy(g.bank, g.BANKV)
    l_own = {k: loads.copy(*v) for k, v in own.items()}
    l_cot = loads.copy(g.cot, g.COT)

    g.TILE[0] = jnp.zeros_like(g.TILE[0])
    g.LATE[0] = jnp.zeros_like(g.LATE[0])
    g.VEC[...] = jnp.zeros_like(g.VEC)
    l_feats.wait()
    f = g.F[h]
    g.TILE[0, 0:1, :features] = row_sum(f)
    g.TILE[0, 1:2, :features] = row_sum(f * f)
    pl.semaphore_wait(barrier, count)
    c_tile = links.copy(g.TILE.at[0], g.TILE.at[1], ctx.twin)
    c_feats = links.copy(g.feats, g.F.at[h], ctx.twin)
    c_tile.wait_recv()
    g.MOM[ctx.row] = g.TILE[0] + g.TILE[1]
    c_mom = share_rows(ctx, g.MOM, count)
    c_own = {k: links.copy(*v, ctx.twin) for k, v in own.items()}

    selector = lax.broadcasted_iota(jnp.int32, (g.bank.shape[0], P_SIZE), 0) == g.pidx[...]
    g.SEL[...] = jnp.where(selector, 1.0, 0.0).astype(BF)
    l_bank.wait()
    g.SRC[CONTEXT_MAX:KEYS, :] = tn(g.SEL[...], g.BANKV[...]).astype(BF)
    visible = lax.broadcasted_iota(jnp.int32, (KEYS, 1), 0)
    visible = (visible < g.splits[0]) | (visible >= CONTEXT_MAX)
    g.BIAS[...] = jnp.where(visible, 0.0, -1e30)
    for c in l_own.values():
        c.wait()
    c_own["qkv"].wait_recv()
    for j in range(4):
        s, w = j // 2, pl.ds(128 * (j % 2), 128)
        g.WKV[j, :, 0:128] = g.WQKV[s, 1, :, w]
        g.WKV[j, :, 128:256] = g.WQKV[s, 2, :, w]

    c_feats.wait_recv()
    for c in c_mom:
        c.wait_recv()
    moments = g.MOM[0]
    for k in range(1, count):
        moments = moments + g.MOM[k]
    mean = moments[0:1, :features] / total_rows
    var = moments[1:2, :features] / total_rows - mean * mean
    inverse = lax.rsqrt(var + EPS)
    live = g.mask[...].astype(F32)
    scale = live * jnp.sqrt(features / jnp.sum(live, axis=-1, keepdims=True))
    g.STAT[0:1, :features] = mean
    g.STAT[1:2, :features] = inverse
    g.STAT[2:3, :features] = scale

    for s in range(2):
        g.NL[s] = (((g.F[s] - mean) * inverse) * scale).astype(BF)
        hidden = nn(g.NL[s], g.encw[...]) + g.encb[...]
        g.HA[s] = hidden
        g.HB[s] = hidden.astype(BF)
    g.SRC[0:n, :] = g.HB[0]
    g.SRC[n:CONTEXT_MAX, :] = g.HB[1, 0 : CONTEXT_MAX - n, :]

    for s in range(2):
        q = nn(g.HB[h], g.WQKV[s, 0]).astype(BF)
        for j in range(2):
            g.Q[2 * s + j] = q[:, 128 * j : 128 * j + 128]

    def project(j, _):
        kv = nn(g.SRC[...], g.WKV[j]).astype(BF)
        g.K[j] = kv[:, 0:128]
        g.V[j] = kv[:, 128:256]
        return 0

    lax.fori_loop(0, 4, project, 0)

    def attend(j, _):
        for t in range(n // 256):
            cols = slice(256 * t, 256 * t + 256)
            scores = nt(g.K[j], g.Q[j, cols, :]) * (DH**-0.5 * LOG2E) + g.BIAS[...]
            e = jnp.exp2(scores - jnp.max(scores, axis=0, keepdims=True))
            inv = 1.0 / row_sum(e)
            g.INV[j, 0:1, cols] = inv
            e = e.astype(BF)
            g.E[j, :, cols] = e
            g.AT[j, :, cols] = (tn(g.V[j], e) * inv).astype(BF)
        return 0

    lax.fori_loop(0, 4, attend, 0)

    c_own["out"].wait_recv()
    c_own["up"].wait_recv()
    c_own["upb"].wait_recv()
    c_own["down"].wait_recv()
    for j in range(4):
        g.A[:, 128 * j : 128 * j + 128] = g.AT[j].T
    l_cot.wait()

    tile = 256

    def forward(t, _):
        rows = pl.ds(pl.multiple_of(t * tile, tile), tile)
        branch = nn(g.A[rows, 0:256], g.WO[0]) + nn(g.A[rows, 256:512], g.WO[1]) + g.outb[...]
        joined = g.HA[h, rows, :] + branch
        center = joined - lane_mean(joined)
        rstd = lax.rsqrt(lane_mean(center * center) + EPS)
        xhat = center * rstd
        after = xhat * g.ag[...] + g.ash[...]
        g.XH[rows, :] = xhat
        g.RS[rows, :] = rstd
        low = after.astype(BF)
        g.AB[rows, :] = low
        mixed = g.downb[...]
        for s in range(2):
            u = nn(low, g.WU[s]) + g.UB[s]
            phi = 0.5 * (1.0 + lax.erf(u * HALF_ROOT))
            g.DG[s, rows, :] = phi + u * (jnp.exp2(u * u * (-0.5 * LOG2E)) * PDF_SCALE)
            act = (u * phi).astype(BF)
            g.ACT[s, rows, :] = act
            mixed = mixed + nn(act, g.WD[s])
        joined = after + mixed
        center = joined - lane_mean(joined)
        rstd = lax.rsqrt(lane_mean(center * center) + EPS)
        xhat = center * rstd
        g.OUTB[rows, :] = xhat * g.fg[...] + g.fsh[...]
        ct = g.COT[rows, :]
        d = ct * g.fg[...]
        d = rstd * (d - lane_mean(d) - xhat * lane_mean(d * xhat))
        g.DJ[rows, :] = d
        gm = d.astype(BF)
        g.GM[rows, :] = gm
        g.VEC[4:5, :] += row_sum(gm.astype(F32))
        g.VEC[5:6, :] += row_sum(ct * xhat)
        g.VEC[6:7, :] += row_sum(ct)
        return 0

    lax.fori_loop(0, n // tile, forward, 0)
    l_output = loads.copy(g.OUTB, g.output)

    def put(ref, first, value):
        r = value.shape[0]
        for b in range(value.shape[1] // 128):
            ref[first + r * b : first + r * b + r, :] = value[:, 128 * b : 128 * b + 128]

    chunks = [
        Chunk(ctx, [getattr(g, f"{p}{i}") for p in ("CG", "CR", "CA", "CV", "CF")], stages[i])
        for i in range(len(chunk_rows))
    ]
    down, up, out, qkv0, qkv1, last = chunks

    put(down.give, 0, tn(g.ACT[o], g.GM[...]).astype(BF))
    down.send_core()
    put(down.acc, 0, tn(g.ACT[h], g.GM[...]).astype(BF))

    def backward(t, _):
        rows = pl.ds(pl.multiple_of(t * tile, tile), tile)
        gm = g.GM[rows, :]
        d = g.DJ[rows, :]
        for s in range(2):
            du = (g.DG[s, rows, :] * nt(gm, g.WD[s])).astype(BF)
            g.DU[s, rows, :] = du
            g.VEC[7 + s : 8 + s, :] += row_sum(du.astype(F32))
            d = d + nt(du, g.WU[s])
        xhat = g.XH[rows, :]
        g.VEC[2:3, :] += row_sum(d * xhat)
        g.VEC[3:4, :] += row_sum(d)
        d = d * g.ag[...]
        d = g.RS[rows, :] * (d - lane_mean(d) - xhat * lane_mean(d * xhat))
        g.DJ[rows, :] = d
        gb = d.astype(BF)
        g.GB[rows, :] = gb
        g.VEC[1:2, :] += row_sum(gb.astype(F32))
        return 0

    down.merge_core()
    lax.fori_loop(0, n // tile, backward, 0)
    put(up.give, 0, tn(g.AB[...], g.DU[o]).astype(BF))
    up.send_core()
    for j in range(2):
        put(out.give, 128 * j * 4, nn(g.AT[2 * o + j], g.GB[...]).astype(BF))
    out.send_core()
    c_vec = links.copy(g.VEC, g.VECR, ctx.twin)
    put(up.acc, 0, tn(g.AB[...], g.DU[h]).astype(BF))
    for j in range(2):
        put(out.acc, 128 * j * 4, nn(g.AT[2 * h + j], g.GB[...]).astype(BF))
    up.merge_core()
    out.merge_core()
    down.advance()

    for j in range(4):
        d = nt(g.WO[j // 2, 128 * (j % 2) : 128 * (j % 2) + 128, :], g.GB[...]).astype(BF)
        g.DOT[j] = d
        df = d.astype(F32)
        g.INNER[j, 0:1, :] = row_sum(df * g.AT[j].astype(F32))
        g.DOT2[j] = (df * g.INV[j, 0:1, :]).astype(BF)
        g.INV[j, 1:2, :] = g.INV[j, 0:1, :] * (DH**-0.5)

    c_vec.wait_recv()
    vec_sum = Ctx()
    vec_sum.k = 0

    def vec_start(value):
        bits = vec_stages[vec_sum.k]
        digit, _ = digits_of(bits, 0)
        slots = g.VECS.at[vec_sum.k]
        slots[digit] = value
        vec_sum.copies = []
        for mask in range(1, 2 ** len(bits)):
            _, row = digits_of(bits, mask)
            vec_sum.copies.append(links.copy(slots.at[digit], slots.at[digit], (row, h)))

    def vec_end():
        bits = vec_stages[vec_sum.k]
        for c in vec_sum.copies:
            c.wait_recv()
        value = g.VECS[vec_sum.k, 0]
        for i in range(1, 2 ** len(bits)):
            value = value + g.VECS[vec_sum.k, i]
        vec_sum.k += 1
        if vec_sum.k < len(vec_stages):
            vec_start(value)
        else:
            g.vec[...] = value

    digits_of = down._digits
    vec_stages = vec_groups(count)
    vec_start(g.VEC[...] + g.VECR[...])

    kv_copies = {}

    def attend_back(j):
        q, dot, dot2 = g.Q[j], g.DOT[j], g.DOT2[j]
        inner, factor = g.INNER[j, 0:1, :], g.INV[j, 1:2, :]

        def block(t, dq):
            rows = pl.ds(pl.multiple_of(t * 256, 256), 256)
            e = g.E[j, rows, :]
            upstream = nn(g.V[j, rows, :], dot)
            ds = (e.astype(F32) * ((upstream - inner) * factor)).astype(BF)
            g.DKV[j, rows, 0:128] = nn(ds, q).astype(BF)
            g.DKV[j, rows, 128:256] = nt(e, dot2).astype(BF)
            return dq + tn(g.K[j, rows, :], ds)

        dq = lax.fori_loop(0, KEYS // 256, block, jnp.zeros((128, n), F32))
        g.DQT[j] = dq.astype(BF)
        other = pl.ds(pl.multiple_of(o * n, n), n)
        kv_copies[j] = links.copy(g.DKV.at[j, other], g.DKVR.at[j], ctx.twin)

    def head_grads(j, chunk, ref):
        put(ref, 0, nt(g.HQT[...], g.DQT[j]).astype(BF))
        put(ref, n, nn(g.SRCT[...], g.DKVO[j]).astype(BF))

    def merge_kv(j):
        kv_copies[j].wait_recv()
        mine = pl.ds(pl.multiple_of(h * n, n), n)
        g.DKVO[j] = (g.DKV[j, mine, :].astype(F32) + g.DKVR[j].astype(F32)).astype(BF)

    g.HQT[...] = g.HB[h].T
    g.SRCT[...] = g.SRC[pl.ds(pl.multiple_of(h * n, n), n), :].T

    attend_back(0)
    down.advance()
    attend_back(2)
    up.advance()
    out.advance()
    merge_kv(0)
    merge_kv(2)

    def pair_grads(p, chunk):
        head_grads(2 * o + p, chunk, chunk.give)
        chunk.send_core()
        head_grads(2 * h + p, chunk, chunk.acc)

    pair_grads(0, qkv0)
    down.advance()
    up.advance()
    attend_back(1)
    qkv0.merge_core()
    out.advance()
    down.advance()
    up.advance()
    vec_end()
    attend_back(3)
    out.advance()
    down.advance()
    qkv0.advance()
    merge_kv(1)
    merge_kv(3)
    pair_grads(1, qkv1)

    kvh = nt(g.DKVO[0], g.WKV[0])
    for j in range(1, 4):
        kvh = kvh + nt(g.DKVO[j], g.WKV[j])
    edge = CONTEXT_MAX - n
    g.DP[0] = kvh[edge:n, :].astype(BF)
    c_prompt = links.copy(g.DP.at[0], g.DP.at[1], ctx.twin)
    for j in range(4):
        g.DQ[:, 128 * j : 128 * j + 128] = g.DQT[j].T
    dh = g.DJ[...]
    for j in range(4):
        w = g.WQKV[j // 2, 0, :, 128 * (j % 2) : 128 * (j % 2) + 128]
        dh = dh + nt(g.DQ[:, 128 * j : 128 * j + 128], w)
    gh = dh[0:edge] + kvh[0:edge]
    g.GH[0:edge, :] = gh.astype(BF)
    first = jnp.where(h == 0, 1.0, 0.0)
    g.GH[edge:n, :] = (dh[edge:n] + kvh[edge:n] * first).astype(BF)
    gh = g.GH[...]
    qkv1.merge_core()

    uf = nt(gh, g.encw[...]) * scale
    g.UF[...] = uf
    g.LATE[0, 0:1, :features] = row_sum(uf)
    g.LATE[0, 1:2, :features] = row_sum(uf * (g.F[h] - mean))
    eb = row_sum(gh.astype(F32))
    for b in range(4):
        g.LATE[0, 2 + b : 3 + b, :] = eb[:, 128 * b : 128 * b + 128]
    c_late = links.copy(g.LATE.at[0], g.LATE.at[1], ctx.twin)
    l_uf = loads.copy(g.UF, g.uf)
    c_late.wait_recv()
    g.LSUM[ctx.row] = g.LATE[0] + g.LATE[1]
    c_late_rows = share_rows(ctx, g.LSUM, count)

    enc = tn(g.NL[h], gh)
    g.ENC[0:features, :] = enc
    g.ENC[features:, :] = jnp.zeros_like(g.ENC[features:, :])
    bank_rows = g.bank.shape[0] // 2
    enc_at = bank_rows * 4
    for b in range(4):
        cols = slice(128 * b, 128 * b + 128)
        last.give[64 * b : 64 * b + 64, :] = g.ENC[pl.ds(pl.multiple_of(o * 64, 64), 64), cols].astype(BF)
        last.acc[enc_at + 64 * b : enc_at + 64 * b + 64, :] = g.ENC[
            pl.ds(pl.multiple_of(h * 64, 64), 64), cols
        ].astype(BF)
    last.send_core()
    c_prompt.wait_recv()
    put(
        last.acc,
        0,
        nn(g.SEL[pl.ds(pl.multiple_of(h * bank_rows, bank_rows), bank_rows), :], g.DP[o]).astype(BF),
    )
    last.core_copy.wait_recv()
    rows = slice(enc_at, enc_at + 256)
    last.acc[rows, :] = (last.acc[rows, :].astype(F32) + last.got[...].astype(F32)).astype(BF)
    if last.n > enc_at + 256:
        last.acc[enc_at + 256 :, :] = jnp.zeros_like(last.acc[enc_at + 256 :, :])
    last.begin()
    up.advance()
    out.advance()

    rest = [down, up, out, qkv0, qkv1, last]
    while any(c.at < c.steps() for c in rest):
        for c in rest:
            c.advance()
    if vec_sum.k < len(vec_stages):
        vec_end()
    c_last = links.copy(last.full, g.TWIN, ctx.twin)
    stores = [l_output, l_uf]
    at = 0
    for c in (down, up, out):
        stores.append(loads.copy(c.full, g.rffn.at[pl.ds(at, c.n)]))
        at += c.n
    at = 0
    for c in (qkv0, qkv1):
        stores.append(loads.copy(c.full.at[0:1536], g.rqkv.at[pl.ds(at, 1536)]))
        at += 1536
    for c in c_late_rows:
        c.wait_recv()
    late = g.LSUM[0]
    for k in range(1, count):
        late = late + g.LSUM[k]
    g.late[...] = late
    g.stat[...] = g.STAT[...]
    stores.append(loads.copy(last.full.at[0 : enc_at + 256], g.rbank.at[h]))
    c_last.wait_recv()
    stores.append(loads.copy(g.TWIN.at[0 : enc_at + 256], g.rbank.at[o]))
    for c in stores:
        c.wait()
    links.drain()


def vec_groups(count):
    bits = [2**i for i in range(count.bit_length() - 1)]
    return [tuple(bits[i : i + 2]) for i in range(0, len(bits), 2)]


def finish_kernel(total_rows, names, *refs):
    g = Ctx()
    for name, ref in zip(names, refs, strict=True):
        setattr(g, name, ref)
    h = lax.axis_index("heads")
    features = g.feats.shape[1]

    def block(ref, first, rows):
        return ref[first : first + rows, :].astype(F32)

    for b in range(4):
        cols = slice(128 * b, 128 * b + 128)
        g.o_down[:, cols] = block(g.rffn, 512 * b, 512)
        g.o_up[:, cols] = block(g.rffn, 2048 + 512 * b, 512)
        for j in range(2):
            g.o_out[128 * j : 128 * j + 128, cols] = block(g.rffn, 4096 + 512 * j + 128 * b, 128)
        for s in range(2):
            g.o_bank[256 * s : 256 * s + 256, cols] = g.rbank[s, 256 * b : 256 * b + 256, :].astype(F32)
        g.o_encw[0:64, cols] = g.rbank[0, 1024 + 64 * b : 1024 + 64 * b + 64, :].astype(F32)
        g.o_encw[64:features, cols] = g.rbank[1, 1024 + 64 * b : 1024 + 64 * b + features - 64, :].astype(F32)
        g.o_encb[:, cols] = g.late[2 + b : 3 + b, :]
    for c in range(3):
        for p in range(2):
            g.o_qkv[c, :, 128 * p : 128 * p + 128] = block(g.rqkv, 1536 * p + 512 * c, 512)
    g.o_outb[...] = g.vec[1:2, :]
    g.o_ag[...] = g.vec[2:3, :]
    g.o_ash[...] = g.vec[3:4, :]
    g.o_downb[...] = g.vec[4:5, :]
    g.o_fg[...] = g.vec[5:6, :]
    g.o_fsh[...] = g.vec[6:7, :]
    g.o_upb[...] = g.vec[pl.ds(7 + h, 1), :]
    mean, inverse = g.stat[0:1, :features], g.stat[1:2, :features]
    b1, b2 = g.late[0:1, :features], g.late[1:2, :features]
    var_grad = -0.5 * inverse * inverse * inverse * b2
    first = (-inverse * b1 - 2.0 * mean * var_grad) / total_rows
    g.o_feats[...] = g.uf[...] * inverse + first + g.feats[...] * (2.0 * var_grad / total_rows)
    g.o_output[...] = g.output[...]


def per_device(
    feats,
    feature_mask,
    splits,
    prompt_index,
    prompt_bank,
    enc_weight,
    enc_bias,
    qkv_weight,
    out_weight,
    out_bias,
    attn_gain,
    attn_shift,
    up_weight,
    up_bias,
    down_weight,
    down_bias,
    ffn_gain,
    ffn_shift,
    cotangent,
):
    n, features = feats.shape
    count = lax.axis_size("rows")
    total_rows = n * count * lax.axis_size("heads")
    d = prompt_bank.shape[1]
    args = [
        feats, feature_mask, splits, prompt_index, prompt_bank, enc_weight, enc_bias[None], qkv_weight, out_weight,
        out_bias[None], attn_gain[None], attn_shift[None], up_weight, up_bias[None], down_weight, down_bias[None],
        ffn_gain[None], ffn_shift[None], cotangent,
    ]
    vmem = pl.BlockSpec(memory_space=pltpu.VMEM)
    hbm = pl.BlockSpec(memory_space=pl.ANY)
    large = {"feats", "bank", "qkvw", "outw", "upw", "upb", "downw", "cot"}
    in_specs = [
        hbm if k in large else pl.BlockSpec(memory_space=pltpu.SMEM) if k == "splits" else vmem for k in IN_NAMES
    ]
    bits = [2**i for i in range(count.bit_length() - 1)]
    grain = 16 * count
    chunk_rows = [-(-r // grain) * grain for r in (2048, 2048, 1024, 1536, 1536, 1280)]
    if count == 16:
        x, y, z, w = bits
        stages = [
            [(x,), (y,), (z,), (w,)],
            [(y,), (z,), (x,), (w,)],
            [(z,), (x,), (y,), (w,)],
            [(x,), (y,), (z,), (w,)],
            [(z,), (x,), (y,), (w,)],
            [(y,), (x,), (z,), (w,)],
        ]
    else:
        stages = [vec_groups(count)] * 6
    S = jax.ShapeDtypeStruct
    outs = {
        "output": S((n, d), F32),
        "uf": S((n, features), F32),
        "rffn": S((sum(chunk_rows[:3]), 128), BF),
        "rqkv": S((3072, 128), BF),
        "rbank": S((2, 1280, 128), BF),
        "vec": S((16, d), F32),
        "late": S((8, 128), F32),
        "stat": S((8, 128), F32),
    }
    out_specs = [vmem if k in ("vec", "late", "stat") else hbm for k in OUT_NAMES]
    V = pltpu.VMEM
    scratch = {
        "F": V((2, n, features), F32),
        "WQKV": V((2, 3, d, 256), BF),
        "WO": V((2, 256, d), BF),
        "UB": V((2, 1, 512), F32),
        "WU": V((2, d, 512), BF),
        "WD": V((2, 512, d), BF),
        "BANKV": V(prompt_bank.shape, BF),
        "COT": V((n, d), F32),
        "TILE": V((2, 8, 128), F32),
        "LATE": V((2, 8, 128), F32),
        "MOM": V((count, 8, 128), F32),
        "LSUM": V((count, 8, 128), F32),
        "STAT": V((8, 128), F32),
        "VEC": V((16, d), F32),
        "VECR": V((16, d), F32),
        "VECS": V((len(vec_groups(count)), 4, 16, d), F32),
        "SEL": V((prompt_bank.shape[0], P_SIZE), BF),
        "SRC": V((KEYS, d), BF),
        "BIAS": V((KEYS, 1), F32),
        "WKV": V((4, d, 256), BF),
        "NL": V((2, n, features), BF),
        "HA": V((2, n, d), F32),
        "HB": V((2, n, d), BF),
        "Q": V((4, n, 128), BF),
        "K": V((4, KEYS, 128), BF),
        "V": V((4, KEYS, 128), BF),
        "E": V((4, KEYS, n), BF),
        "INV": V((4, 8, n), F32),
        "INNER": V((4, 8, n), F32),
        "AT": V((4, 128, n), BF),
        "A": V((n, d), BF),
        "XH": V((n, d), F32),
        "RS": V((n, 1), F32),
        "AB": V((n, d), BF),
        "DG": V((2, n, 512), F32),
        "ACT": V((2, n, 512), BF),
        "DU": V((2, n, 512), BF),
        "OUTB": V((n, d), F32),
        "DJ": V((n, d), F32),
        "GM": V((n, d), BF),
        "GB": V((n, d), BF),
        "DOT": V((4, 128, n), BF),
        "DOT2": V((4, 128, n), BF),
        "DKV": V((4, KEYS, 256), BF),
        "DKVR": V((4, n, 256), BF),
        "DKVO": V((4, n, 256), BF),
        "DQT": V((4, 128, n), BF),
        "DQ": V((n, d), BF),
        "HQT": V((d, n), BF),
        "SRCT": V((d, n), BF),
        "DP": V((2, P_SIZE, d), BF),
        "GH": V((n, d), BF),
        "UF": V((n, features), F32),
        "ENC": V((128, d), F32),
        "TWIN": V((chunk_rows[5], 128), BF),
    }
    for i, r in enumerate(chunk_rows):
        small = 256 if i == 5 else r
        scratch[f"CG{i}"] = V((small, 128), BF)
        scratch[f"CR{i}"] = V((small, 128), BF)
        scratch[f"CA{i}"] = V((r, 128), BF)
        scratch[f"CV{i}"] = V((r, 128), BF)
        scratch[f"CF{i}"] = V((r, 128), BF)
    scratch["ssem"] = pltpu.SemaphoreType.DMA((SEMS,))
    scratch["rsem"] = pltpu.SemaphoreType.DMA((SEMS,))
    scratch["lsem"] = pltpu.SemaphoreType.DMA((40,))
    names = IN_NAMES + OUT_NAMES + list(scratch)
    results = pl.pallas_call(
        functools.partial(layer_kernel, count, total_rows, stages, chunk_rows, names),
        out_shape=[outs[k] for k in OUT_NAMES],
        in_specs=in_specs,
        out_specs=out_specs,
        scratch_shapes=list(scratch.values()),
        compiler_params=pltpu.CompilerParams(
            collective_id=0, has_side_effects=True, vmem_limit_bytes=VMEM_LIMIT
        ),
        name="layer",
    )(*args)
    finals = {
        "o_output": S((n, d), F32),
        "o_feats": S((n, features), F32),
        "o_bank": S(prompt_bank.shape, F32),
        "o_encw": S(enc_weight.shape, F32),
        "o_encb": S((1, d), F32),
        "o_qkv": S(qkv_weight.shape, F32),
        "o_out": S(out_weight.shape, F32),
        "o_outb": S((1, d), F32),
        "o_ag": S((1, d), F32),
        "o_ash": S((1, d), F32),
        "o_up": S(up_weight.shape, F32),
        "o_upb": S((1, up_bias.shape[0]), F32),
        "o_down": S(down_weight.shape, F32),
        "o_downb": S((1, d), F32),
        "o_fg": S((1, d), F32),
        "o_fsh": S((1, d), F32),
    }
    final = pl.pallas_call(
        functools.partial(finish_kernel, total_rows, ["feats"] + OUT_NAMES + list(finals)),
        out_shape=list(finals.values()),
        in_specs=[vmem] * (1 + len(OUT_NAMES)),
        out_specs=[vmem] * len(finals),
        compiler_params=pltpu.CompilerParams(vmem_limit_bytes=VMEM_LIMIT),
        name="finish",
    )(feats, *results)
    return tuple(
        v[0] if k in ("o_encb", "o_outb", "o_ag", "o_ash", "o_upb", "o_downb", "o_fg", "o_fsh") else v
        for k, v in zip(finals, final, strict=True)
    )


def solution(mesh):
    whole = P(("rows", "heads"), None)
    placed = (
        whole, P("rows", None), P("rows"), P("rows", None), P(), P(), P(), P(None, None, "heads"), P("heads", None),
        P(), P(), P(), P(None, "heads"), P("heads"), P("heads", None), P(), P(), P(), whole,
    )
    return jax.shard_map(
        per_device,
        mesh=mesh,
        in_specs=placed,
        out_specs=(
            whole, whole, P(), P(), P(), P(None, None, "heads"), P("heads", None), P(), P(), P(), P(None, "heads"),
            P("heads"), P("heads", None), P(), P(), P(),
        ),
        check_vma=False,
    )
```

time: 575 us -> 126 us (0.22)
  waiting for transfers between devices: 288 us -> 0 us
  blocking collectives: 122 us -> 0 us
  Pallas kernels: 0 us -> 120 us
  matrix products: 91.4 us -> 0 us
  local copies, waits for them, and re-layouts: 31.1 us -> 3.55 us
  other arithmetic: 24.1 us -> 0 us
  between operations: 16.2 us -> 1.31 us
    psum x2 -> x0, waiting for transfers between devices: 222 us -> none  [the longest x1 176 us: per_device(): lax.psum((local_sharded[0], local_sharded[1], local_sharded[2], local_sha...]
    psum x3 -> x0, blocking collectives: 122 us -> none  [the longest x1 42.7 us: per_device(): lax.psum((local_sharded[0], local_sharded[1], local_sharded[2], local_sha...]
    pallas_call x0 -> x2, Pallas kernels: none -> 120 us  [the longest x1 115 us: per_device(): pl.pallas_call(functools.partial(layer_kernel, count, total_rows, stages,...]
    dot_general x37 -> x0, matrix products: 91.4 us -> none  [the longest x8 19.1 us: product(): return jnp.dot(left, right, preferred_element_type=jnp.float32)]
    all_gather x4 -> x0, waiting for transfers between devices: 38.7 us -> none  [the longest x1 10.3 us: per_device(): episode_grad_mixed = lax.all_gather(grad_mixed, 'heads', axis=0, tiled=True)]
    reduce_scatter x4 -> x0, waiting for transfers between devices: 26.7 us -> none  [the longest x1 9.81 us: per_device(): lax.psum_scatter(product_nt(d_upper, up_weight).astype(jnp.bfloat16), 'he...]
    reduce_sum x16 -> x0, other arithmetic: 18.8 us -> none  [the longest x4 6.07 us: normalize(): center = values - jnp.mean(values, axis=-1, keepdims=True)]
    unnamed x115 -> x2, local copies, waits for them, and re-layouts: 19 us -> 3.55 us
  transfers between devices with their start and end apart: 10 -> 0, of which waited for: 9 -> 0; matrix products, arithmetic and copies ran while one was open for 3% -> 0% of each run, Pallas kernels for 0% -> 0%
where the time goes in v1:
time: 126 us; the launch traced here: 125 us
  Pallas kernels  120 us (95%)
  local copies, waits for them, and re-layouts  3.55 us (3%)
  between operations  1.31 us (1%)
    pallas_call x1, Pallas kernels, per_device(): pl.pallas_call(functools.partial(layer_kernel, count, total_rows, stages,...  115 us
    pallas_call x1, Pallas kernels, per_device(): pl.pallas_call(functools.partial(finish_kernel, total_rows, ['feats'] + O...  5.19 us
    unnamed x2, local copies, waits for them, and re-layouts  3.55 us

profile of v1, /device:TPU:0, one launch (start us, length us, event | category | flops | bytes accessed | tf_op | source)
XLA Modules:
  0.0 125.2 jit_solution(926407519974570671)
XLA Ops:
  1.3 1.8 %copy.36.refs_0_ = f32[512,100]{1,0:T(8,128)} copy(f32[512,100]{0,1:T(8,128)} %param.19) | data formatting | bytes 409600 | tf_op args[0]
  3.1 115.2 %layer.1 = (f32[512,512]{1,0:T(8,128)}, f32[512,100]{1,0:T(8,128)}, bf16[5120,128]{1,0:T(8,128)(2,1)}, bf16[3072,128]{1,0:T(8,128)(2,1)}, bf16[2,1280,128]{2,1,0...) custom-call(f32[512,100]{1,0:T(8,128)} %copy.36.refs_0_, s32[1,100]{1,0:T(1,128)} %refs_1_.1, ...), custom_call_target="tpu_custom_call" | custom-call | tf_op jit(solution)/shard_map/layer/pallas_call | solution.py:783
  118.2 5.2 %finish.1 = (f32[512,512]{1,0:T(8,128)}, f32[512,100]{1,0:T(8,128)}, f32[512,512]{1,0:T(8,128)}, f32[100,512]{1,0:T(8,128)}, f32[1,512]{1,0:T(1,128)}, /*index=5...) custom-call(f32[512,100]{1,0:T(8,128)} %copy.36.refs_0_, ...), custom_call_target="tpu_custom_call" | custom-call | tf_op jit(solution)/shard_map/finish/pallas_call | solution.py:812
  123.4 1.8 %copy.37 = f32[512,100]{0,1:T(8,128)} copy(f32[512,100]{1,0:T(8,128)} %get-tuple-element.65) | data formatting | bytes 409600

commit v2 on v1

v2 whole, which is shorter than its diff:
```python
import functools
import math

import jax
import jax.numpy as jnp
from jax import lax
from jax.experimental import pallas as pl
from jax.experimental.pallas import tpu as pltpu
from jax.sharding import PartitionSpec as P

BF = jnp.bfloat16
F32 = jnp.float32
MESH = pl.DeviceIdType.MESH
DH = 128
P_SIZE = 128
CONTEXT_MAX = 896
KEYS = CONTEXT_MAX + P_SIZE
EPS = 1e-05
HALF_ROOT = math.sqrt(0.5)
PDF_SCALE = 1.0 / math.sqrt(2.0 * math.pi)
LOG2E = math.log2(math.e)
VMEM_LIMIT = 60 * 2**20


def _dot(a, b, ca, cb):
    return lax.dot_general(a, b, (((ca,), (cb,)), ((), ())), preferred_element_type=F32)


def nn(a, b):
    return _dot(a, b, 1, 0)


def nt(a, b):
    return _dot(a, b, 1, 1)


def tn(a, b):
    return _dot(a, b, 0, 0)


def row_sum(v):
    return jnp.sum(v, axis=0, keepdims=True)


def lane_mean(v):
    return jnp.mean(v, axis=-1, keepdims=True)


class Links:
    def __init__(self, send, recv):
        self.send, self.recv, self.sent, self.received, self.open = send, recv, 0, 0, []

    def send_sem(self):
        self.sent += 1
        return self.send.at[self.sent - 1]

    def recv_sem(self):
        self.received += 1
        return self.recv.at[self.received - 1]

    def start(self, src, dst, device, send, recv):
        c = pltpu.make_async_remote_copy(
            src_ref=src, dst_ref=dst, send_sem=send, recv_sem=recv, device_id=device, device_id_type=MESH
        )
        c.start()
        return c

    def copy(self, src, dst, device):
        c = self.start(src, dst, device, self.send_sem(), self.recv_sem())
        self.open.append(c.wait_send)
        return c

    def drain(self):
        for wait in self.open:
            wait()
        self.open = []


def wait_bytes(ref, sem):
    pltpu.make_async_copy(ref, ref, sem).wait()


class Loads:
    def __init__(self, sems):
        self.sems, self.used = sems, 0

    def copy(self, src, dst):
        c = pltpu.make_async_copy(src, dst, self.sems.at[self.used])
        self.used += 1
        c.start()
        return c


class Part:
    def __init__(self, ctx, block, first, rows, stages):
        self.ctx, self.first, self.rows, self.stages = ctx, first, rows, stages
        self.acc, self.recv, self.full = block.acc, block.recv, block.full
        self.at = 0
        self.send_sem = None

    def begin(self):
        self.base, self.len, self.off, self.k = self.first, self.rows, self.first, 0
        self.send_sem = self.ctx.links.send_sem()
        self._start_scatter()

    def _digits(self, bits, mask):
        digit, row = 0, self.ctx.row
        for i, b in enumerate(bits):
            bit = (self.ctx.row // b) % 2
            if mask >> i & 1:
                row = row + b * (1 - 2 * bit)
                bit = 1 - bit
            digit = digit * 2 + bit
        return digit, row

    def _wait(self, rows):
        view = self.full.at[pl.ds(0, rows)]
        wait_bytes(view, self.recv_sem)
        wait_bytes(view, self.send_sem)

    def _start_scatter(self):
        bits = self.stages[self.k]
        ways = 2 ** len(bits)
        q = self.len // ways
        self.recv_sem = self.ctx.links.recv_sem()
        for mask in range(1, ways):
            digit, row = self._digits(bits, mask)
            src = self.acc.at[pl.ds(pl.multiple_of(self.base + digit * q, 16), q)]
            dst = self.recv.at[pl.ds(self.off + (mask - 1) * q, q)]
            self.ctx.links.start(src, dst, (row, self.ctx.head), self.send_sem, self.recv_sem)

    def _end_scatter(self):
        bits = self.stages[self.k]
        ways = 2 ** len(bits)
        q = self.len // ways
        digit, _ = self._digits(bits, 0)
        self.base = self.base + digit * q
        mine = pl.ds(pl.multiple_of(self.base, 16), q)
        self._wait((ways - 1) * q)
        total = self.acc[mine, :].astype(F32)
        for i in range(ways - 1):
            total = total + self.recv[pl.ds(self.off + i * q, q), :].astype(F32)
        self.off += (ways - 1) * q
        self.len = q
        self.k += 1
        if self.k < len(self.stages):
            self.acc[mine, :] = total.astype(BF)
            self._start_scatter()
        else:
            self.full[mine, :] = total.astype(BF)
            self._start_gather()

    def _start_gather(self):
        bits = self.stages[self.k - 1]
        mine = self.full.at[pl.ds(pl.multiple_of(self.base, 16), self.len)]
        self.recv_sem = self.ctx.links.recv_sem()
        for mask in range(1, 2 ** len(bits)):
            _, row = self._digits(bits, mask)
            self.ctx.links.start(mine, mine, (row, self.ctx.head), self.send_sem, self.recv_sem)

    def _end_gather(self):
        bits = self.stages[self.k - 1]
        ways = 2 ** len(bits)
        self._wait((ways - 1) * self.len)
        digit, _ = self._digits(bits, 0)
        self.base = self.base - digit * self.len
        self.len = self.len * ways
        self.k -= 1
        if self.k > 0:
            self._start_gather()

    def done(self):
        return self.at == 2 * len(self.stages)

    def advance(self):
        if self.at < len(self.stages):
            self._end_scatter()
        elif not self.done():
            self._end_gather()
        self.at += 1


class Block:
    def __init__(self, ctx, refs, cuts):
        self.ctx = ctx
        self.give, self.got, self.acc, self.recv, self.full = refs
        self.n = self.acc.shape[0]
        self.parts, first = [], 0
        for rows, stages in cuts:
            self.parts.append(Part(ctx, self, first, rows, stages))
            first += rows

    def send_core(self):
        self.core_copy = self.ctx.links.copy(self.give, self.got, self.ctx.twin)

    def merge_core(self):
        self.core_copy.wait_recv()
        for part in self.parts:
            rows = slice(part.first, part.first + part.rows)
            self.acc[rows, :] = (self.acc[rows, :].astype(F32) + self.got[rows, :].astype(F32)).astype(BF)
            part.begin()


class Ctx:
    pass


def share_rows(ctx, slots, count):
    mine = slots.at[ctx.row]
    send, recv = ctx.links.send_sem(), ctx.links.recv_sem()
    for k in range(1, count):
        ctx.links.start(mine, mine, (lax.rem(ctx.row + k, count), ctx.head), send, recv)
    others = slots.at[pl.ds(0, count - 1)]
    ctx.links.open.append(functools.partial(wait_bytes, others, send))
    return functools.partial(wait_bytes, others, recv)


SMALL = [
    "mask", "pidx", "encw", "encb", "outb", "ag", "ash", "downb", "fg", "fsh",
]
IN_NAMES = [
    "feats", "mask", "splits", "pidx", "bank", "encw", "encb", "qkvw", "outw", "outb", "ag", "ash", "upw",
    "upb", "downw", "downb", "fg", "fsh", "cot",
]
OUT_NAMES = [
    "output", "uf", "rffn", "rqkv", "rbank", "vec", "late", "stat",
]
CUTS = {
    "d": [(1024, [(1, 2), (4, 8)]), (1024, [(1, 2), (4, 8)])],
    "u": [(1024, [(2,), (1,), (4, 8)]), (1024, [(1,), (2,), (4, 8)])],
    "o": [(1024, [(1,), (2,), (4, 8)])],
    "q": [(768, [(1, 2), (4,), (8,)]), (768, [(4,), (1, 2), (8,)])],
    "r": [(512, [(2,), (1, 4), (8,)]), (512, [(2, 4), (1,), (8,)]), (512, [(1,), (2, 4), (8,)])],
    "l": [(512, [(1,), (2,), (4, 8)]), (512, [(4, 8), (1, 2)]), (256, [(1, 2), (4,), (8,)])],
}
PLAN = [
    [],
    [],
    [],
    ["d0"],
    [],
    [],
    ["d1", "d0"],
    ["u0", "u1"],
    ["d1", "o0", "d0"],
    ["u1", "u0"],
    [],
    ["d1", "o0"],
    ["q1", "u1", "d0", "u0"],
    ["o0", "q0"],
    ["u1", "d1", "q1", "r2", "u0", "r0"],
    ["o0", "q0", "r1", "l0"],
    ["l2", "l1", "u1", "q1", "u0", "r2", "r0", "r1", "q0", "o0", "l2", "l0", "l1", "q1", "r2", "r0", "r1", "q0", "l2", "u1", "l0", "u0", "r2", "r0", "r1", "q0", "l2", "o0", "l1", "l0", "r2", "q1", "l2", "r0", "r1", "l0", "q0", "l1", "r2", "r0", "l2", "q1", "l0", "r1"],
]


def layer_kernel(count, total_rows, cuts, plan, sem_counts, names, *refs):
    g = Ctx()
    for name, ref in zip(names, refs, strict=True):
        setattr(g, name, ref)
    features, n = g.feats.shape
    ctx = Ctx()
    ctx.row, ctx.head = lax.axis_index("rows"), lax.axis_index("heads")
    h = ctx.head
    o = 1 - h
    ctx.twin = (ctx.row, o)
    ctx.links = links = Links(g.ssem, g.rsem)
    loads = Loads(g.lsem)

    l_feats = loads.copy(g.feats, g.F.at[h])
    own = {
        "qkv": (g.qkvw, g.WQKV.at[h]),
        "out": (g.outw, g.WO.at[h]),
        "upb": (g.upb, g.UB.at[h]),
        "up": (g.upw, g.WU.at[h]),
        "down": (g.downw, g.WD.at[h]),
    }
    g.TILE[...] = jnp.zeros_like(g.TILE)
    barrier = pltpu.get_barrier_semaphore()
    pl.semaphore_signal(barrier, inc=1, device_id=ctx.twin, device_id_type=MESH)
    for k in range(1, count):
        pl.semaphore_signal(
            barrier, inc=1, device_id=(lax.rem(ctx.row + k, count), h), device_id_type=MESH
        )
    l_small = [loads.copy(getattr(g, k), getattr(g, k + "_")) for k in SMALL]
    l_bank = loads.copy(g.bank, g.BANKV)
    l_own = {k: loads.copy(*v) for k, v in own.items()}
    l_cot = loads.copy(g.cot, g.COT)

    def to_rows(columns):
        for i, c in enumerate(columns):
            g.SQUARE[0:features, i : i + 1] = c
        return g.SQUARE[...].T[0:8, :]

    def lane_sum(v):
        return jnp.sum(v, axis=-1, keepdims=True)

    g.SQUARE[...] = jnp.zeros_like(g.SQUARE)
    l_feats.wait()
    f = g.F[h]
    g.TILE[0] = to_rows([lane_sum(f), lane_sum(f * f)])
    pl.semaphore_wait(barrier, count)
    c_tile = links.copy(g.TILE.at[0], g.TILE.at[1], ctx.twin)
    c_feats = links.copy(g.feats, g.F.at[h], ctx.twin)
    c_tile.wait_recv()
    g.MOM[ctx.row] = g.TILE[0] + g.TILE[1]
    wait_moments = share_rows(ctx, g.MOM, count)
    c_own = {k: links.copy(*v, ctx.twin) for k, v in own.items()}

    for c in l_small:
        c.wait()
    selector = lax.broadcasted_iota(jnp.int32, (g.bank.shape[0], P_SIZE), 0) == g.pidx_[...]
    g.SEL[...] = jnp.where(selector, 1.0, 0.0).astype(BF)
    l_bank.wait()
    g.SRC[CONTEXT_MAX:KEYS, :] = tn(g.SEL[...], g.BANKV[...]).astype(BF)
    visible = lax.broadcasted_iota(jnp.int32, (KEYS, 1), 0)
    visible = (visible < g.splits[0]) | (visible >= CONTEXT_MAX)
    g.BIAS[...] = jnp.where(visible, 0.0, -1e30)
    g.VEC[...] = jnp.zeros_like(g.VEC)
    g.LATE[0] = jnp.zeros_like(g.LATE[0])
    live = g.mask_[...].astype(F32)
    scale = live * jnp.sqrt(features / jnp.sum(live, axis=-1, keepdims=True))
    g.STAT[...] = jnp.zeros_like(g.STAT)
    g.STAT[2:3, 0:features] = scale
    for c in l_own.values():
        c.wait()
    c_own["qkv"].wait_recv()
    for j in range(4):
        s, w = j // 2, pl.ds(128 * (j % 2), 128)
        g.WKV[j, :, 0:128] = g.WQKV[s, 1, :, w]
        g.WKV[j, :, 128:256] = g.WQKV[s, 2, :, w]

    c_feats.wait_recv()
    wait_moments()
    moments = g.MOM[0]
    for k in range(1, count):
        moments = moments + g.MOM[k]
    mean = moments[0:1, :] / total_rows
    var = moments[1:2, :] / total_rows - mean * mean
    g.STAT[0:1, :] = mean
    g.STAT[1:2, :] = lax.rsqrt(var + EPS)
    g.SQUARE[0:8, :] = g.STAT[...]
    columns = g.SQUARE[...].T
    mean, inverse, scale = [columns[0:features, i : i + 1] for i in range(3)]
    g.COLS[...] = columns[0:features, :]

    for s in range(2):
        g.NL[s] = (((g.F[s] - mean) * inverse) * scale).astype(BF)
        hidden = tn(g.NL[s], g.encw_[...]) + g.encb_[...]
        g.HA[s] = hidden
        g.HB[s] = hidden.astype(BF)
    g.SRC[0:n, :] = g.HB[0]
    g.SRC[n:CONTEXT_MAX, :] = g.HB[1, 0 : CONTEXT_MAX - n, :]

    for s in range(2):
        q = nn(g.HB[h], g.WQKV[s, 0]).astype(BF)
        for j in range(2):
            g.Q[2 * s + j] = q[:, 128 * j : 128 * j + 128]

    def project(j, _):
        kv = nn(g.SRC[...], g.WKV[j]).astype(BF)
        g.K[j] = kv[:, 0:128]
        g.V[j] = kv[:, 128:256]
        return 0

    lax.fori_loop(0, 4, project, 0)

    def attend(j, _):
        for t in range(n // 256):
            cols = slice(256 * t, 256 * t + 256)
            scores = nt(g.K[j], g.Q[j, cols, :]) * (DH**-0.5 * LOG2E) + g.BIAS[...]
            e = jnp.exp2(scores - jnp.max(scores, axis=0, keepdims=True))
            inv = 1.0 / row_sum(e)
            g.INV[j, 0:1, cols] = inv
            e = e.astype(BF)
            g.E[j, :, cols] = e
            g.AT[j, :, cols] = (tn(g.V[j], e) * inv).astype(BF)
        return 0

    lax.fori_loop(0, 4, attend, 0)

    c_own["out"].wait_recv()
    c_own["up"].wait_recv()
    c_own["upb"].wait_recv()
    c_own["down"].wait_recv()
    for j in range(4):
        g.A[:, 128 * j : 128 * j + 128] = g.AT[j].T
    l_cot.wait()

    tile = 256

    def forward(t, _):
        rows = pl.ds(pl.multiple_of(t * tile, tile), tile)
        branch = nn(g.A[rows, 0:256], g.WO[0]) + nn(g.A[rows, 256:512], g.WO[1]) + g.outb_[...]
        joined = g.HA[h, rows, :] + branch
        center = joined - lane_mean(joined)
        rstd = lax.rsqrt(lane_mean(center * center) + EPS)
        xhat = center * rstd
        after = xhat * g.ag_[...] + g.ash_[...]
        g.XH[rows, :] = xhat
        g.RS[rows, :] = rstd
        low = after.astype(BF)
        g.AB[rows, :] = low
        mixed = g.downb_[...]
        for s in range(2):
            u = nn(low, g.WU[s]) + g.UB[s]
            phi = 0.5 * (1.0 + lax.erf(u * HALF_ROOT))
            g.DG[s, rows, :] = phi + u * (jnp.exp2(u * u * (-0.5 * LOG2E)) * PDF_SCALE)
            act = (u * phi).astype(BF)
            g.ACT[s, rows, :] = act
            mixed = mixed + nn(act, g.WD[s])
        joined = after + mixed
        center = joined - lane_mean(joined)
        rstd = lax.rsqrt(lane_mean(center * center) + EPS)
        xhat = center * rstd
        g.OUTB[rows, :] = xhat * g.fg_[...] + g.fsh_[...]
        ct = g.COT[rows, :]
        d = ct * g.fg_[...]
        d = rstd * (d - lane_mean(d) - xhat * lane_mean(d * xhat))
        g.DJ[rows, :] = d
        gm = d.astype(BF)
        g.GM[rows, :] = gm
        g.VEC[4:5, :] += row_sum(gm.astype(F32))
        g.VEC[5:6, :] += row_sum(ct * xhat)
        g.VEC[6:7, :] += row_sum(ct)
        return 0

    lax.fori_loop(0, n // tile, forward, 0)
    l_output = loads.copy(g.OUTB, g.output)

    def put(ref, first, value):
        r = value.shape[0]
        for b in range(value.shape[1] // 128):
            ref[first + r * b : first + r * b + r, :] = value[:, 128 * b : 128 * b + 128]

    blocks = {
        k: Block(ctx, [getattr(g, p + k) for p in ("CG", "CR", "CA", "CV", "CF")], v) for k, v in cuts.items()
    }
    down, up, out, qkv0, qkv1, last = blocks.values()

    def tick(i):
        for k in plan[i] if i < len(plan) else []:
            blocks[k[0]].parts[int(k[1])].advance()

    put(down.give, 0, tn(g.ACT[o], g.GM[...]).astype(BF))
    down.send_core()
    put(down.acc, 0, tn(g.ACT[h], g.GM[...]).astype(BF))
    down.merge_core()

    def backward(t):
        rows = slice(t * tile, t * tile + tile)
        gm = g.GM[rows, :]
        d = g.DJ[rows, :]
        for s in range(2):
            du = (g.DG[s, rows, :] * nt(gm, g.WD[s])).astype(BF)
            g.DU[s, rows, :] = du
            g.VEC[7 + s : 8 + s, :] += row_sum(du.astype(F32))
            d = d + nt(du, g.WU[s])
        xhat = g.XH[rows, :]
        g.VEC[2:3, :] += row_sum(d * xhat)
        g.VEC[3:4, :] += row_sum(d)
        d = d * g.ag_[...]
        d = g.RS[rows, :] * (d - lane_mean(d) - xhat * lane_mean(d * xhat))
        g.DJ[rows, :] = d
        gb = d.astype(BF)
        g.GB[rows, :] = gb
        g.VEC[1:2, :] += row_sum(gb.astype(F32))

    for t in range(n // tile):
        backward(t)
    tick(2)
    put(up.give, 0, tn(g.AB[...], g.DU[o]).astype(BF))
    up.send_core()
    for j in range(2):
        put(out.give, 128 * j * 4, nn(g.AT[2 * o + j], g.GB[...]).astype(BF))
    out.send_core()
    c_vec = links.copy(g.VEC, g.VECR, ctx.twin)
    put(up.acc, 0, tn(g.AB[...], g.DU[h]).astype(BF))
    for j in range(2):
        put(out.acc, 128 * j * 4, nn(g.AT[2 * h + j], g.GB[...]).astype(BF))
    tick(3)
    up.merge_core()
    out.merge_core()
    tick(4)

    for j in range(4):
        d = nt(g.WO[j // 2, 128 * (j % 2) : 128 * (j % 2) + 128, :], g.GB[...]).astype(BF)
        g.DOT[j] = d
        df = d.astype(F32)
        g.INNER[j, 0:1, :] = row_sum(df * g.AT[j].astype(F32))
        g.DOT2[j] = (df * g.INV[j, 0:1, :]).astype(BF)
        g.INV[j, 1:2, :] = g.INV[j, 0:1, :] * (DH**-0.5)

    vec_stages = vec_groups(count)
    vec = Ctx()
    vec.k = 0

    def vec_start(value):
        bits = vec_stages[vec.k]
        digit, _ = down.parts[0]._digits(bits, 0)
        slots = g.VECS.at[vec.k]
        slots[digit] = value
        send, vec.sem = links.send_sem(), links.recv_sem()
        others = slots.at[pl.ds(0, 2 ** len(bits) - 1)]
        for mask in range(1, 2 ** len(bits)):
            _, row = down.parts[0]._digits(bits, mask)
            links.start(slots.at[digit], slots.at[digit], (row, h), send, vec.sem)
        links.open.append(functools.partial(wait_bytes, others, send))

    def vec_end():
        ways = 2 ** len(vec_stages[vec.k])
        wait_bytes(g.VECS.at[vec.k, pl.ds(0, ways - 1)], vec.sem)
        value = g.VECS[vec.k, 0]
        for i in range(1, ways):
            value = value + g.VECS[vec.k, i]
        vec.k += 1
        if vec.k < len(vec_stages):
            vec_start(value)
        else:
            g.vec[...] = value

    kv_copies = {}

    def attend_back(j):
        q, dot, dot2 = g.Q[j], g.DOT[j], g.DOT2[j]
        inner, factor = g.INNER[j, 0:1, :], g.INV[j, 1:2, :]

        def block(t, dq):
            rows = pl.ds(pl.multiple_of(t * 256, 256), 256)
            e = g.E[j, rows, :]
            upstream = nn(g.V[j, rows, :], dot)
            ds = (e.astype(F32) * ((upstream - inner) * factor)).astype(BF)
            g.DKV[j, rows, 0:128] = nn(ds, q).astype(BF)
            g.DKV[j, rows, 128:256] = nt(e, dot2).astype(BF)
            return dq + tn(g.K[j, rows, :], ds)

        dq = lax.fori_loop(0, KEYS // 256, block, jnp.zeros((128, n), F32))
        g.DQT[j] = dq.astype(BF)
        other = pl.ds(pl.multiple_of(o * n, n), n)
        kv_copies[j] = links.copy(g.DKV.at[j, other], g.DKVR.at[j], ctx.twin)

    def merge_kv(j):
        kv_copies[j].wait_recv()
        mine = pl.ds(pl.multiple_of(h * n, n), n)
        g.DKVO[j] = (g.DKV[j, mine, :].astype(F32) + g.DKVR[j].astype(F32)).astype(BF)

    def head_grads(j, ref):
        put(ref, 0, nt(g.HQT[...], g.DQT[j]).astype(BF))
        put(ref, n, nn(g.SRCT[...], g.DKVO[j]).astype(BF))

    def pair_grads(p, block):
        head_grads(2 * o + p, block.give)
        block.send_core()
        head_grads(2 * h + p, block.acc)

    g.HQT[...] = g.HB[h].T
    g.SRCT[...] = g.SRC[pl.ds(pl.multiple_of(h * n, n), n), :].T
    tick(5)
    attend_back(0)
    tick(6)
    attend_back(2)
    tick(7)
    merge_kv(0)
    merge_kv(2)
    pair_grads(0, qkv0)
    tick(8)
    qkv0.merge_core()
    c_vec.wait_recv()
    vec_start(g.VEC[...] + g.VECR[...])
    tick(9)
    attend_back(1)
    tick(10)
    attend_back(3)
    tick(11)
    vec_end()
    merge_kv(1)
    merge_kv(3)
    pair_grads(1, qkv1)
    tick(12)
    qkv1.merge_core()
    tick(13)

    kvh = nt(g.DKVO[0], g.WKV[0])
    for j in range(1, 4):
        kvh = kvh + nt(g.DKVO[j], g.WKV[j])
    edge = CONTEXT_MAX - n
    g.DP[0] = kvh[edge:n, :].astype(BF)
    c_prompt = links.copy(g.DP.at[0], g.DP.at[1], ctx.twin)
    for j in range(4):
        g.DQ[:, 128 * j : 128 * j + 128] = g.DQT[j].T
    dh = g.DJ[...]
    for j in range(4):
        w = g.WQKV[j // 2, 0, :, 128 * (j % 2) : 128 * (j % 2) + 128]
        dh = dh + nt(g.DQ[:, 128 * j : 128 * j + 128], w)
    g.GH[0:edge, :] = (dh[0:edge] + kvh[0:edge]).astype(BF)
    first = jnp.where(h == 0, 1.0, 0.0)
    g.GH[edge:n, :] = (dh[edge:n] + kvh[edge:n] * first).astype(BF)
    gh = g.GH[...]
    g.ENC[0:features, :] = nn(g.NL[h], gh)
    g.ENC[features:, :] = jnp.zeros_like(g.ENC[features:, :])
    bank_rows = g.bank.shape[0] // 2
    enc_at = bank_rows * 4
    for b in range(4):
        cols = slice(128 * b, 128 * b + 128)
        last.give[64 * b : 64 * b + 64, :] = g.ENC[pl.ds(pl.multiple_of(o * 64, 64), 64), cols].astype(BF)
        last.acc[enc_at + 64 * b : enc_at + 64 * b + 64, :] = g.ENC[
            pl.ds(pl.multiple_of(h * 64, 64), 64), cols
        ].astype(BF)
    last.send_core()
    c_prompt.wait_recv()
    put(
        last.acc,
        0,
        nn(g.SEL[pl.ds(pl.multiple_of(h * bank_rows, bank_rows), bank_rows), :], g.DP[o]).astype(BF),
    )
    last.core_copy.wait_recv()
    rows = slice(enc_at, enc_at + 256)
    last.acc[rows, :] = (last.acc[rows, :].astype(F32) + last.got[...].astype(F32)).astype(BF)
    if last.n > enc_at + 256:
        last.acc[enc_at + 256 :, :] = jnp.zeros_like(last.acc[enc_at + 256 :, :])
    for part in last.parts:
        part.begin()
    tick(14)

    scale = g.COLS[:, 2:3]
    uf = nt(g.encw_[...], gh) * scale
    g.UF[...] = uf
    g.SQUARE[...] = jnp.zeros_like(g.SQUARE)
    g.LATE[0] = to_rows([lane_sum(uf), lane_sum(uf * (g.F[h] - g.COLS[:, 0:1]))])
    eb = row_sum(gh.astype(F32))
    for b in range(4):
        g.LATE[0, 2 + b : 3 + b, :] = eb[:, 128 * b : 128 * b + 128]
    c_late = links.copy(g.LATE.at[0], g.LATE.at[1], ctx.twin)
    l_uf = loads.copy(g.UF, g.uf)
    tick(15)
    c_late.wait_recv()
    g.LSUM[ctx.row] = g.LATE[0] + g.LATE[1]
    wait_late = share_rows(ctx, g.LSUM, count)
    tick(16)
    rest = [p for b in blocks.values() for p in b.parts]
    while not all(p.done() for p in rest):
        for p in rest:
            if not p.done():
                p.advance()
    while vec.k < len(vec_stages):
        vec_end()
    c_last = links.copy(last.full, g.TWIN, ctx.twin)
    stores = [l_output, l_uf]
    at = 0
    for b in (down, up, out):
        stores.append(loads.copy(b.full, g.rffn.at[pl.ds(at, b.n)]))
        at += b.n
    at = 0
    for b in (qkv0, qkv1):
        stores.append(loads.copy(b.full.at[0:1536], g.rqkv.at[pl.ds(at, 1536)]))
        at += 1536
    wait_late()
    late = g.LSUM[0]
    for k in range(1, count):
        late = late + g.LSUM[k]
    g.late[...] = late
    g.stat[...] = g.STAT[...]
    stores.append(loads.copy(last.full.at[0 : enc_at + 256], g.rbank.at[h]))
    c_last.wait_recv()
    stores.append(loads.copy(g.TWIN.at[0 : enc_at + 256], g.rbank.at[o]))
    for c in stores:
        c.wait()
    links.drain()
    assert (links.sent, links.received, loads.used) == sem_counts, (links.sent, links.received, loads.used)


def vec_groups(count):
    bits = [2**i for i in range(count.bit_length() - 1)]
    return [tuple(bits[i : i + 2]) for i in range(0, len(bits), 2)]


def finish_kernel(total_rows, names, *refs):
    g = Ctx()
    for name, ref in zip(names, refs, strict=True):
        setattr(g, name, ref)
    h = lax.axis_index("heads")
    features = g.feats.shape[0]
    copies = []

    def copy(src, dst):
        c = pltpu.make_async_copy(src, dst, g.sems.at[len(copies)])
        c.start()
        copies.append(c)
        return c

    c_output = copy(g.output, g.OUTPUT)
    c_ffn = copy(g.rffn, g.RFFN)
    c_qkv = copy(g.rqkv, g.RQKV)
    c_bank = copy(g.rbank, g.RBANK)
    c_feats = copy(g.feats, g.FEATS)
    c_uf = copy(g.uf, g.UF)

    def block(ref, first, rows):
        return ref[first : first + rows, :].astype(F32)

    c_output.wait()
    outs = [copy(g.OUTPUT, g.o_output)]
    c_ffn.wait()
    for b in range(4):
        cols = slice(128 * b, 128 * b + 128)
        g.DOWN[:, cols] = block(g.RFFN, 512 * b, 512)
    outs.append(copy(g.DOWN, g.o_down))
    for b in range(4):
        cols = slice(128 * b, 128 * b + 128)
        g.UP[:, cols] = block(g.RFFN, 2048 + 512 * b, 512)
    outs.append(copy(g.UP, g.o_up))
    for b in range(4):
        cols = slice(128 * b, 128 * b + 128)
        for j in range(2):
            g.OUT[128 * j : 128 * j + 128, cols] = block(g.RFFN, 4096 + 512 * j + 128 * b, 128)
    outs.append(copy(g.OUT, g.o_out))
    c_qkv.wait()
    for c in range(3):
        for p in range(2):
            g.QKV[c, :, 128 * p : 128 * p + 128] = block(g.RQKV, 1536 * p + 512 * c, 512)
    outs.append(copy(g.QKV, g.o_qkv))
    c_bank.wait()
    for b in range(4):
        cols = slice(128 * b, 128 * b + 128)
        for s in range(2):
            g.BANKV[256 * s : 256 * s + 256, cols] = g.RBANK[s, 256 * b : 256 * b + 256, :].astype(F32)
        g.o_encw[0:64, cols] = g.RBANK[0, 1024 + 64 * b : 1024 + 64 * b + 64, :].astype(F32)
        g.o_encw[64:features, cols] = g.RBANK[1, 1024 + 64 * b : 1024 + 64 * b + features - 64, :].astype(F32)
        g.o_encb[:, cols] = g.late[2 + b : 3 + b, :]
    outs.append(copy(g.BANKV, g.o_bank))
    g.o_outb[...] = g.vec[1:2, :]
    g.o_ag[...] = g.vec[2:3, :]
    g.o_ash[...] = g.vec[3:4, :]
    g.o_downb[...] = g.vec[4:5, :]
    g.o_fg[...] = g.vec[5:6, :]
    g.o_fsh[...] = g.vec[6:7, :]
    g.o_upb[...] = g.vec[pl.ds(7 + h, 1), :]
    mean, inverse = g.stat[0:1, :], g.stat[1:2, :]
    b1, b2 = g.late[0:1, :], g.late[1:2, :]
    var_grad = -0.5 * inverse * inverse * inverse * b2
    g.SQUARE[...] = jnp.zeros_like(g.SQUARE)
    g.SQUARE[0:1, :] = inverse
    g.SQUARE[1:2, :] = (-inverse * b1 - 2.0 * mean * var_grad) / total_rows
    g.SQUARE[2:3, :] = 2.0 * var_grad / total_rows
    columns = g.SQUARE[...].T
    inverse, first, slope = [columns[0:features, i : i + 1] for i in range(3)]
    c_feats.wait()
    c_uf.wait()
    g.o_feats[...] = g.UF[...] * inverse + first + g.FEATS[...] * slope
    for c in outs:
        c.wait()


def per_device(
    feats,
    feature_mask,
    splits,
    prompt_index,
    prompt_bank,
    enc_weight,
    enc_bias,
    qkv_weight,
    out_weight,
    out_bias,
    attn_gain,
    attn_shift,
    up_weight,
    up_bias,
    down_weight,
    down_bias,
    ffn_gain,
    ffn_shift,
    cotangent,
):
    n, features = feats.shape
    count = lax.axis_size("rows")
    total_rows = n * count * lax.axis_size("heads")
    d = prompt_bank.shape[1]
    columns = feats.T
    args = [
        columns, feature_mask, splits, prompt_index, prompt_bank, enc_weight, enc_bias[None], qkv_weight, out_weight,
        out_bias[None], attn_gain[None], attn_shift[None], up_weight, up_bias[None], down_weight, down_bias[None],
        ffn_gain[None], ffn_shift[None], cotangent,
    ]
    vmem = pl.BlockSpec(memory_space=pltpu.VMEM)
    hbm = pl.BlockSpec(memory_space=pl.ANY)
    in_specs = [pl.BlockSpec(memory_space=pltpu.SMEM) if k == "splits" else hbm for k in IN_NAMES]
    bits = [2**i for i in range(count.bit_length() - 1)]
    grain = 16 * count
    block_rows = {"d": 2048, "u": 2048, "o": 1024, "q": 1536, "r": 1536, "l": 1280}
    if count == 16:
        cuts, plan = CUTS, PLAN
    else:
        cuts, plan = {k: [(-(-r // grain) * grain, vec_groups(count))] for k, r in block_rows.items()}, []
    block_rows = {k: sum(r for r, _ in v) for k, v in cuts.items()}
    S = jax.ShapeDtypeStruct
    outs = {
        "output": S((n, d), F32),
        "uf": S((features, n), F32),
        "rffn": S((block_rows["d"] + block_rows["u"] + block_rows["o"], 128), BF),
        "rqkv": S((3072, 128), BF),
        "rbank": S((2, 1280, 128), BF),
        "vec": S((16, d), F32),
        "late": S((8, 128), F32),
        "stat": S((8, 128), F32),
    }
    out_specs = [vmem if k in ("vec", "late", "stat") else hbm for k in OUT_NAMES]
    V = pltpu.VMEM
    scratch = {k + "_": V(args[IN_NAMES.index(k)].shape, args[IN_NAMES.index(k)].dtype) for k in SMALL}
    scratch |= {
        "F": V((2, features, n), F32),
        "WQKV": V((2, 3, d, 256), BF),
        "WO": V((2, 256, d), BF),
        "UB": V((2, 1, 512), F32),
        "WU": V((2, d, 512), BF),
        "WD": V((2, 512, d), BF),
        "BANKV": V(prompt_bank.shape, BF),
        "COT": V((n, d), F32),
        "SQUARE": V((128, 128), F32),
        "COLS": V((features, 128), F32),
        "TILE": V((2, 8, 128), F32),
        "LATE": V((2, 8, 128), F32),
        "MOM": V((count, 8, 128), F32),
        "LSUM": V((count, 8, 128), F32),
        "STAT": V((8, 128), F32),
        "VEC": V((16, d), F32),
        "VECR": V((16, d), F32),
        "VECS": V((len(vec_groups(count)), 4, 16, d), F32),
        "SEL": V((prompt_bank.shape[0], P_SIZE), BF),
        "SRC": V((KEYS, d), BF),
        "BIAS": V((KEYS, 1), F32),
        "WKV": V((4, d, 256), BF),
        "NL": V((2, features, n), BF),
        "HA": V((2, n, d), F32),
        "HB": V((2, n, d), BF),
        "Q": V((4, n, 128), BF),
        "K": V((4, KEYS, 128), BF),
        "V": V((4, KEYS, 128), BF),
        "E": V((4, KEYS, n), BF),
        "INV": V((4, 8, n), F32),
        "INNER": V((4, 8, n), F32),
        "AT": V((4, 128, n), BF),
        "A": V((n, d), BF),
        "XH": V((n, d), F32),
        "RS": V((n, 1), F32),
        "AB": V((n, d), BF),
        "DG": V((2, n, 512), F32),
        "ACT": V((2, n, 512), BF),
        "DU": V((2, n, 512), BF),
        "OUTB": V((n, d), F32),
        "DJ": V((n, d), F32),
        "GM": V((n, d), BF),
        "GB": V((n, d), BF),
        "DOT": V((4, 128, n), BF),
        "DOT2": V((4, 128, n), BF),
        "DKV": V((4, KEYS, 256), BF),
        "DKVR": V((4, n, 256), BF),
        "DKVO": V((4, n, 256), BF),
        "DQT": V((4, 128, n), BF),
        "DQ": V((n, d), BF),
        "HQT": V((d, n), BF),
        "SRCT": V((d, n), BF),
        "DP": V((2, P_SIZE, d), BF),
        "GH": V((n, d), BF),
        "UF": V((features, n), F32),
        "ENC": V((128, d), F32),
        "TWIN": V((block_rows["l"], 128), BF),
    }
    for k, r in block_rows.items():
        small = 256 if k == "l" else r
        scratch["CG" + k] = V((small, 128), BF)
        scratch["CR" + k] = V((small, 128), BF)
        scratch["CA" + k] = V((r, 128), BF)
        scratch["CV" + k] = V((r, 128), BF)
        scratch["CF" + k] = V((r, 128), BF)
    parts = [stages for v in cuts.values() for _, stages in v]
    once = 23 + len(vec_groups(count))
    sem_counts = (once + len(parts), once + sum(2 * len(s) for s in parts), 17 + len(SMALL))
    for k, v in zip(("ssem", "rsem", "lsem"), sem_counts, strict=True):
        scratch[k] = pltpu.SemaphoreType.DMA((v,))
    names = IN_NAMES + OUT_NAMES + list(scratch)
    results = pl.pallas_call(
        functools.partial(layer_kernel, count, total_rows, cuts, plan, sem_counts, names),
        out_shape=[outs[k] for k in OUT_NAMES],
        in_specs=in_specs,
        out_specs=out_specs,
        scratch_shapes=list(scratch.values()),
        compiler_params=pltpu.CompilerParams(
            collective_id=0, has_side_effects=True, vmem_limit_bytes=VMEM_LIMIT
        ),
        name="layer",
    )(*args)
    finals = {
        "o_output": S((n, d), F32),
        "o_feats": S((features, n), F32),
        "o_bank": S(prompt_bank.shape, F32),
        "o_encw": S(enc_weight.shape, F32),
        "o_encb": S((1, d), F32),
        "o_qkv": S(qkv_weight.shape, F32),
        "o_out": S(out_weight.shape, F32),
        "o_outb": S((1, d), F32),
        "o_ag": S((1, d), F32),
        "o_ash": S((1, d), F32),
        "o_up": S(up_weight.shape, F32),
        "o_upb": S((1, up_bias.shape[0]), F32),
        "o_down": S(down_weight.shape, F32),
        "o_downb": S((1, d), F32),
        "o_fg": S((1, d), F32),
        "o_fsh": S((1, d), F32),
    }
    moved = {"o_output", "o_bank", "o_qkv", "o_out", "o_up", "o_down"}
    work = {
        "OUTPUT": V((n, d), F32),
        "RFFN": V(outs["rffn"].shape, BF),
        "RQKV": V((3072, 128), BF),
        "RBANK": V((2, 1280, 128), BF),
        "FEATS": V((features, n), F32),
        "UF": V((features, n), F32),
        "DOWN": V(down_weight.shape, F32),
        "UP": V(up_weight.shape, F32),
        "OUT": V(out_weight.shape, F32),
        "QKV": V(qkv_weight.shape, F32),
        "BANKV": V(prompt_bank.shape, F32),
        "SQUARE": V((128, 128), F32),
        "sems": pltpu.SemaphoreType.DMA((12,)),
    }
    final = pl.pallas_call(
        functools.partial(finish_kernel, total_rows, ["feats"] + OUT_NAMES + list(finals) + list(work)),
        out_shape=list(finals.values()),
        in_specs=[vmem if k in ("vec", "late", "stat") else hbm for k in ["feats"] + OUT_NAMES],
        out_specs=[hbm if k in moved else vmem for k in finals],
        scratch_shapes=list(work.values()),
        compiler_params=pltpu.CompilerParams(vmem_limit_bytes=VMEM_LIMIT),
        name="finish",
    )(columns, *results)
    vectors = ("o_encb", "o_outb", "o_ag", "o_ash", "o_upb", "o_downb", "o_fg", "o_fsh")
    return tuple(
        v[0] if k in vectors else v.T if k == "o_feats" else v for k, v in zip(finals, final, strict=True)
    )


def solution(mesh):
    whole = P(("rows", "heads"), None)
    placed = (
        whole, P("rows", None), P("rows"), P("rows", None), P(), P(), P(), P(None, None, "heads"), P("heads", None),
        P(), P(), P(), P(None, "heads"), P("heads"), P("heads", None), P(), P(), P(), whole,
    )
    return jax.shard_map(
        per_device,
        mesh=mesh,
        in_specs=placed,
        out_specs=(
            whole, whole, P(), P(), P(), P(None, None, "heads"), P("heads", None), P(), P(), P(), P(None, "heads"),
            P("heads"), P("heads", None), P(), P(), P(),
        ),
        check_vma=False,
    )
```

time: 126 us -> 92.4 us (0.73)
  Pallas kernels: 120 us -> 90.4 us
  local copies, waits for them, and re-layouts: 3.55 us -> 0 us
    pallas_call x1, Pallas kernels: 115 us -> 84.6 us  [per_device(): pl.pallas_call(functools.partial(layer_kernel, count, total_rows, cuts, p...]
    unnamed x2 -> x0, local copies, waits for them, and re-layouts: 3.55 us -> none
where the time goes in v2:
time: 92.4 us; the launch traced here: 91.9 us
  Pallas kernels  90.4 us (98%)
  between operations  1.47 us (2%)
    pallas_call x1, Pallas kernels, per_device(): pl.pallas_call(functools.partial(layer_kernel, count, total_rows, cuts, p...  84.6 us
    pallas_call x1, Pallas kernels, per_device(): pl.pallas_call(functools.partial(finish_kernel, total_rows, ['feats'] + O...  5.78 us

profile of v2, /device:TPU:0, one launch (start us, length us, event | category | flops | bytes accessed | tf_op | source)
XLA Modules:
  0.0 91.9 jit_solution(620827452486452930)
XLA Ops:
  1.3 84.6 %layer.1 = (f32[512,512]{1,0:T(8,128)}, f32[100,512]{1,0:T(8,128)}, bf16[5120,128]{1,0:T(8,128)(2,1)}, bf16[3072,128]{1,0:T(8,128)(2,1)}, bf16[2,1280,128]{2,1,0...) custom-call(f32[100,512]{1,0:T(8,128)} %bitcast.18, s32[1,100]{1,0:T(1,128)} %refs_1_.1, ...), custom_call_target="tpu_custom_call" | custom-call | tf_op jit(solution)/shard_map/layer/pallas_call | solution.py:882
  85.9 5.8 %finish.1 = (f32[512,512]{1,0:T(8,128)}, f32[100,512]{1,0:T(8,128)}, f32[512,512]{1,0:T(8,128)}, f32[100,512]{1,0:T(8,128)}, f32[1,512]{1,0:T(1,128)}, /*index=5...) custom-call(f32[100,512]{1,0:T(8,128)} %bitcast.19, ...), custom_call_target="tpu_custom_call" | custom-call | tf_op jit(solution)/shard_map/finish/pallas_call | solution.py:927

commit v3 on v2

--- a/solution.py
+++ b/solution.py
@@ -14,12 +14,14 @@
 DH = 128
 P_SIZE = 128
 CONTEXT_MAX = 896
+CONTEXT_MIN = 640
 KEYS = CONTEXT_MAX + P_SIZE
 EPS = 1e-05
 HALF_ROOT = math.sqrt(0.5)
 PDF_SCALE = 1.0 / math.sqrt(2.0 * math.pi)
 LOG2E = math.log2(math.e)
-VMEM_LIMIT = 60 * 2**20
+Q_SCALE = DH**-0.5 * LOG2E
+VMEM_LIMIT = 52 * 2**20
 
 
 def _dot(a, b, ca, cb):
@@ -226,31 +228,35 @@
     "output", "uf", "rffn", "rqkv", "rbank", "vec", "late", "stat",
 ]
 CUTS = {
-    "d": [(1024, [(1, 2), (4, 8)]), (1024, [(1, 2), (4, 8)])],
-    "u": [(1024, [(2,), (1,), (4, 8)]), (1024, [(1,), (2,), (4, 8)])],
-    "o": [(1024, [(1,), (2,), (4, 8)])],
-    "q": [(768, [(1, 2), (4,), (8,)]), (768, [(4,), (1, 2), (8,)])],
-    "r": [(512, [(2,), (1, 4), (8,)]), (512, [(2, 4), (1,), (8,)]), (512, [(1,), (2, 4), (8,)])],
-    "l": [(512, [(1,), (2,), (4, 8)]), (512, [(4, 8), (1, 2)]), (256, [(1, 2), (4,), (8,)])],
+    "d": [(1536, [(1, 2), (4, 8)]), (512, [(2,), (1,), (4,), (8,)])],
+    "u": [(1024, [(4,), (1, 2), (8,)]), (1024, [(1, 2), (4, 8)])],
+    "o": [(1024, [(2,), (8,), (1, 4)])],
+    "q": [(768, [(1,), (2,), (4,), (8,)]), (768, [(4,), (1,), (2,), (8,)])],
+    "r": [(512, [(1,), (2, 4), (8,)]), (768, [(1,), (2,), (4, 8)]), (256, [(1,), (2, 4), (8,)])],
+    "l": [(512, [(2, 4), (1,), (8,)]), (512, [(4,), (1, 2), (8,)]), (256, [(1, 2), (4, 8)])],
 }
 PLAN = [
     [],
     [],
     [],
+    [],
+    [],
+    [],
+    [],
+    [],
+    [],
+    [],
+    [],
     ["d0"],
     [],
-    [],
-    ["d1", "d0"],
-    ["u0", "u1"],
-    ["d1", "o0", "d0"],
-    ["u1", "u0"],
-    [],
-    ["d1", "o0"],
-    ["q1", "u1", "d0", "u0"],
-    ["o0", "q0"],
-    ["u1", "d1", "q1", "r2", "u0", "r0"],
-    ["o0", "q0", "r1", "l0"],
-    ["l2", "l1", "u1", "q1", "u0", "r2", "r0", "r1", "q0", "o0", "l2", "l0", "l1", "q1", "r2", "r0", "r1", "q0", "l2", "u1", "l0", "u0", "r2", "r0", "r1", "q0", "l2", "o0", "l1", "l0", "r2", "q1", "l2", "r0", "r1", "l0", "q0", "l1", "r2", "r0", "l2", "q1", "l0", "r1"],
+    ["d1"],
+    ["u0"],
+    [],
+    ["u1", "d0"],
+    ["q0", "q1", "d1"],
+    ["o0"],
+    [],
+    ["u1", "u0", "q0", "q1", "d1", "d0", "r0", "l0", "l1", "q1", "r1", "r2", "o0", "l2", "u1", "u0", "q0", "d1", "q1", "r0", "l2", "d0", "u0", "l0", "q0", "d1", "r1", "l1", "q1", "r2", "r0", "o0", "l2", "l0", "d1", "q0", "u1", "r1", "l1", "r2", "r0", "l0", "u0", "q1", "q0", "o0", "l2", "r1", "d1", "l1", "l0", "r2", "r0", "q1", "q0", "r1", "u0", "d1", "r0", "o0", "l1", "l0", "q0", "r2", "q1", "r1", "o0", "r2", "l1"],
 ]
 
 
@@ -313,9 +319,8 @@
     g.SEL[...] = jnp.where(selector, 1.0, 0.0).astype(BF)
     l_bank.wait()
     g.SRC[CONTEXT_MAX:KEYS, :] = tn(g.SEL[...], g.BANKV[...]).astype(BF)
-    visible = lax.broadcasted_iota(jnp.int32, (KEYS, 1), 0)
-    visible = (visible < g.splits[0]) | (visible >= CONTEXT_MAX)
-    g.BIAS[...] = jnp.where(visible, 0.0, -1e30)
+    maybe = lax.broadcasted_iota(jnp.int32, (CONTEXT_MAX - CONTEXT_MIN, 1), 0) + CONTEXT_MIN
+    g.BIAS[...] = jnp.where(maybe < g.splits[0], 0.0, -1e30)
     g.VEC[...] = jnp.zeros_like(g.VEC)
     g.LATE[0] = jnp.zeros_like(g.LATE[0])
     live = g.mask_[...].astype(F32)
@@ -353,31 +358,30 @@
     g.SRC[n:CONTEXT_MAX, :] = g.HB[1, 0 : CONTEXT_MAX - n, :]
 
     for s in range(2):
-        q = nn(g.HB[h], g.WQKV[s, 0]).astype(BF)
+        q = (nn(g.HB[h], g.WQKV[s, 0]) * Q_SCALE).astype(BF)
         for j in range(2):
             g.Q[2 * s + j] = q[:, 128 * j : 128 * j + 128]
 
-    def project(j, _):
+    for j in range(4):
         kv = nn(g.SRC[...], g.WKV[j]).astype(BF)
         g.K[j] = kv[:, 0:128]
         g.V[j] = kv[:, 128:256]
-        return 0
-
-    lax.fori_loop(0, 4, project, 0)
-
-    def attend(j, _):
-        for t in range(n // 256):
-            cols = slice(256 * t, 256 * t + 256)
-            scores = nt(g.K[j], g.Q[j, cols, :]) * (DH**-0.5 * LOG2E) + g.BIAS[...]
+
+    for j in range(5):
+        if j < 4:
+            scores = nt(g.K[j], g.Q[j])
+            g.S[j % 2, 0:CONTEXT_MIN, :] = scores[0:CONTEXT_MIN]
+            g.S[j % 2, CONTEXT_MIN:CONTEXT_MAX, :] = scores[CONTEXT_MIN:CONTEXT_MAX] + g.BIAS[...]
+            g.S[j % 2, CONTEXT_MAX:KEYS, :] = scores[CONTEXT_MAX:KEYS]
+        if j > 0:
+            p = j - 1
+            scores = g.S[p % 2]
             e = jnp.exp2(scores - jnp.max(scores, axis=0, keepdims=True))
             inv = 1.0 / row_sum(e)
-            g.INV[j, 0:1, cols] = inv
+            g.INV[p, 0:1, :] = inv
             e = e.astype(BF)
-            g.E[j, :, cols] = e
-            g.AT[j, :, cols] = (tn(g.V[j], e) * inv).astype(BF)
-        return 0
-
-    lax.fori_loop(0, 4, attend, 0)
+            g.E[p] = e
+            g.AT[p] = (tn(g.V[p], e) * inv).astype(BF)
 
     c_own["out"].wait_recv()
     c_own["up"].wait_recv()
@@ -387,54 +391,54 @@
         g.A[:, 128 * j : 128 * j + 128] = g.AT[j].T
     l_cot.wait()
 
-    tile = 256
-
-    def forward(t, _):
-        rows = pl.ds(pl.multiple_of(t * tile, tile), tile)
-        branch = nn(g.A[rows, 0:256], g.WO[0]) + nn(g.A[rows, 256:512], g.WO[1]) + g.outb_[...]
-        joined = g.HA[h, rows, :] + branch
-        center = joined - lane_mean(joined)
-        rstd = lax.rsqrt(lane_mean(center * center) + EPS)
-        xhat = center * rstd
-        after = xhat * g.ag_[...] + g.ash_[...]
-        g.XH[rows, :] = xhat
-        g.RS[rows, :] = rstd
-        low = after.astype(BF)
-        g.AB[rows, :] = low
-        mixed = g.downb_[...]
-        for s in range(2):
-            u = nn(low, g.WU[s]) + g.UB[s]
-            phi = 0.5 * (1.0 + lax.erf(u * HALF_ROOT))
-            g.DG[s, rows, :] = phi + u * (jnp.exp2(u * u * (-0.5 * LOG2E)) * PDF_SCALE)
-            act = (u * phi).astype(BF)
-            g.ACT[s, rows, :] = act
-            mixed = mixed + nn(act, g.WD[s])
-        joined = after + mixed
-        center = joined - lane_mean(joined)
-        rstd = lax.rsqrt(lane_mean(center * center) + EPS)
-        xhat = center * rstd
-        g.OUTB[rows, :] = xhat * g.fg_[...] + g.fsh_[...]
-        ct = g.COT[rows, :]
-        d = ct * g.fg_[...]
-        d = rstd * (d - lane_mean(d) - xhat * lane_mean(d * xhat))
-        g.DJ[rows, :] = d
-        gm = d.astype(BF)
-        g.GM[rows, :] = gm
-        g.VEC[4:5, :] += row_sum(gm.astype(F32))
-        g.VEC[5:6, :] += row_sum(ct * xhat)
-        g.VEC[6:7, :] += row_sum(ct)
-        return 0
-
-    lax.fori_loop(0, n // tile, forward, 0)
-    l_output = loads.copy(g.OUTB, g.output)
+    branch = nn(g.A[:, 0:256], g.WO[0]) + nn(g.A[:, 256:512], g.WO[1]) + g.outb_[...]
+    joined = g.HA[h] + branch
+    center = joined - lane_mean(joined)
+    rstd = lax.rsqrt(lane_mean(center * center) + EPS)
+    xhat = center * rstd
+    after = xhat * g.ag_[...] + g.ash_[...]
+    g.XH[...] = xhat
+    g.RS[...] = rstd
+    low = after.astype(BF)
+    g.AB[...] = low
+    mixed = g.downb_[...]
+    for s in range(2):
+        u = nn(low, g.WU[s]) + g.UB[s]
+        phi = 0.5 * (1.0 + lax.erf(u * HALF_ROOT))
+        g.DG[s] = phi + u * (jnp.exp2(u * u * (-0.5 * LOG2E)) * PDF_SCALE)
+        act = (u * phi).astype(BF)
+        g.ACT[s] = act
+        mixed = mixed + nn(act, g.WD[s])
+    joined = after + mixed
+    center = joined - lane_mean(joined)
+    rstd = lax.rsqrt(lane_mean(center * center) + EPS)
+    xhat = center * rstd
+    g.output[...] = xhat * g.fg_[...] + g.fsh_[...]
+    ct = g.COT[...]
+    d = ct * g.fg_[...]
+    d = rstd * (d - lane_mean(d) - xhat * lane_mean(d * xhat))
+    g.DJ[...] = d
+    gm = d.astype(BF)
+    g.GM[...] = gm
+    g.VEC[4:5, :] = row_sum(gm.astype(F32))
+    g.VEC[5:6, :] = row_sum(ct * xhat)
+    g.VEC[6:7, :] = row_sum(ct)
 
     def put(ref, first, value):
         r = value.shape[0]
         for b in range(value.shape[1] // 128):
             ref[first + r * b : first + r * b + r, :] = value[:, 128 * b : 128 * b + 128]
 
+    rows_of = {k: sum(r for r, _ in v) for k, v in cuts.items()}
+    fulls, at = {"l": g.rbank.at[h]}, 0
+    for k in ("d", "u", "o"):
+        fulls[k] = g.rffn.at[pl.ds(at, rows_of[k])]
+        at += rows_of[k]
+    for i, k in enumerate(("q", "r")):
+        fulls[k] = g.rqkv.at[i]
     blocks = {
-        k: Block(ctx, [getattr(g, p + k) for p in ("CG", "CR", "CA", "CV", "CF")], v) for k, v in cuts.items()
+        k: Block(ctx, [getattr(g, p + k) for p in ("CG", "CR", "CA", "CV")] + [fulls[k]], v)
+        for k, v in cuts.items()
     }
     down, up, out, qkv0, qkv1, last = blocks.values()
 
@@ -445,7 +449,8 @@
     put(down.give, 0, tn(g.ACT[o], g.GM[...]).astype(BF))
     down.send_core()
     put(down.acc, 0, tn(g.ACT[h], g.GM[...]).astype(BF))
-    down.merge_core()
+
+    tile = n // 2
 
     def backward(t):
         rows = slice(t * tile, t * tile + tile)
@@ -466,9 +471,10 @@
         g.GB[rows, :] = gb
         g.VEC[1:2, :] += row_sum(gb.astype(F32))
 
-    for t in range(n // tile):
-        backward(t)
-    tick(2)
+    backward(0)
+    down.merge_core()
+    backward(1)
+    tick(4)
     put(up.give, 0, tn(g.AB[...], g.DU[o]).astype(BF))
     up.send_core()
     for j in range(2):
@@ -478,10 +484,7 @@
     put(up.acc, 0, tn(g.AB[...], g.DU[h]).astype(BF))
     for j in range(2):
         put(out.acc, 128 * j * 4, nn(g.AT[2 * h + j], g.GB[...]).astype(BF))
-    tick(3)
-    up.merge_core()
-    out.merge_core()
-    tick(4)
+    tick(5)
 
     for j in range(4):
         d = nt(g.WO[j // 2, 128 * (j % 2) : 128 * (j % 2) + 128, :], g.GB[...]).astype(BF)
@@ -489,7 +492,10 @@
         df = d.astype(F32)
         g.INNER[j, 0:1, :] = row_sum(df * g.AT[j].astype(F32))
         g.DOT2[j] = (df * g.INV[j, 0:1, :]).astype(BF)
-        g.INV[j, 1:2, :] = g.INV[j, 0:1, :] * (DH**-0.5)
+    tick(6)
+    up.merge_core()
+    out.merge_core()
+    tick(7)
 
     vec_stages = vec_groups(count)
     vec = Ctx()
@@ -523,19 +529,18 @@
 
     def attend_back(j):
         q, dot, dot2 = g.Q[j], g.DOT[j], g.DOT2[j]
-        inner, factor = g.INNER[j, 0:1, :], g.INV[j, 1:2, :]
-
-        def block(t, dq):
-            rows = pl.ds(pl.multiple_of(t * 256, 256), 256)
+        inner, factor = g.INNER[j, 0:1, :], g.INV[j, 0:1, :]
+        dq = None
+        for t in range(KEYS // 256):
+            rows = slice(256 * t, 256 * t + 256)
             e = g.E[j, rows, :]
             upstream = nn(g.V[j, rows, :], dot)
             ds = (e.astype(F32) * ((upstream - inner) * factor)).astype(BF)
-            g.DKV[j, rows, 0:128] = nn(ds, q).astype(BF)
+            g.DKV[j, rows, 0:128] = (nn(ds, q) * (DH**-0.5 / Q_SCALE)).astype(BF)
             g.DKV[j, rows, 128:256] = nt(e, dot2).astype(BF)
-            return dq + tn(g.K[j, rows, :], ds)
-
-        dq = lax.fori_loop(0, KEYS // 256, block, jnp.zeros((128, n), F32))
-        g.DQT[j] = dq.astype(BF)
+            part = tn(g.K[j, rows, :], ds)
+            dq = part if dq is None else dq + part
+        g.DQT[j] = (dq * DH**-0.5).astype(BF)
         other = pl.ds(pl.multiple_of(o * n, n), n)
         kv_copies[j] = links.copy(g.DKV.at[j, other], g.DKVR.at[j], ctx.twin)
 
@@ -544,57 +549,54 @@
         mine = pl.ds(pl.multiple_of(h * n, n), n)
         g.DKVO[j] = (g.DKV[j, mine, :].astype(F32) + g.DKVR[j].astype(F32)).astype(BF)
 
-    def head_grads(j, ref):
-        put(ref, 0, nt(g.HQT[...], g.DQT[j]).astype(BF))
-        put(ref, n, nn(g.SRCT[...], g.DKVO[j]).astype(BF))
-
-    def pair_grads(p, block):
-        head_grads(2 * o + p, block.give)
+    def q_grads(p, block):
+        for j, ref in ((2 * o + p, block.give), (2 * h + p, block.acc)):
+            put(ref, 0, nt(g.HQT[...], g.DQT[j]).astype(BF))
+
+    def kv_grads(p, block):
+        put(block.give, n, nn(g.SRCT[...], g.DKVO[2 * o + p]).astype(BF))
         block.send_core()
-        head_grads(2 * h + p, block.acc)
+        put(block.acc, n, nn(g.SRCT[...], g.DKVO[2 * h + p]).astype(BF))
 
     g.HQT[...] = g.HB[h].T
     g.SRCT[...] = g.SRC[pl.ds(pl.multiple_of(h * n, n), n), :].T
-    tick(5)
     attend_back(0)
-    tick(6)
+    tick(8)
     attend_back(2)
-    tick(7)
+    tick(9)
+    q_grads(0, qkv0)
+    attend_back(1)
+    tick(10)
     merge_kv(0)
     merge_kv(2)
-    pair_grads(0, qkv0)
-    tick(8)
+    kv_grads(0, qkv0)
+    tick(11)
+    attend_back(3)
+    tick(12)
     qkv0.merge_core()
     c_vec.wait_recv()
     vec_start(g.VEC[...] + g.VECR[...])
-    tick(9)
-    attend_back(1)
-    tick(10)
-    attend_back(3)
-    tick(11)
-    vec_end()
+    tick(13)
+    q_grads(1, qkv1)
+    for j in range(4):
+        g.DQ[:, 128 * j : 128 * j + 128] = g.DQT[j].T
+    dh = g.DJ[...] + nt(g.DQ[:, 0:256], g.WQKV[0, 0]) + nt(g.DQ[:, 256:512], g.WQKV[1, 0])
+    tick(14)
+
     merge_kv(1)
     merge_kv(3)
-    pair_grads(1, qkv1)
-    tick(12)
-    qkv1.merge_core()
-    tick(13)
-
     kvh = nt(g.DKVO[0], g.WKV[0])
     for j in range(1, 4):
         kvh = kvh + nt(g.DKVO[j], g.WKV[j])
     edge = CONTEXT_MAX - n
     g.DP[0] = kvh[edge:n, :].astype(BF)
     c_prompt = links.copy(g.DP.at[0], g.DP.at[1], ctx.twin)
-    for j in range(4):
-        g.DQ[:, 128 * j : 128 * j + 128] = g.DQT[j].T
-    dh = g.DJ[...]
-    for j in range(4):
-        w = g.WQKV[j // 2, 0, :, 128 * (j % 2) : 128 * (j % 2) + 128]
-        dh = dh + nt(g.DQ[:, 128 * j : 128 * j + 128], w)
     g.GH[0:edge, :] = (dh[0:edge] + kvh[0:edge]).astype(BF)
     first = jnp.where(h == 0, 1.0, 0.0)
     g.GH[edge:n, :] = (dh[edge:n] + kvh[edge:n] * first).astype(BF)
+    tick(15)
+    kv_grads(1, qkv1)
+    tick(16)
     gh = g.GH[...]
     g.ENC[0:features, :] = nn(g.NL[h], gh)
     g.ENC[features:, :] = jnp.zeros_like(g.ENC[features:, :])
@@ -613,6 +615,8 @@
         0,
         nn(g.SEL[pl.ds(pl.multiple_of(h * bank_rows, bank_rows), bank_rows), :], g.DP[o]).astype(BF),
     )
+    tick(17)
+    qkv1.merge_core()
     last.core_copy.wait_recv()
     rows = slice(enc_at, enc_at + 256)
     last.acc[rows, :] = (last.acc[rows, :].astype(F32) + last.got[...].astype(F32)).astype(BF)
@@ -620,23 +624,23 @@
         last.acc[enc_at + 256 :, :] = jnp.zeros_like(last.acc[enc_at + 256 :, :])
     for part in last.parts:
         part.begin()
-    tick(14)
+    tick(18)
+    vec_end()
 
     scale = g.COLS[:, 2:3]
     uf = nt(g.encw_[...], gh) * scale
-    g.UF[...] = uf
+    g.uf[...] = uf
     g.SQUARE[...] = jnp.zeros_like(g.SQUARE)
     g.LATE[0] = to_rows([lane_sum(uf), lane_sum(uf * (g.F[h] - g.COLS[:, 0:1]))])
     eb = row_sum(gh.astype(F32))
     for b in range(4):
         g.LATE[0, 2 + b : 3 + b, :] = eb[:, 128 * b : 128 * b + 128]
     c_late = links.copy(g.LATE.at[0], g.LATE.at[1], ctx.twin)
-    l_uf = loads.copy(g.UF, g.uf)
-    tick(15)
+    tick(19)
     c_late.wait_recv()
     g.LSUM[ctx.row] = g.LATE[0] + g.LATE[1]
     wait_late = share_rows(ctx, g.LSUM, count)
-    tick(16)
+    tick(20)
     rest = [p for b in blocks.values() for p in b.parts]
     while not all(p.done() for p in rest):
         for p in rest:
@@ -644,27 +648,14 @@
                 p.advance()
     while vec.k < len(vec_stages):
         vec_end()
-    c_last = links.copy(last.full, g.TWIN, ctx.twin)
-    stores = [l_output, l_uf]
-    at = 0
-    for b in (down, up, out):
-        stores.append(loads.copy(b.full, g.rffn.at[pl.ds(at, b.n)]))
-        at += b.n
-    at = 0
-    for b in (qkv0, qkv1):
-        stores.append(loads.copy(b.full.at[0:1536], g.rqkv.at[pl.ds(at, 1536)]))
-        at += 1536
+    c_last = links.copy(g.rbank.at[h], g.rbank.at[h], ctx.twin)
     wait_late()
     late = g.LSUM[0]
     for k in range(1, count):
         late = late + g.LSUM[k]
     g.late[...] = late
     g.stat[...] = g.STAT[...]
-    stores.append(loads.copy(last.full.at[0 : enc_at + 256], g.rbank.at[h]))
     c_last.wait_recv()
-    stores.append(loads.copy(g.TWIN.at[0 : enc_at + 256], g.rbank.at[o]))
-    for c in stores:
-        c.wait()
     links.drain()
     assert (links.sent, links.received, loads.used) == sem_counts, (links.sent, links.received, loads.used)
 
@@ -688,44 +679,36 @@
         copies.append(c)
         return c
 
-    c_output = copy(g.output, g.OUTPUT)
-    c_ffn = copy(g.rffn, g.RFFN)
-    c_qkv = copy(g.rqkv, g.RQKV)
-    c_bank = copy(g.rbank, g.RBANK)
+    outs = [copy(g.output, g.o_output)]
     c_feats = copy(g.feats, g.FEATS)
-    c_uf = copy(g.uf, g.UF)
+    up_at = g.rffn.shape[0] // 5 * 2
 
     def block(ref, first, rows):
         return ref[first : first + rows, :].astype(F32)
 
-    c_output.wait()
-    outs = [copy(g.OUTPUT, g.o_output)]
-    c_ffn.wait()
     for b in range(4):
         cols = slice(128 * b, 128 * b + 128)
-        g.DOWN[:, cols] = block(g.RFFN, 512 * b, 512)
+        g.DOWN[:, cols] = block(g.rffn, 512 * b, 512)
     outs.append(copy(g.DOWN, g.o_down))
     for b in range(4):
         cols = slice(128 * b, 128 * b + 128)
-        g.UP[:, cols] = block(g.RFFN, 2048 + 512 * b, 512)
+        g.UP[:, cols] = block(g.rffn, up_at + 512 * b, 512)
     outs.append(copy(g.UP, g.o_up))
     for b in range(4):
         cols = slice(128 * b, 128 * b + 128)
         for j in range(2):
-            g.OUT[128 * j : 128 * j + 128, cols] = block(g.RFFN, 4096 + 512 * j + 128 * b, 128)
+            g.OUT[128 * j : 128 * j + 128, cols] = block(g.rffn, 2 * up_at + 512 * j + 128 * b, 128)
     outs.append(copy(g.OUT, g.o_out))
-    c_qkv.wait()
     for c in range(3):
         for p in range(2):
-            g.QKV[c, :, 128 * p : 128 * p + 128] = block(g.RQKV, 1536 * p + 512 * c, 512)
+            g.QKV[c, :, 128 * p : 128 * p + 128] = g.rqkv[p, 512 * c : 512 * c + 512, :].astype(F32)
     outs.append(copy(g.QKV, g.o_qkv))
-    c_bank.wait()
     for b in range(4):
         cols = slice(128 * b, 128 * b + 128)
         for s in range(2):
-            g.BANKV[256 * s : 256 * s + 256, cols] = g.RBANK[s, 256 * b : 256 * b + 256, :].astype(F32)
-        g.o_encw[0:64, cols] = g.RBANK[0, 1024 + 64 * b : 1024 + 64 * b + 64, :].astype(F32)
-        g.o_encw[64:features, cols] = g.RBANK[1, 1024 + 64 * b : 1024 + 64 * b + features - 64, :].astype(F32)
+            g.BANKV[256 * s : 256 * s + 256, cols] = g.rbank[s, 256 * b : 256 * b + 256, :].astype(F32)
+        g.o_encw[0:64, cols] = g.rbank[0, 1024 + 64 * b : 1024 + 64 * b + 64, :].astype(F32)
+        g.o_encw[64:features, cols] = g.rbank[1, 1024 + 64 * b : 1024 + 64 * b + features - 64, :].astype(F32)
         g.o_encb[:, cols] = g.late[2 + b : 3 + b, :]
     outs.append(copy(g.BANKV, g.o_bank))
     g.o_outb[...] = g.vec[1:2, :]
@@ -745,8 +728,7 @@
     columns = g.SQUARE[...].T
     inverse, first, slope = [columns[0:features, i : i + 1] for i in range(3)]
     c_feats.wait()
-    c_uf.wait()
-    g.o_feats[...] = g.UF[...] * inverse + first + g.FEATS[...] * slope
+    g.o_feats[...] = g.uf[...] * inverse + first + g.FEATS[...] * slope
     for c in outs:
         c.wait()
 
@@ -798,13 +780,12 @@
         "output": S((n, d), F32),
         "uf": S((features, n), F32),
         "rffn": S((block_rows["d"] + block_rows["u"] + block_rows["o"], 128), BF),
-        "rqkv": S((3072, 128), BF),
-        "rbank": S((2, 1280, 128), BF),
+        "rqkv": S((2, block_rows["q"], 128), BF),
+        "rbank": S((2, block_rows["l"], 128), BF),
         "vec": S((16, d), F32),
         "late": S((8, 128), F32),
         "stat": S((8, 128), F32),
     }
-    out_specs = [vmem if k in ("vec", "late", "stat") else hbm for k in OUT_NAMES]
     V = pltpu.VMEM
     scratch = {k + "_": V(args[IN_NAMES.index(k)].shape, args[IN_NAMES.index(k)].dtype) for k in SMALL}
     scratch |= {
@@ -828,7 +809,8 @@
         "VECS": V((len(vec_groups(count)), 4, 16, d), F32),
         "SEL": V((prompt_bank.shape[0], P_SIZE), BF),
         "SRC": V((KEYS, d), BF),
-        "BIAS": V((KEYS, 1), F32),
+        "BIAS": V((CONTEXT_MAX - CONTEXT_MIN, 1), F32),
+        "S": V((2, KEYS, n), F32),
         "WKV": V((4, d, 256), BF),
         "NL": V((2, features, n), BF),
         "HA": V((2, n, d), F32),
@@ -847,7 +829,6 @@
         "DG": V((2, n, 512), F32),
         "ACT": V((2, n, 512), BF),
         "DU": V((2, n, 512), BF),
-        "OUTB": V((n, d), F32),
         "DJ": V((n, d), F32),
         "GM": V((n, d), BF),
         "GB": V((n, d), BF),
@@ -862,9 +843,7 @@
         "SRCT": V((d, n), BF),
         "DP": V((2, P_SIZE, d), BF),
         "GH": V((n, d), BF),
-        "UF": V((features, n), F32),
         "ENC": V((128, d), F32),
-        "TWIN": V((block_rows["l"], 128), BF),
     }
     for k, r in block_rows.items():
         small = 256 if k == "l" else r
@@ -872,18 +851,17 @@
         scratch["CR" + k] = V((small, 128), BF)
         scratch["CA" + k] = V((r, 128), BF)
         scratch["CV" + k] = V((r, 128), BF)
-        scratch["CF" + k] = V((r, 128), BF)
     parts = [stages for v in cuts.values() for _, stages in v]
     once = 23 + len(vec_groups(count))
-    sem_counts = (once + len(parts), once + sum(2 * len(s) for s in parts), 17 + len(SMALL))
+    sem_counts = (once + len(parts), once + sum(2 * len(s) for s in parts), 8 + len(SMALL))
     for k, v in zip(("ssem", "rsem", "lsem"), sem_counts, strict=True):
         scratch[k] = pltpu.SemaphoreType.DMA((v,))
     names = IN_NAMES + OUT_NAMES + list(scratch)
     results = pl.pallas_call(
         functools.partial(layer_kernel, count, total_rows, cuts, plan, sem_counts, names),
-        out_shape=[outs[k] for k in OUT_NAMES],
+        out_shape=[pltpu.VMEM(outs[k].shape, outs[k].dtype) for k in OUT_NAMES],
         in_specs=in_specs,
-        out_specs=out_specs,
+        out_specs=[vmem] * len(OUT_NAMES),
         scratch_shapes=list(scratch.values()),
         compiler_params=pltpu.CompilerParams(
             collective_id=0, has_side_effects=True, vmem_limit_bytes=VMEM_LIMIT
@@ -910,29 +888,24 @@
     }
     moved = {"o_output", "o_bank", "o_qkv", "o_out", "o_up", "o_down"}
     work = {
-        "OUTPUT": V((n, d), F32),
-        "RFFN": V(outs["rffn"].shape, BF),
-        "RQKV": V((3072, 128), BF),
-        "RBANK": V((2, 1280, 128), BF),
         "FEATS": V((features, n), F32),
-        "UF": V((features, n), F32),
         "DOWN": V(down_weight.shape, F32),
         "UP": V(up_weight.shape, F32),
         "OUT": V(out_weight.shape, F32),
         "QKV": V(qkv_weight.shape, F32),
         "BANKV": V(prompt_bank.shape, F32),
         "SQUARE": V((128, 128), F32),
-        "sems": pltpu.SemaphoreType.DMA((12,)),
+        "sems": pltpu.SemaphoreType.DMA((7,)),
     }
     final = pl.pallas_call(
         functools.partial(finish_kernel, total_rows, ["feats"] + OUT_NAMES + list(finals) + list(work)),
         out_shape=list(finals.values()),
-        in_specs=[vmem if k in ("vec", "late", "stat") else hbm for k in ["feats"] + OUT_NAMES],
+        in_specs=[hbm] + [vmem] * len(OUT_NAMES),
         out_specs=[hbm if k in moved else vmem for k in finals],
         scratch_shapes=list(work.values()),
         compiler_params=pltpu.CompilerParams(vmem_limit_bytes=VMEM_LIMIT),
         name="finish",
-    )(columns, *results)
+    )(columns, *[pltpu.with_memory_space_constraint(v, pltpu.VMEM) for v in results])
     vectors = ("o_encb", "o_outb", "o_ag", "o_ash", "o_upb", "o_downb", "o_fg", "o_fsh")
     return tuple(
         v[0] if k in vectors else v.T if k == "o_feats" else v for k, v in zip(finals, final, strict=True)

time: 92.4 us -> 82 us (0.89)
  Pallas kernels: 90.4 us -> 80.3 us
    pallas_call x1, Pallas kernels: 84.6 us -> 76.8 us  [per_device(): pl.pallas_call(functools.partial(layer_kernel, count, total_rows, cuts, p...]
    pallas_call x1, Pallas kernels: 5.78 us -> 3.55 us  [per_device(): pl.pallas_call(functools.partial(finish_kernel, total_rows, ['feats'] + O...]
where the time goes in v3:
time: 82 us; the launch traced here: 81.8 us
  Pallas kernels  80.3 us (98%)
  between operations  1.47 us (2%)
    pallas_call x1, Pallas kernels, per_device(): pl.pallas_call(functools.partial(layer_kernel, count, total_rows, cuts, p...  76.8 us
    pallas_call x1, Pallas kernels, per_device(): pl.pallas_call(functools.partial(finish_kernel, total_rows, ['feats'] + O...  3.55 us

profile of v3, /device:TPU:0, one launch (start us, length us, event | category | flops | bytes accessed | tf_op | source)
XLA Modules:
  0.0 81.8 jit_solution(13065058171231568542)
XLA Ops:
  1.3 76.8 %layer.1 = (f32[512,512]{1,0:T(8,128)S(1)}, f32[100,512]{1,0:T(8,128)S(1)}, bf16[5120,128]{1,0:T(8,128)(2,1)S(1)}, bf16[2,1536,128]{2,1,0:T(8,128)(2,1)S(1)}, bf...) custom-call(f32[100,512]{1,0:T(8,128)} %bitcast.18, ...), custom_call_target="tpu_custom_call" | custom-call | tf_op jit(solution)/shard_map/layer/pallas_call | solution.py:860
  78.1 3.5 %finish.1 = (f32[512,512]{1,0:T(8,128)}, f32[100,512]{1,0:T(8,128)}, f32[512,512]{1,0:T(8,128)}, f32[100,512]{1,0:T(8,128)}, f32[1,512]{1,0:T(1,128)}, /*index=5...) custom-call(f32[100,512]{1,0:T(8,128)} %bitcast.19, ...), custom_call_target="tpu_custom_call" | custom-call | tf_op jit(solution)/shard_map/finish/pallas_call | solution.py:900

commit v4 on v3

--- a/solution.py
+++ b/solution.py
@@ -95,13 +95,14 @@
 
 class Part:
     def __init__(self, ctx, block, first, rows, stages):
-        self.ctx, self.first, self.rows, self.stages = ctx, first, rows, stages
+        self.ctx, self.first, self.rows = ctx, first, rows
+        self.stages = [tuple(b for b in s if b) for s in stages]
+        self.whole = len(stages[-1]) == 1 or 0 in stages[-1]
         self.acc, self.recv, self.full = block.acc, block.recv, block.full
-        self.at = 0
-        self.send_sem = None
+        self.at = -1
 
     def begin(self):
-        self.base, self.len, self.off, self.k = self.first, self.rows, self.first, 0
+        self.base, self.len, self.off, self.k = self.first, self.rows, 2 * self.first, 0
         self.send_sem = self.ctx.links.send_sem()
         self._start_scatter()
 
@@ -120,22 +121,43 @@
         wait_bytes(view, self.recv_sem)
         wait_bytes(view, self.send_sem)
 
+    def _exchanges(self):
+        return self.whole and self.k == len(self.stages) - 1
+
+    def _slot(self, digit):
+        return pl.ds(pl.multiple_of(self.off + digit * self.len, 16), self.len)
+
     def _start_scatter(self):
         bits = self.stages[self.k]
         ways = 2 ** len(bits)
+        self.recv_sem = self.ctx.links.recv_sem()
+        mine, _ = self._digits(bits, 0)
         q = self.len // ways
-        self.recv_sem = self.ctx.links.recv_sem()
         for mask in range(1, ways):
             digit, row = self._digits(bits, mask)
-            src = self.acc.at[pl.ds(pl.multiple_of(self.base + digit * q, 16), q)]
-            dst = self.recv.at[pl.ds(self.off + (mask - 1) * q, q)]
+            if self._exchanges():
+                src = self.acc.at[pl.ds(pl.multiple_of(self.base, 16), self.len)]
+                dst = self.recv.at[self._slot(mine)]
+            else:
+                src = self.acc.at[pl.ds(pl.multiple_of(self.base + digit * q, 16), q)]
+                dst = self.recv.at[pl.ds(self.off + (mask - 1) * q, q)]
             self.ctx.links.start(src, dst, (row, self.ctx.head), self.send_sem, self.recv_sem)
 
     def _end_scatter(self):
         bits = self.stages[self.k]
         ways = 2 ** len(bits)
+        digit, _ = self._digits(bits, 0)
+        if self._exchanges():
+            mine = pl.ds(pl.multiple_of(self.base, 16), self.len)
+            self.recv[self._slot(digit), :] = self.acc[mine, :]
+            self._wait((ways - 1) * self.len)
+            total = self.recv[self._slot(0), :].astype(F32)
+            for i in range(1, ways):
+                total = total + self.recv[self._slot(i), :].astype(F32)
+            self.full[mine, :] = total.astype(BF)
+            self._start_gather()
+            return
         q = self.len // ways
-        digit, _ = self._digits(bits, 0)
         self.base = self.base + digit * q
         mine = pl.ds(pl.multiple_of(self.base, 16), q)
         self._wait((ways - 1) * q)
@@ -153,6 +175,8 @@
             self._start_gather()
 
     def _start_gather(self):
+        if self.k == 0:
+            return
         bits = self.stages[self.k - 1]
         mine = self.full.at[pl.ds(pl.multiple_of(self.base, 16), self.len)]
         self.recv_sem = self.ctx.links.recv_sem()
@@ -168,14 +192,18 @@
         self.base = self.base - digit * self.len
         self.len = self.len * ways
         self.k -= 1
-        if self.k > 0:
-            self._start_gather()
+        self._start_gather()
+
+    def steps(self):
+        return 2 * len(self.stages) - self.whole
 
     def done(self):
-        return self.at == 2 * len(self.stages)
+        return self.at == self.steps()
 
     def advance(self):
-        if self.at < len(self.stages):
+        if self.at < 0:
+            self.begin()
+        elif self.at < len(self.stages):
             self._end_scatter()
         elif not self.done():
             self._end_gather()
@@ -200,25 +228,30 @@
         for part in self.parts:
             rows = slice(part.first, part.first + part.rows)
             self.acc[rows, :] = (self.acc[rows, :].astype(F32) + self.got[rows, :].astype(F32)).astype(BF)
-            part.begin()
 
 
 class Ctx:
     pass
 
 
-def share_rows(ctx, slots, count):
-    mine = slots.at[ctx.row]
+def others_of(ctx, count):
+    steps = sorted(range(1, count), key=lambda k: min(k, count - k))
+    rows = [lax.rem(ctx.row + k, count) for k in steps]
+    return [(row, head) for row in rows for head in (ctx.head, 1 - ctx.head)] + [ctx.twin]
+
+
+def share_slots(ctx, slots, place, devices):
+    mine = slots.at[place]
     send, recv = ctx.links.send_sem(), ctx.links.recv_sem()
-    for k in range(1, count):
-        ctx.links.start(mine, mine, (lax.rem(ctx.row + k, count), ctx.head), send, recv)
-    others = slots.at[pl.ds(0, count - 1)]
+    for device in devices:
+        ctx.links.start(mine, mine, device, send, recv)
+    others = slots.at[pl.ds(0, len(devices))]
     ctx.links.open.append(functools.partial(wait_bytes, others, send))
     return functools.partial(wait_bytes, others, recv)
 
 
 SMALL = [
-    "mask", "pidx", "encw", "encb", "outb", "ag", "ash", "downb", "fg", "fsh",
+    "mask", "splits", "pidx", "encw", "encb", "outb", "ag", "ash", "downb", "fg", "fsh",
 ]
 IN_NAMES = [
     "feats", "mask", "splits", "pidx", "bank", "encw", "encb", "qkvw", "outw", "outb", "ag", "ash", "upw",
@@ -228,35 +261,33 @@
     "output", "uf", "rffn", "rqkv", "rbank", "vec", "late", "stat",
 ]
 CUTS = {
-    "d": [(1536, [(1, 2), (4, 8)]), (512, [(2,), (1,), (4,), (8,)])],
-    "u": [(1024, [(4,), (1, 2), (8,)]), (1024, [(1, 2), (4, 8)])],
-    "o": [(1024, [(2,), (8,), (1, 4)])],
-    "q": [(768, [(1,), (2,), (4,), (8,)]), (768, [(4,), (1,), (2,), (8,)])],
-    "r": [(512, [(1,), (2, 4), (8,)]), (768, [(1,), (2,), (4, 8)]), (256, [(1,), (2, 4), (8,)])],
-    "l": [(512, [(2, 4), (1,), (8,)]), (512, [(4,), (1, 2), (8,)]), (256, [(1, 2), (4, 8)])],
+    "d": [(1024, [(2,), (1,), (4, 8)]), (1024, [(1, 2), (4, 8)])],
+    "u": [(1024, [(1,), (4,), (2, 8)]), (1024, [(4,), (2,), (1,), (8,)])],
+    "o": [(1024, [(1, 2), (8,), (4,)])],
+    "q": [(256, [(2,), (1,), (4,), (8,)]), (512, [(1,), (2,), (4,), (8,)]), (768, [(4,), (1, 2), (8,)])],
+    "r": [(768, [(1,), (2, 4), (8,)]), (768, [(2,), (1, 4), (8,)])],
+    "l": [(768, [(4,), (1, 2), (8,)]), (512, [(1, 2), (4, 8)])],
 }
 PLAN = [
     [],
     [],
+    ["d1", "d0"],
     [],
     [],
-    [],
-    [],
-    [],
-    [],
-    [],
-    [],
-    [],
-    ["d0"],
+    ["u1", "u0", "o0"],
     [],
     ["d1"],
-    ["u0"],
     [],
-    ["u1", "d0"],
-    ["q0", "q1", "d1"],
+    ["d0", "u1", "u0"],
+    ["d1"],
+    ["o0", "q1", "q0", "q2"],
+    ["d0", "u1", "u0"],
+    ["d1", "q0", "q1"],
     ["o0"],
+    ["u1", "q2", "d0"],
+    ["u0", "r0", "l0", "r1", "l1", "o0"],
     [],
-    ["u1", "u0", "q0", "q1", "d1", "d0", "r0", "l0", "l1", "q1", "r1", "r2", "o0", "l2", "u1", "u0", "q0", "d1", "q1", "r0", "l2", "d0", "u0", "l0", "q0", "d1", "r1", "l1", "q1", "r2", "r0", "o0", "l2", "l0", "d1", "q0", "u1", "r1", "l1", "r2", "r0", "l0", "u0", "q1", "q0", "o0", "l2", "r1", "d1", "l1", "l0", "r2", "r0", "q1", "q0", "r1", "u0", "d1", "r0", "o0", "l1", "l0", "q0", "r2", "q1", "r1", "o0", "r2", "l1"],
+    ["d1", "q0", "q1", "u1", "q2", "d0", "r0", "u0", "l0", "r1", "q0", "o0", "q1", "u1", "l1", "q2", "d0", "r0", "l0", "u0", "r1", "q0", "q1", "l1", "r0", "l0", "o0", "u1", "q0", "q1", "r1", "q2", "l1", "u0", "d0", "q0", "r0", "u1", "l0", "r1", "q1", "l1", "q2", "q0", "r0", "l0", "q1", "r1"],
 ]
 
 
@@ -281,13 +312,10 @@
         "up": (g.upw, g.WU.at[h]),
         "down": (g.downw, g.WD.at[h]),
     }
-    g.TILE[...] = jnp.zeros_like(g.TILE)
+    everyone = others_of(ctx, count)
     barrier = pltpu.get_barrier_semaphore()
-    pl.semaphore_signal(barrier, inc=1, device_id=ctx.twin, device_id_type=MESH)
-    for k in range(1, count):
-        pl.semaphore_signal(
-            barrier, inc=1, device_id=(lax.rem(ctx.row + k, count), h), device_id_type=MESH
-        )
+    for device in everyone:
+        pl.semaphore_signal(barrier, inc=1, device_id=device, device_id_type=MESH)
     l_small = [loads.copy(getattr(g, k), getattr(g, k + "_")) for k in SMALL]
     l_bank = loads.copy(g.bank, g.BANKV)
     l_own = {k: loads.copy(*v) for k, v in own.items()}
@@ -304,14 +332,15 @@
     g.SQUARE[...] = jnp.zeros_like(g.SQUARE)
     l_feats.wait()
     f = g.F[h]
-    g.TILE[0] = to_rows([lane_sum(f), lane_sum(f * f)])
-    pl.semaphore_wait(barrier, count)
-    c_tile = links.copy(g.TILE.at[0], g.TILE.at[1], ctx.twin)
+    rows = to_rows([lane_sum(f), lane_sum(f * f)])
+    place = ctx.row * 2 + h
+    g.MOM[place, :, 0:128] = rows[0:1]
+    g.MOM[place, :, 128:256] = rows[1:2]
+    pl.semaphore_wait(barrier, len(everyone))
+    wait_moments = share_slots(ctx, g.MOM, place, everyone)
     c_feats = links.copy(g.feats, g.F.at[h], ctx.twin)
-    c_tile.wait_recv()
-    g.MOM[ctx.row] = g.TILE[0] + g.TILE[1]
-    wait_moments = share_rows(ctx, g.MOM, count)
-    c_own = {k: links.copy(*v, ctx.twin) for k, v in own.items()}
+    c_own = {"qkv": links.copy(*own["qkv"], ctx.twin)}
+    c_own |= {k: links.copy(*v, ctx.twin) for k, v in own.items() if k != "qkv"}
 
     for c in l_small:
         c.wait()
@@ -320,7 +349,7 @@
     l_bank.wait()
     g.SRC[CONTEXT_MAX:KEYS, :] = tn(g.SEL[...], g.BANKV[...]).astype(BF)
     maybe = lax.broadcasted_iota(jnp.int32, (CONTEXT_MAX - CONTEXT_MIN, 1), 0) + CONTEXT_MIN
-    g.BIAS[...] = jnp.where(maybe < g.splits[0], 0.0, -1e30)
+    g.BIAS[...] = jnp.where(maybe < g.splits_[0], 0.0, -1e30)
     g.VEC[...] = jnp.zeros_like(g.VEC)
     g.LATE[0] = jnp.zeros_like(g.LATE[0])
     live = g.mask_[...].astype(F32)
@@ -338,10 +367,10 @@
     c_feats.wait_recv()
     wait_moments()
     moments = g.MOM[0]
-    for k in range(1, count):
+    for k in range(1, 2 * count):
         moments = moments + g.MOM[k]
-    mean = moments[0:1, :] / total_rows
-    var = moments[1:2, :] / total_rows - mean * mean
+    mean = moments[:, 0:128] / total_rows
+    var = moments[:, 128:256] / total_rows - mean * mean
     g.STAT[0:1, :] = mean
     g.STAT[1:2, :] = lax.rsqrt(var + EPS)
     g.SQUARE[0:8, :] = g.STAT[...]
@@ -448,33 +477,26 @@
 
     put(down.give, 0, tn(g.ACT[o], g.GM[...]).astype(BF))
     down.send_core()
+
+    gm = g.GM[...]
+    d = g.DJ[...]
+    for s in range(2):
+        du = (g.DG[s] * nt(gm, g.WD[s])).astype(BF)
+        g.DU[s] = du
+        g.VEC[7 + s : 8 + s, :] = row_sum(du.astype(F32))
+        d = d + nt(du, g.WU[s])
+    xhat = g.XH[...]
+    g.VEC[2:3, :] = row_sum(d * xhat)
+    g.VEC[3:4, :] = row_sum(d)
+    d = d * g.ag_[...]
+    d = g.RS[...] * (d - lane_mean(d) - xhat * lane_mean(d * xhat))
+    g.DJ[...] = d
+    gb = d.astype(BF)
+    g.GB[...] = gb
+    g.VEC[1:2, :] = row_sum(gb.astype(F32))
     put(down.acc, 0, tn(g.ACT[h], g.GM[...]).astype(BF))
-
-    tile = n // 2
-
-    def backward(t):
-        rows = slice(t * tile, t * tile + tile)
-        gm = g.GM[rows, :]
-        d = g.DJ[rows, :]
-        for s in range(2):
-            du = (g.DG[s, rows, :] * nt(gm, g.WD[s])).astype(BF)
-            g.DU[s, rows, :] = du
-            g.VEC[7 + s : 8 + s, :] += row_sum(du.astype(F32))
-            d = d + nt(du, g.WU[s])
-        xhat = g.XH[rows, :]
-        g.VEC[2:3, :] += row_sum(d * xhat)
-        g.VEC[3:4, :] += row_sum(d)
-        d = d * g.ag_[...]
-        d = g.RS[rows, :] * (d - lane_mean(d) - xhat * lane_mean(d * xhat))
-        g.DJ[rows, :] = d
-        gb = d.astype(BF)
-        g.GB[rows, :] = gb
-        g.VEC[1:2, :] += row_sum(gb.astype(F32))
-
-    backward(0)
     down.merge_core()
-    backward(1)
-    tick(4)
+    tick(2)
     put(up.give, 0, tn(g.AB[...], g.DU[o]).astype(BF))
     up.send_core()
     for j in range(2):
@@ -484,18 +506,20 @@
     put(up.acc, 0, tn(g.AB[...], g.DU[h]).astype(BF))
     for j in range(2):
         put(out.acc, 128 * j * 4, nn(g.AT[2 * h + j], g.GB[...]).astype(BF))
-    tick(5)
-
+    tick(3)
+
+    g.HQT[...] = g.HB[h].T
+    g.SRCT[...] = g.SRC[pl.ds(pl.multiple_of(h * n, n), n), :].T
     for j in range(4):
         d = nt(g.WO[j // 2, 128 * (j % 2) : 128 * (j % 2) + 128, :], g.GB[...]).astype(BF)
         g.DOT[j] = d
         df = d.astype(F32)
         g.INNER[j, 0:1, :] = row_sum(df * g.AT[j].astype(F32))
         g.DOT2[j] = (df * g.INV[j, 0:1, :]).astype(BF)
-    tick(6)
+    tick(4)
     up.merge_core()
     out.merge_core()
-    tick(7)
+    tick(5)
 
     vec_stages = vec_groups(count)
     vec = Ctx()
@@ -531,8 +555,8 @@
         q, dot, dot2 = g.Q[j], g.DOT[j], g.DOT2[j]
         inner, factor = g.INNER[j, 0:1, :], g.INV[j, 0:1, :]
         dq = None
-        for t in range(KEYS // 256):
-            rows = slice(256 * t, 256 * t + 256)
+        for t in range(KEYS // 512):
+            rows = slice(512 * t, 512 * t + 512)
             e = g.E[j, rows, :]
             upstream = nn(g.V[j, rows, :], dot)
             ds = (e.astype(F32) * ((upstream - inner) * factor)).astype(BF)
@@ -558,30 +582,28 @@
         block.send_core()
         put(block.acc, n, nn(g.SRCT[...], g.DKVO[2 * h + p]).astype(BF))
 
-    g.HQT[...] = g.HB[h].T
-    g.SRCT[...] = g.SRC[pl.ds(pl.multiple_of(h * n, n), n), :].T
     attend_back(0)
-    tick(8)
+    tick(6)
     attend_back(2)
-    tick(9)
+    tick(7)
     q_grads(0, qkv0)
     attend_back(1)
-    tick(10)
+    tick(8)
     merge_kv(0)
     merge_kv(2)
     kv_grads(0, qkv0)
-    tick(11)
+    tick(9)
     attend_back(3)
-    tick(12)
+    tick(10)
     qkv0.merge_core()
     c_vec.wait_recv()
     vec_start(g.VEC[...] + g.VECR[...])
-    tick(13)
+    tick(11)
     q_grads(1, qkv1)
     for j in range(4):
         g.DQ[:, 128 * j : 128 * j + 128] = g.DQT[j].T
     dh = g.DJ[...] + nt(g.DQ[:, 0:256], g.WQKV[0, 0]) + nt(g.DQ[:, 256:512], g.WQKV[1, 0])
-    tick(14)
+    tick(12)
 
     merge_kv(1)
     merge_kv(3)
@@ -594,9 +616,9 @@
     g.GH[0:edge, :] = (dh[0:edge] + kvh[0:edge]).astype(BF)
     first = jnp.where(h == 0, 1.0, 0.0)
     g.GH[edge:n, :] = (dh[edge:n] + kvh[edge:n] * first).astype(BF)
-    tick(15)
+    tick(13)
     kv_grads(1, qkv1)
-    tick(16)
+    tick(14)
     gh = g.GH[...]
     g.ENC[0:features, :] = nn(g.NL[h], gh)
     g.ENC[features:, :] = jnp.zeros_like(g.ENC[features:, :])
@@ -615,16 +637,14 @@
         0,
         nn(g.SEL[pl.ds(pl.multiple_of(h * bank_rows, bank_rows), bank_rows), :], g.DP[o]).astype(BF),
     )
-    tick(17)
+    tick(15)
     qkv1.merge_core()
     last.core_copy.wait_recv()
     rows = slice(enc_at, enc_at + 256)
     last.acc[rows, :] = (last.acc[rows, :].astype(F32) + last.got[...].astype(F32)).astype(BF)
     if last.n > enc_at + 256:
         last.acc[enc_at + 256 :, :] = jnp.zeros_like(last.acc[enc_at + 256 :, :])
-    for part in last.parts:
-        part.begin()
-    tick(18)
+    tick(16)
     vec_end()
 
     scale = g.COLS[:, 2:3]
@@ -636,11 +656,11 @@
     for b in range(4):
         g.LATE[0, 2 + b : 3 + b, :] = eb[:, 128 * b : 128 * b + 128]
     c_late = links.copy(g.LATE.at[0], g.LATE.at[1], ctx.twin)
-    tick(19)
+    tick(17)
     c_late.wait_recv()
     g.LSUM[ctx.row] = g.LATE[0] + g.LATE[1]
-    wait_late = share_rows(ctx, g.LSUM, count)
-    tick(20)
+    wait_late = share_slots(ctx, g.LSUM, ctx.row, everyone[0:-1:2])
+    tick(18)
     rest = [p for b in blocks.values() for p in b.parts]
     while not all(p.done() for p in rest):
         for p in rest:
@@ -766,7 +786,6 @@
     ]
     vmem = pl.BlockSpec(memory_space=pltpu.VMEM)
     hbm = pl.BlockSpec(memory_space=pl.ANY)
-    in_specs = [pl.BlockSpec(memory_space=pltpu.SMEM) if k == "splits" else hbm for k in IN_NAMES]
     bits = [2**i for i in range(count.bit_length() - 1)]
     grain = 16 * count
     block_rows = {"d": 2048, "u": 2048, "o": 1024, "q": 1536, "r": 1536, "l": 1280}
@@ -788,6 +807,7 @@
     }
     V = pltpu.VMEM
     scratch = {k + "_": V(args[IN_NAMES.index(k)].shape, args[IN_NAMES.index(k)].dtype) for k in SMALL}
+    scratch["splits_"] = pltpu.SMEM(splits.shape, splits.dtype)
     scratch |= {
         "F": V((2, features, n), F32),
         "WQKV": V((2, 3, d, 256), BF),
@@ -799,9 +819,8 @@
         "COT": V((n, d), F32),
         "SQUARE": V((128, 128), F32),
         "COLS": V((features, 128), F32),
-        "TILE": V((2, 8, 128), F32),
         "LATE": V((2, 8, 128), F32),
-        "MOM": V((count, 8, 128), F32),
+        "MOM": V((2 * count, 1, 256), F32),
         "LSUM": V((count, 8, 128), F32),
         "STAT": V((8, 128), F32),
         "VEC": V((16, d), F32),
@@ -850,17 +869,17 @@
         scratch["CG" + k] = V((small, 128), BF)
         scratch["CR" + k] = V((small, 128), BF)
         scratch["CA" + k] = V((r, 128), BF)
-        scratch["CV" + k] = V((r, 128), BF)
+        scratch["CV" + k] = V((2 * r, 128), BF)
     parts = [stages for v in cuts.values() for _, stages in v]
-    once = 23 + len(vec_groups(count))
-    sem_counts = (once + len(parts), once + sum(2 * len(s) for s in parts), 8 + len(SMALL))
+    once = 22 + len(vec_groups(count))
+    sem_counts = (once + len(parts), once + sum(2 * len(s) - (len(s[-1]) == 1 or 0 in s[-1]) for s in parts), 8 + len(SMALL))
     for k, v in zip(("ssem", "rsem", "lsem"), sem_counts, strict=True):
         scratch[k] = pltpu.SemaphoreType.DMA((v,))
     names = IN_NAMES + OUT_NAMES + list(scratch)
     results = pl.pallas_call(
         functools.partial(layer_kernel, count, total_rows, cuts, plan, sem_counts, names),
         out_shape=[pltpu.VMEM(outs[k].shape, outs[k].dtype) for k in OUT_NAMES],
-        in_specs=in_specs,
+        in_specs=[hbm] * len(IN_NAMES),
         out_specs=[vmem] * len(OUT_NAMES),
         scratch_shapes=list(scratch.values()),
         compiler_params=pltpu.CompilerParams(

time: 82 us -> 75.7 us (0.923)
  Pallas kernels: 80.3 us -> 74.1 us
    pallas_call x1, Pallas kernels: 76.8 us -> 70.5 us  [per_device(): pl.pallas_call(functools.partial(layer_kernel, count, total_rows, cuts, p...]
where the time goes in v4:
time: 75.7 us; the launch traced here: 75.6 us
  Pallas kernels  74.1 us (98%)
  between operations  1.47 us (2%)
    pallas_call x1, Pallas kernels, per_device(): pl.pallas_call(functools.partial(layer_kernel, count, total_rows, cuts, p...  70.5 us
    pallas_call x1, Pallas kernels, per_device(): pl.pallas_call(functools.partial(finish_kernel, total_rows, ['feats'] + O...  3.55 us

profile of v4, /device:TPU:0, one launch (start us, length us, event | category | flops | bytes accessed | tf_op | source)
XLA Modules:
  0.0 75.6 jit_solution(10403941847223496056)
XLA Ops:
  1.3 70.5 %layer.1 = (f32[512,512]{1,0:T(8,128)S(1)}, f32[100,512]{1,0:T(8,128)S(1)}, bf16[5120,128]{1,0:T(8,128)(2,1)S(1)}, bf16[2,1536,128]{2,1,0:T(8,128)(2,1)S(1)}, bf...) custom-call(f32[100,512]{1,0:T(8,128)} %bitcast.18, ...), custom_call_target="tpu_custom_call" | custom-call | tf_op jit(solution)/shard_map/layer/pallas_call | solution.py:879
  71.8 3.5 %finish.1 = (f32[512,512]{1,0:T(8,128)}, f32[100,512]{1,0:T(8,128)}, f32[512,512]{1,0:T(8,128)}, f32[100,512]{1,0:T(8,128)}, f32[1,512]{1,0:T(1,128)}, /*index=5...) custom-call(f32[100,512]{1,0:T(8,128)} %bitcast.19, ...), custom_call_target="tpu_custom_call" | custom-call | tf_op jit(solution)/shard_map/finish/pallas_call | solution.py:919

commit v5 on v4

--- a/solution.py
+++ b/solution.py
@@ -287,7 +287,8 @@
     ["u1", "q2", "d0"],
     ["u0", "r0", "l0", "r1", "l1", "o0"],
     [],
-    ["d1", "q0", "q1", "u1", "q2", "d0", "r0", "u0", "l0", "r1", "q0", "o0", "q1", "u1", "l1", "q2", "d0", "r0", "l0", "u0", "r1", "q0", "q1", "l1", "r0", "l0", "o0", "u1", "q0", "q1", "r1", "q2", "l1", "u0", "d0", "q0", "r0", "u1", "l0", "r1", "q1", "l1", "q2", "q0", "r0", "l0", "q1", "r1"],
+    ["d1", "q0", "q1", "u1", "q2", "d0", "r0", "u0", "l0", "r1", "q0", "o0", "q1", "u1", "l1", "q2", "d0", "r0", "l0", "u0", "r1", "q0", "q1", "l1"],
+    ["r0", "l0", "o0", "u1", "q0", "q1", "r1", "q2", "l1", "u0", "d0", "q0", "r0", "u1", "l0", "r1", "q1", "l1", "q2", "q0", "r0", "l0", "q1", "r1"],
 ]
 
 
@@ -329,6 +330,10 @@
     def lane_sum(v):
         return jnp.sum(v, axis=-1, keepdims=True)
 
+    def put_vector(half, i, value):
+        for b in range(4):
+            g.VEC[half, 4 * i + b : 4 * i + b + 1, :] = value[:, 128 * b : 128 * b + 128]
+
     g.SQUARE[...] = jnp.zeros_like(g.SQUARE)
     l_feats.wait()
     f = g.F[h]
@@ -350,8 +355,6 @@
     g.SRC[CONTEXT_MAX:KEYS, :] = tn(g.SEL[...], g.BANKV[...]).astype(BF)
     maybe = lax.broadcasted_iota(jnp.int32, (CONTEXT_MAX - CONTEXT_MIN, 1), 0) + CONTEXT_MIN
     g.BIAS[...] = jnp.where(maybe < g.splits_[0], 0.0, -1e30)
-    g.VEC[...] = jnp.zeros_like(g.VEC)
-    g.LATE[0] = jnp.zeros_like(g.LATE[0])
     live = g.mask_[...].astype(F32)
     scale = live * jnp.sqrt(features / jnp.sum(live, axis=-1, keepdims=True))
     g.STAT[...] = jnp.zeros_like(g.STAT)
@@ -449,9 +452,9 @@
     g.DJ[...] = d
     gm = d.astype(BF)
     g.GM[...] = gm
-    g.VEC[4:5, :] = row_sum(gm.astype(F32))
-    g.VEC[5:6, :] = row_sum(ct * xhat)
-    g.VEC[6:7, :] = row_sum(ct)
+    put_vector(1, 0, row_sum(gm.astype(F32)))
+    put_vector(1, 1, row_sum(ct * xhat))
+    put_vector(1, 2, row_sum(ct))
 
     def put(ref, first, value):
         r = value.shape[0]
@@ -474,6 +477,11 @@
     def tick(i):
         for k in plan[i] if i < len(plan) else []:
             blocks[k[0]].parts[int(k[1])].advance()
+            share_last()
+
+    def share_last():
+        if not hasattr(ctx, "c_last") and all(p.done() for p in last.parts):
+            ctx.c_last = links.copy(g.rbank.at[h], g.rbank.at[h], ctx.twin)
 
     put(down.give, 0, tn(g.ACT[o], g.GM[...]).astype(BF))
     down.send_core()
@@ -483,17 +491,17 @@
     for s in range(2):
         du = (g.DG[s] * nt(gm, g.WD[s])).astype(BF)
         g.DU[s] = du
-        g.VEC[7 + s : 8 + s, :] = row_sum(du.astype(F32))
+        put_vector(s, 3, row_sum(du.astype(F32)))
         d = d + nt(du, g.WU[s])
     xhat = g.XH[...]
-    g.VEC[2:3, :] = row_sum(d * xhat)
-    g.VEC[3:4, :] = row_sum(d)
+    put_vector(0, 1, row_sum(d * xhat))
+    put_vector(0, 2, row_sum(d))
     d = d * g.ag_[...]
     d = g.RS[...] * (d - lane_mean(d) - xhat * lane_mean(d * xhat))
     g.DJ[...] = d
     gb = d.astype(BF)
     g.GB[...] = gb
-    g.VEC[1:2, :] = row_sum(gb.astype(F32))
+    put_vector(0, 0, row_sum(gb.astype(F32)))
     put(down.acc, 0, tn(g.ACT[h], g.GM[...]).astype(BF))
     down.merge_core()
     tick(2)
@@ -502,7 +510,7 @@
     for j in range(2):
         put(out.give, 128 * j * 4, nn(g.AT[2 * o + j], g.GB[...]).astype(BF))
     out.send_core()
-    c_vec = links.copy(g.VEC, g.VECR, ctx.twin)
+    c_vec = links.copy(g.VEC.at[o], g.VECR, ctx.twin)
     put(up.acc, 0, tn(g.AB[...], g.DU[h]).astype(BF))
     for j in range(2):
         put(out.acc, 128 * j * 4, nn(g.AT[2 * h + j], g.GB[...]).astype(BF))
@@ -547,7 +555,8 @@
         if vec.k < len(vec_stages):
             vec_start(value)
         else:
-            g.vec[...] = value
+            g.vec[h] = value
+            vec.copy = links.copy(g.vec.at[h], g.vec.at[h], ctx.twin)
 
     kv_copies = {}
 
@@ -597,7 +606,7 @@
     tick(10)
     qkv0.merge_core()
     c_vec.wait_recv()
-    vec_start(g.VEC[...] + g.VECR[...])
+    vec_start(g.VEC[h] + g.VECR[...])
     tick(11)
     q_grads(1, qkv1)
     for j in range(4):
@@ -651,31 +660,37 @@
     uf = nt(g.encw_[...], gh) * scale
     g.uf[...] = uf
     g.SQUARE[...] = jnp.zeros_like(g.SQUARE)
-    g.LATE[0] = to_rows([lane_sum(uf), lane_sum(uf * (g.F[h] - g.COLS[:, 0:1]))])
+    rows = to_rows([lane_sum(uf), lane_sum(uf * (g.F[h] - g.COLS[:, 0:1]))])
     eb = row_sum(gh.astype(F32))
-    for b in range(4):
-        g.LATE[0, 2 + b : 3 + b, :] = eb[:, 128 * b : 128 * b + 128]
-    c_late = links.copy(g.LATE.at[0], g.LATE.at[1], ctx.twin)
+    g.LATE[0, :, 0:128] = rows[0:1]
+    g.LATE[0, :, 128:256] = rows[1:2]
+    g.LATE[0, :, 256:384] = eb[:, 0:128]
+    g.LATE[1] = eb[:, 128:512]
+    c_late = links.copy(g.LATE.at[o], g.LATER, ctx.twin)
     tick(17)
     c_late.wait_recv()
-    g.LSUM[ctx.row] = g.LATE[0] + g.LATE[1]
+    g.LSUM[ctx.row] = g.LATE[h] + g.LATER[...]
     wait_late = share_slots(ctx, g.LSUM, ctx.row, everyone[0:-1:2])
     tick(18)
+    while vec.k < len(vec_stages):
+        vec_end()
+    wait_late()
+    late = g.LSUM[0]
+    for k in range(1, count):
+        late = late + g.LSUM[k]
+    g.late[h] = late
+    c_late_half = links.copy(g.late.at[h], g.late.at[h], ctx.twin)
+    tick(19)
     rest = [p for b in blocks.values() for p in b.parts]
     while not all(p.done() for p in rest):
         for p in rest:
             if not p.done():
                 p.advance()
-    while vec.k < len(vec_stages):
-        vec_end()
-    c_last = links.copy(g.rbank.at[h], g.rbank.at[h], ctx.twin)
-    wait_late()
-    late = g.LSUM[0]
-    for k in range(1, count):
-        late = late + g.LSUM[k]
-    g.late[...] = late
+                share_last()
     g.stat[...] = g.STAT[...]
-    c_last.wait_recv()
+    vec.copy.wait_recv()
+    c_late_half.wait_recv()
+    ctx.c_last.wait_recv()
     links.drain()
     assert (links.sent, links.received, loads.used) == sem_counts, (links.sent, links.received, loads.used)
 
@@ -702,6 +717,11 @@
     outs = [copy(g.output, g.o_output)]
     c_feats = copy(g.feats, g.FEATS)
     up_at = g.rffn.shape[0] // 5 * 2
+
+    late = jnp.concatenate([g.late[0], g.late[1]], axis=-1)
+    vectors = [
+        (0, 0, g.o_outb), (0, 1, g.o_ag), (0, 2, g.o_ash), (1, 0, g.o_downb), (1, 1, g.o_fg), (1, 2, g.o_fsh),
+    ]
 
     def block(ref, first, rows):
         return ref[first : first + rows, :].astype(F32)
@@ -729,17 +749,13 @@
             g.BANKV[256 * s : 256 * s + 256, cols] = g.rbank[s, 256 * b : 256 * b + 256, :].astype(F32)
         g.o_encw[0:64, cols] = g.rbank[0, 1024 + 64 * b : 1024 + 64 * b + 64, :].astype(F32)
         g.o_encw[64:features, cols] = g.rbank[1, 1024 + 64 * b : 1024 + 64 * b + features - 64, :].astype(F32)
-        g.o_encb[:, cols] = g.late[2 + b : 3 + b, :]
+        g.o_encb[:, cols] = late[:, 256 + 128 * b : 384 + 128 * b]
+        for s, i, ref in vectors:
+            ref[:, cols] = g.vec[s, 4 * i + b : 4 * i + b + 1, :]
+        g.o_upb[:, cols] = g.vec[h, 12 + b : 13 + b, :]
     outs.append(copy(g.BANKV, g.o_bank))
-    g.o_outb[...] = g.vec[1:2, :]
-    g.o_ag[...] = g.vec[2:3, :]
-    g.o_ash[...] = g.vec[3:4, :]
-    g.o_downb[...] = g.vec[4:5, :]
-    g.o_fg[...] = g.vec[5:6, :]
-    g.o_fsh[...] = g.vec[6:7, :]
-    g.o_upb[...] = g.vec[pl.ds(7 + h, 1), :]
     mean, inverse = g.stat[0:1, :], g.stat[1:2, :]
-    b1, b2 = g.late[0:1, :], g.late[1:2, :]
+    b1, b2 = late[:, 0:128], late[:, 128:256]
     var_grad = -0.5 * inverse * inverse * inverse * b2
     g.SQUARE[...] = jnp.zeros_like(g.SQUARE)
     g.SQUARE[0:1, :] = inverse
@@ -801,8 +817,8 @@
         "rffn": S((block_rows["d"] + block_rows["u"] + block_rows["o"], 128), BF),
         "rqkv": S((2, block_rows["q"], 128), BF),
         "rbank": S((2, block_rows["l"], 128), BF),
-        "vec": S((16, d), F32),
-        "late": S((8, 128), F32),
+        "vec": S((2, 16, 128), F32),
+        "late": S((2, 1, 384), F32),
         "stat": S((8, 128), F32),
     }
     V = pltpu.VMEM
@@ -819,13 +835,14 @@
         "COT": V((n, d), F32),
         "SQUARE": V((128, 128), F32),
         "COLS": V((features, 128), F32),
-        "LATE": V((2, 8, 128), F32),
+        "LATE": V((2, 1, 384), F32),
+        "LATER": V((1, 384), F32),
         "MOM": V((2 * count, 1, 256), F32),
-        "LSUM": V((count, 8, 128), F32),
+        "LSUM": V((count, 1, 384), F32),
         "STAT": V((8, 128), F32),
-        "VEC": V((16, d), F32),
-        "VECR": V((16, d), F32),
-        "VECS": V((len(vec_groups(count)), 4, 16, d), F32),
+        "VEC": V((2, 16, 128), F32),
+        "VECR": V((16, 128), F32),
+        "VECS": V((len(vec_groups(count)), 4, 16, 128), F32),
         "SEL": V((prompt_bank.shape[0], P_SIZE), BF),
         "SRC": V((KEYS, d), BF),
         "BIAS": V((CONTEXT_MAX - CONTEXT_MIN, 1), F32),
@@ -871,7 +888,7 @@
         scratch["CA" + k] = V((r, 128), BF)
         scratch["CV" + k] = V((2 * r, 128), BF)
     parts = [stages for v in cuts.values() for _, stages in v]
-    once = 22 + len(vec_groups(count))
+    once = 24 + len(vec_groups(count))
     sem_counts = (once + len(parts), once + sum(2 * len(s) - (len(s[-1]) == 1 or 0 in s[-1]) for s in parts), 8 + len(SMALL))
     for k, v in zip(("ssem", "rsem", "lsem"), sem_counts, strict=True):
         scratch[k] = pltpu.SemaphoreType.DMA((v,))

time: 75.7 us -> 72.5 us (0.958)
  Pallas kernels: 74.1 us -> 70.9 us
    pallas_call x1, Pallas kernels: 70.5 us -> 67.3 us  [per_device(): pl.pallas_call(functools.partial(layer_kernel, count, total_rows, cuts, p...]
where the time goes in v5:
time: 72.5 us; the launch traced here: 72.4 us
  Pallas kernels  70.9 us (98%)
  between operations  1.47 us (2%)
    pallas_call x1, Pallas kernels, per_device(): pl.pallas_call(functools.partial(layer_kernel, count, total_rows, cuts, p...  67.3 us
    pallas_call x1, Pallas kernels, per_device(): pl.pallas_call(functools.partial(finish_kernel, total_rows, ['feats'] + O...  3.55 us

profile of v5, /device:TPU:0, one launch (start us, length us, event | category | flops | bytes accessed | tf_op | source)
XLA Modules:
  0.0 72.4 jit_solution(14371968335863939455)
XLA Ops:
  1.3 67.3 %layer.1 = (f32[512,512]{1,0:T(8,128)S(1)}, f32[100,512]{1,0:T(8,128)S(1)}, bf16[5120,128]{1,0:T(8,128)(2,1)S(1)}, bf16[2,1536,128]{2,1,0:T(8,128)(2,1)S(1)}, bf...) custom-call(f32[100,512]{1,0:T(8,128)} %bitcast.18, ...), custom_call_target="tpu_custom_call" | custom-call | tf_op jit(solution)/shard_map/layer/pallas_call | solution.py:896
  68.6 3.5 %finish.1 = (f32[512,512]{1,0:T(8,128)}, f32[100,512]{1,0:T(8,128)}, f32[512,512]{1,0:T(8,128)}, f32[100,512]{1,0:T(8,128)}, f32[1,512]{1,0:T(1,128)}, /*index=5...) custom-call(f32[100,512]{1,0:T(8,128)} %bitcast.19, ...), custom_call_target="tpu_custom_call" | custom-call | tf_op jit(solution)/shard_map/finish/pallas_call | solution.py:936

commit v6 on v5

--- a/solution.py
+++ b/solution.py
@@ -358,6 +358,7 @@
     live = g.mask_[...].astype(F32)
     scale = live * jnp.sqrt(features / jnp.sum(live, axis=-1, keepdims=True))
     g.STAT[...] = jnp.zeros_like(g.STAT)
+    g.V[:, :, 128:] = jnp.ones_like(g.V[:, :, 128:])
     g.STAT[2:3, 0:features] = scale
     for c in l_own.values():
         c.wait()
@@ -397,7 +398,7 @@
     for j in range(4):
         kv = nn(g.SRC[...], g.WKV[j]).astype(BF)
         g.K[j] = kv[:, 0:128]
-        g.V[j] = kv[:, 128:256]
+        g.V[j, :, 0:128] = kv[:, 128:256]
 
     for j in range(5):
         if j < 4:
@@ -409,11 +410,12 @@
             p = j - 1
             scores = g.S[p % 2]
             e = jnp.exp2(scores - jnp.max(scores, axis=0, keepdims=True))
-            inv = 1.0 / row_sum(e)
-            g.INV[p, 0:1, :] = inv
             e = e.astype(BF)
             g.E[p] = e
-            g.AT[p] = (tn(g.V[p], e) * inv).astype(BF)
+            mixed = tn(g.V[p], e)
+            inv = 1.0 / mixed[128:129]
+            g.INV[p, 0:1, :] = inv
+            g.AT[p] = (mixed[0:128] * inv).astype(BF)
 
     c_own["out"].wait_recv()
     c_own["up"].wait_recv()
@@ -567,7 +569,7 @@
         for t in range(KEYS // 512):
             rows = slice(512 * t, 512 * t + 512)
             e = g.E[j, rows, :]
-            upstream = nn(g.V[j, rows, :], dot)
+            upstream = nn(g.V[j, rows, 0:128], dot)
             ds = (e.astype(F32) * ((upstream - inner) * factor)).astype(BF)
             g.DKV[j, rows, 0:128] = (nn(ds, q) * (DH**-0.5 / Q_SCALE)).astype(BF)
             g.DKV[j, rows, 128:256] = nt(e, dot2).astype(BF)
@@ -680,6 +682,7 @@
         late = late + g.LSUM[k]
     g.late[h] = late
     c_late_half = links.copy(g.late.at[h], g.late.at[h], ctx.twin)
+    links.drain()
     tick(19)
     rest = [p for b in blocks.values() for p in b.parts]
     while not all(p.done() for p in rest):
@@ -714,46 +717,45 @@
         copies.append(c)
         return c
 
-    outs = [copy(g.output, g.o_output)]
+    def done(*results):
+        for k in results:
+            copy(getattr(g, "s_" + k), getattr(g, "o_" + k))
+
+    copy(g.output, g.o_output)
     c_feats = copy(g.feats, g.FEATS)
     up_at = g.rffn.shape[0] // 5 * 2
 
-    late = jnp.concatenate([g.late[0], g.late[1]], axis=-1)
-    vectors = [
-        (0, 0, g.o_outb), (0, 1, g.o_ag), (0, 2, g.o_ash), (1, 0, g.o_downb), (1, 1, g.o_fg), (1, 2, g.o_fsh),
-    ]
-
     def block(ref, first, rows):
         return ref[first : first + rows, :].astype(F32)
 
-    for b in range(4):
-        cols = slice(128 * b, 128 * b + 128)
-        g.DOWN[:, cols] = block(g.rffn, 512 * b, 512)
-    outs.append(copy(g.DOWN, g.o_down))
-    for b in range(4):
-        cols = slice(128 * b, 128 * b + 128)
-        g.UP[:, cols] = block(g.rffn, up_at + 512 * b, 512)
-    outs.append(copy(g.UP, g.o_up))
-    for b in range(4):
-        cols = slice(128 * b, 128 * b + 128)
-        for j in range(2):
-            g.OUT[128 * j : 128 * j + 128, cols] = block(g.rffn, 2 * up_at + 512 * j + 128 * b, 128)
-    outs.append(copy(g.OUT, g.o_out))
+    columns = [slice(128 * b, 128 * b + 128) for b in range(4)]
+    for b, cols in enumerate(columns):
+        g.s_down[:, cols] = block(g.rffn, 512 * b, 512)
+    done("down")
+    for b, cols in enumerate(columns):
+        g.s_up[:, cols] = block(g.rffn, up_at + 512 * b, 512)
+    done("up")
     for c in range(3):
         for p in range(2):
-            g.QKV[c, :, 128 * p : 128 * p + 128] = g.rqkv[p, 512 * c : 512 * c + 512, :].astype(F32)
-    outs.append(copy(g.QKV, g.o_qkv))
-    for b in range(4):
-        cols = slice(128 * b, 128 * b + 128)
+            g.s_qkv[c, :, 128 * p : 128 * p + 128] = g.rqkv[p, 512 * c : 512 * c + 512, :].astype(F32)
+    done("qkv")
+    for b, cols in enumerate(columns):
         for s in range(2):
-            g.BANKV[256 * s : 256 * s + 256, cols] = g.rbank[s, 256 * b : 256 * b + 256, :].astype(F32)
-        g.o_encw[0:64, cols] = g.rbank[0, 1024 + 64 * b : 1024 + 64 * b + 64, :].astype(F32)
-        g.o_encw[64:features, cols] = g.rbank[1, 1024 + 64 * b : 1024 + 64 * b + features - 64, :].astype(F32)
-        g.o_encb[:, cols] = late[:, 256 + 128 * b : 384 + 128 * b]
-        for s, i, ref in vectors:
-            ref[:, cols] = g.vec[s, 4 * i + b : 4 * i + b + 1, :]
-        g.o_upb[:, cols] = g.vec[h, 12 + b : 13 + b, :]
-    outs.append(copy(g.BANKV, g.o_bank))
+            g.s_bank[256 * s : 256 * s + 256, cols] = g.rbank[s, 256 * b : 256 * b + 256, :].astype(F32)
+    done("bank")
+    for b, cols in enumerate(columns):
+        for j in range(2):
+            g.s_out[128 * j : 128 * j + 128, cols] = block(g.rffn, 2 * up_at + 512 * j + 128 * b, 128)
+    done("out")
+    late = jnp.concatenate([g.late[0], g.late[1]], axis=-1)
+    vectors = [(0, 0, "outb"), (0, 1, "ag"), (0, 2, "ash"), (1, 0, "downb"), (1, 1, "fg"), (1, 2, "fsh"), (h, 3, "upb")]
+    for b, cols in enumerate(columns):
+        g.s_encw[0:64, cols] = g.rbank[0, 1024 + 64 * b : 1024 + 64 * b + 64, :].astype(F32)
+        g.s_encw[64:features, cols] = g.rbank[1, 1024 + 64 * b : 1024 + 64 * b + features - 64, :].astype(F32)
+        g.s_encb[:, cols] = late[:, 256 + 128 * b : 384 + 128 * b]
+        for s, i, k in vectors:
+            getattr(g, "s_" + k)[:, cols] = g.vec[s, 4 * i + b : 4 * i + b + 1, :]
+    done("encw", "encb", *[k for _, _, k in vectors])
     mean, inverse = g.stat[0:1, :], g.stat[1:2, :]
     b1, b2 = late[:, 0:128], late[:, 128:256]
     var_grad = -0.5 * inverse * inverse * inverse * b2
@@ -761,12 +763,14 @@
     g.SQUARE[0:1, :] = inverse
     g.SQUARE[1:2, :] = (-inverse * b1 - 2.0 * mean * var_grad) / total_rows
     g.SQUARE[2:3, :] = 2.0 * var_grad / total_rows
-    columns = g.SQUARE[...].T
-    inverse, first, slope = [columns[0:features, i : i + 1] for i in range(3)]
+    turned = g.SQUARE[...].T
+    inverse, first, slope = [turned[0:features, i : i + 1] for i in range(3)]
     c_feats.wait()
-    g.o_feats[...] = g.uf[...] * inverse + first + g.FEATS[...] * slope
-    for c in outs:
-        c.wait()
+    g.s_feats[...] = g.uf[...] * inverse + first + g.FEATS[...] * slope
+    done("feats")
+    for c in copies:
+        if c is not c_feats:
+            c.wait()
 
 
 def per_device(
@@ -853,7 +857,7 @@
         "HB": V((2, n, d), BF),
         "Q": V((4, n, 128), BF),
         "K": V((4, KEYS, 128), BF),
-        "V": V((4, KEYS, 128), BF),
+        "V": V((4, KEYS, 144), BF),
         "E": V((4, KEYS, n), BF),
         "INV": V((4, 8, n), F32),
         "INNER": V((4, 8, n), F32),
@@ -922,22 +926,14 @@
         "o_fg": S((1, d), F32),
         "o_fsh": S((1, d), F32),
     }
-    moved = {"o_output", "o_bank", "o_qkv", "o_out", "o_up", "o_down"}
-    work = {
-        "FEATS": V((features, n), F32),
-        "DOWN": V(down_weight.shape, F32),
-        "UP": V(up_weight.shape, F32),
-        "OUT": V(out_weight.shape, F32),
-        "QKV": V(qkv_weight.shape, F32),
-        "BANKV": V(prompt_bank.shape, F32),
-        "SQUARE": V((128, 128), F32),
-        "sems": pltpu.SemaphoreType.DMA((7,)),
-    }
+    work = {"FEATS": V((features, n), F32), "SQUARE": V((128, 128), F32)}
+    work |= {"s" + k[1:]: V(v.shape, F32) for k, v in finals.items() if k != "o_output"}
+    work["sems"] = pltpu.SemaphoreType.DMA((1 + len(finals),))
     final = pl.pallas_call(
         functools.partial(finish_kernel, total_rows, ["feats"] + OUT_NAMES + list(finals) + list(work)),
         out_shape=list(finals.values()),
         in_specs=[hbm] + [vmem] * len(OUT_NAMES),
-        out_specs=[hbm if k in moved else vmem for k in finals],
+        out_specs=[hbm] * len(finals),
         scratch_shapes=list(work.values()),
         compiler_params=pltpu.CompilerParams(vmem_limit_bytes=VMEM_LIMIT),
         name="finish",

time: 72.5 us -> 71.8 us (level)
  no operation moved by 1% of the time
where the time goes in v6:
time: 71.8 us; the launch traced here: 71.6 us
  Pallas kernels  70.2 us (98%)
  between operations  1.47 us (2%)
    pallas_call x1, Pallas kernels, per_device(): pl.pallas_call(functools.partial(layer_kernel, count, total_rows, cuts, p...  67.2 us
    pallas_call x1, Pallas kernels, per_device(): pl.pallas_call(functools.partial(finish_kernel, total_rows, ['feats'] + O...  2.97 us

profile of v6, /device:TPU:0, one launch (start us, length us, event | category | flops | bytes accessed | tf_op | source)
XLA Modules:
  0.0 71.6 jit_solution(2211591560319435428)
XLA Ops:
  1.3 67.2 %layer.1 = (f32[512,512]{1,0:T(8,128)S(1)}, f32[100,512]{1,0:T(8,128)S(1)}, bf16[5120,128]{1,0:T(8,128)(2,1)S(1)}, bf16[2,1536,128]{2,1,0:T(8,128)(2,1)S(1)}, bf...) custom-call(f32[100,512]{1,0:T(8,128)} %bitcast.18, ...), custom_call_target="tpu_custom_call" | custom-call | tf_op jit(solution)/shard_map/layer/pallas_call | solution.py:900
  68.5 3.0 %finish.1 = (f32[512,512]{1,0:T(8,128)}, f32[100,512]{1,0:T(8,128)}, f32[512,512]{1,0:T(8,128)}, f32[100,512]{1,0:T(8,128)}, f32[1,512]{1,0:T(1,128)}, /*index=5...) custom-call(f32[100,512]{1,0:T(8,128)} %bitcast.19, ...), custom_call_target="tpu_custom_call" | custom-call | tf_op jit(solution)/shard_map/finish/pallas_call | solution.py:932

commit v7 on v6

--- a/solution.py
+++ b/solution.py
@@ -522,10 +522,9 @@
     g.SRCT[...] = g.SRC[pl.ds(pl.multiple_of(h * n, n), n), :].T
     for j in range(4):
         d = nt(g.WO[j // 2, 128 * (j % 2) : 128 * (j % 2) + 128, :], g.GB[...]).astype(BF)
-        g.DOT[j] = d
-        df = d.astype(F32)
-        g.INNER[j, 0:1, :] = row_sum(df * g.AT[j].astype(F32))
-        g.DOT2[j] = (df * g.INV[j, 0:1, :]).astype(BF)
+        d = (d.astype(F32) * g.INV[j, 0:1, :]).astype(BF)
+        g.DOT2[j] = d
+        g.INNER[j, 0:1, :] = row_sum(d.astype(F32) * g.AT[j].astype(F32))
     tick(4)
     up.merge_core()
     out.merge_core()
@@ -563,14 +562,13 @@
     kv_copies = {}
 
     def attend_back(j):
-        q, dot, dot2 = g.Q[j], g.DOT[j], g.DOT2[j]
-        inner, factor = g.INNER[j, 0:1, :], g.INV[j, 0:1, :]
+        q, dot2, inner = g.Q[j], g.DOT2[j], g.INNER[j, 0:1, :]
         dq = None
         for t in range(KEYS // 512):
             rows = slice(512 * t, 512 * t + 512)
             e = g.E[j, rows, :]
-            upstream = nn(g.V[j, rows, 0:128], dot)
-            ds = (e.astype(F32) * ((upstream - inner) * factor)).astype(BF)
+            upstream = nn(g.V[j, rows, 0:128], dot2)
+            ds = (e.astype(F32) * (upstream - inner)).astype(BF)
             g.DKV[j, rows, 0:128] = (nn(ds, q) * (DH**-0.5 / Q_SCALE)).astype(BF)
             g.DKV[j, rows, 128:256] = nt(e, dot2).astype(BF)
             part = tn(g.K[j, rows, :], ds)
@@ -872,7 +870,6 @@
         "DJ": V((n, d), F32),
         "GM": V((n, d), BF),
         "GB": V((n, d), BF),
-        "DOT": V((4, 128, n), BF),
         "DOT2": V((4, 128, n), BF),
         "DKV": V((4, KEYS, 256), BF),
         "DKVR": V((4, n, 256), BF),

time: 71.8 us -> 72.1 us (level)
  no operation moved by 1% of the time
where the time goes in v7:
time: 72.1 us; the launch traced here: 72 us
  Pallas kernels  70.5 us (98%)
  between operations  1.47 us (2%)
    pallas_call x1, Pallas kernels, per_device(): pl.pallas_call(functools.partial(layer_kernel, count, total_rows, cuts, p...  67.5 us
    pallas_call x1, Pallas kernels, per_device(): pl.pallas_call(functools.partial(finish_kernel, total_rows, ['feats'] + O...  2.97 us

profile of v7, /device:TPU:0, one launch (start us, length us, event | category | flops | bytes accessed | tf_op | source)
XLA Modules:
  0.0 72.0 jit_solution(5027735392853838203)
XLA Ops:
  1.3 67.5 %layer.1 = (f32[512,512]{1,0:T(8,128)S(1)}, f32[100,512]{1,0:T(8,128)S(1)}, bf16[5120,128]{1,0:T(8,128)(2,1)S(1)}, bf16[2,1536,128]{2,1,0:T(8,128)(2,1)S(1)}, bf...) custom-call(f32[100,512]{1,0:T(8,128)} %bitcast.18, ...), custom_call_target="tpu_custom_call" | custom-call | tf_op jit(solution)/shard_map/layer/pallas_call | solution.py:897
  68.8 3.0 %finish.1 = (f32[512,512]{1,0:T(8,128)}, f32[100,512]{1,0:T(8,128)}, f32[512,512]{1,0:T(8,128)}, f32[100,512]{1,0:T(8,128)}, f32[1,512]{1,0:T(1,128)}, /*index=5...) custom-call(f32[100,512]{1,0:T(8,128)} %bitcast.19, ...), custom_call_target="tpu_custom_call" | custom-call | tf_op jit(solution)/shard_map/finish/pallas_call | solution.py:929
